TPU v7x, 32 devices: a whole 2x2x4 slice. The times are simulated.
32 devices in a mesh: seq: 4 (over y, x), fsdp: 8 (over z, core).
Axes of the slice: x: 2, y: 2, z: 4, core: 2. Of those that a mesh axis runs over, the one named last changes fastest.
Arguments:
- patches: bfloat16 [8, 2176, 1176], P('fsdp', 'seq'), may hold values from -6 to 6
- send_slot: int32 [8, 68], P('fsdp', 'seq'), may hold values from 0 to 67, as said below
- segments: int32 [8, 68], P('fsdp'), may hold values from 0 to 7, never falling along the last dimension, each value on 1 to 24 neighbouring positions
- stem_weight: bfloat16 [3584, 1176], P('fsdp'), may hold values from -0.1875 to 0.1875
- norm_gain: bfloat16 [3584], P('fsdp'), may hold values from 0.099609375 to 1.8984375
- conv_kernel: bfloat16 [5, 3584], P(None, 'fsdp'), may hold values from -3 to 3
- cotangent: bfloat16 [8, 2176, 3584], P('fsdp', 'seq'), may hold values from -6 to 6
Outputs:
- features: bfloat16 [8, 2176, 3584], P('fsdp', 'seq')
- grad_patches: bfloat16 [8, 2176, 1176], P('fsdp', 'seq')
- grad_weight: bfloat16 [3584, 1176], P('fsdp')
- grad_channels: float32 [6, 3584], P(None, 'fsdp')
Inputs may be any that keep to these rules, and one draw needn't show every extreme that they name: `send_slot`: each row is a permutation of the packed slots. At most 8 frame slots of one device go to one device's packed slots, and every device sends exactly 8 to some device; within a row the number that device s sends to device (s + o) modulo the seq axis size depends on o alone. `segments`: ids never fall along a row; a clip holds 1 to 24 slots, one exactly 24.
All inputs are finite; a program needn't handle non-finite values.
Results may differ from a plain program's by a relative error of at most 0.0056.
Values may be sent and summed in bfloat16 or wider, within the bound.
No kernel may reach another device: no remote copies, remote signals or barrier semaphores. Data moves between devices by JAX's collectives and lax.ppermute only.
A program may use at most 192 MiB of HBM per device.

v0:
```python
import math

import jax
import jax.numpy as jnp
from jax import lax
from jax.sharding import PartitionSpec as P

EPSILON = 1e-06


def extended_2(cells, sides, width):
    for axis, dim in sides:
        count = lax.axis_size(axis)
        ends = count - 1
        head = lax.slice_in_dim(cells, 0, width, axis=dim)
        tail = lax.slice_in_dim(cells, cells.shape[dim] - width, cells.shape[dim], axis=dim)
        cells = jnp.concatenate(
            [
                lax.ppermute(tail, axis, [(i, (i + 1) % count) for i in range(ends)]),
                cells,
                lax.ppermute(head, axis, [((i + 1) % count, i) for i in range(ends)]),
            ],
            axis=dim,
        )
    return cells


def slot_mask(segment_row, centre):
    slot_total = segment_row.shape[0]
    safe_centre = jnp.clip(centre, 0, slot_total - 1)
    columns = []
    for offset in range(5):
        neighbour = centre + (offset - 2)
        inside = (neighbour >= 0) & (neighbour < slot_total) & (centre >= 0) & (centre < slot_total)
        same_clip = segment_row[jnp.clip(neighbour, 0, slot_total - 1)] == segment_row[safe_centre]
        columns.append((inside & same_clip).astype(jnp.float32))
    return jnp.stack(columns, axis=1)


def temporal_mix(padded, clip_mask, kernel, slot_total):
    kernel_wide = kernel.astype(jnp.float32)
    result = padded[0:slot_total].astype(jnp.float32) * (
        clip_mask[:, 0][:, None, None] * kernel_wide[0][None, None, :]
    )
    for offset in range(1, 5):
        addend = padded[offset : offset + slot_total].astype(jnp.float32) * (
            clip_mask[:, offset][:, None, None] * kernel_wide[offset][None, None, :]
        )
        result = result + addend
    return result


def temporal_back(slope_padded, mask_padded, kernel, slot_total):
    kernel_wide = kernel.astype(jnp.float32)
    result = jnp.zeros((slot_total,) + slope_padded.shape[1:], jnp.float32)
    for offset in range(5):
        first_row = 4 - offset
        weights_row = (
            mask_padded[first_row : first_row + slot_total, offset][:, None, None]
            * kernel_wide[offset][None, None, :]
        )
        result = (
            result
            + slope_padded[first_row : first_row + slot_total].astype(jnp.float32) * weights_row
        )
    return result


def kernel_sums(slope_blocks, padded, clip_mask, slot_total):
    stacked = []
    for offset in range(5):
        product = jnp.sum(
            slope_blocks.astype(jnp.float32)
            * padded[offset : offset + slot_total].astype(jnp.float32),
            axis=1,
        )
        stacked.append(jnp.sum(product * clip_mask[:, offset][:, None], axis=0))
    return jnp.stack(stacked, axis=0)


def rim_rows(values, margin):
    return extended_2(values, (("seq", 0),), margin)


def shards(patches, send_slot, segments, stem_weight, norm_gain, conv_kernel, cotangent):
    seq_size = lax.axis_size("seq")
    fsdp_size = lax.axis_size("fsdp")
    seq_index = lax.axis_index("seq")
    slot_count = send_slot.shape[1]
    tokens = patches.shape[1]
    slot_rows = tokens // slot_count
    pixel_width = patches.shape[2]
    capacity = 2 * slot_count // seq_size
    destination = send_slot[0]
    owner_index = destination // slot_count
    same_owner = owner_index[:, None] == owner_index[None, :]
    earlier = destination[None, :] < destination[:, None]
    ranking = jnp.sum((same_owner & earlier).astype(jnp.int32), axis=1)
    buffer_row = owner_index * capacity + ranking
    frames = patches[0].reshape(slot_count, slot_rows, pixel_width)
    outbox = (
        jnp.zeros((seq_size * capacity, slot_rows, pixel_width), jnp.bfloat16)
        .at[buffer_row]
        .set(frames)
    )
    position = (
        jnp.full((seq_size * capacity,), -1.0, jnp.float32)
        .at[buffer_row]
        .set((destination % slot_count).astype(jnp.float32))
        .astype(jnp.bfloat16)
    )
    incoming, arrived = (
        lax.all_to_all(outbox, "seq", split_axis=0, concat_axis=0, tiled=True),
        lax.all_to_all(position, "seq", split_axis=0, concat_axis=0, tiled=True),
    )
    arrived_float = arrived.astype(jnp.float32)
    target = jnp.where(arrived_float >= 0.0, arrived_float, float(slot_count)).astype(jnp.int32)
    packed = (
        jnp.zeros((slot_count + 1, slot_rows, pixel_width), jnp.bfloat16)
        .at[target]
        .set(incoming)[:slot_count]
        .reshape(tokens, pixel_width)
    )
    weight_full, gain_low, kernel_full = (
        lax.all_gather(stem_weight, "fsdp", axis=0, tiled=True),
        lax.all_gather(norm_gain, "fsdp", axis=0, tiled=True),
        lax.all_gather(conv_kernel, "fsdp", axis=1, tiled=True),
    )
    gain_wide = gain_low.astype(jnp.float32)
    channels = weight_full.shape[0]
    stem_out = lax.dot_general(
        packed, weight_full, (((1,), (1,)), ((), ())), preferred_element_type=jnp.float32
    )
    inv_rms = lax.rsqrt(jnp.mean(stem_out * stem_out, axis=1, keepdims=True) + EPSILON)
    unit_rows = stem_out * inv_rms
    normed = (unit_rows * gain_wide).astype(jnp.bfloat16)
    segment_row = segments[0]
    centre = seq_index * slot_count + jnp.arange(slot_count, dtype=jnp.int32)
    extended = seq_index * slot_count + jnp.arange(-2, slot_count + 2, dtype=jnp.int32)
    clip_mask = slot_mask(segment_row, centre)
    mask_padded = slot_mask(segment_row, extended)
    padded = rim_rows(normed, 2 * slot_rows).reshape(slot_count + 4, slot_rows, channels)
    mixed_rows = temporal_mix(padded, clip_mask, kernel_full, slot_count).reshape(tokens, channels)
    features = (stem_out + jax.nn.silu(mixed_rows)).astype(jnp.bfloat16)
    upstream_wide = cotangent[0].astype(jnp.float32)
    gate_value = jax.nn.sigmoid(mixed_rows)
    slope_low = (upstream_wide * gate_value * (1.0 + mixed_rows * (1.0 - gate_value))).astype(
        jnp.bfloat16
    )
    slope_padded = rim_rows(slope_low, 2 * slot_rows).reshape(slot_count + 4, slot_rows, channels)
    d_normed = temporal_back(slope_padded, mask_padded, kernel_full, slot_count).reshape(
        tokens, channels
    )
    gated = d_normed * gain_wide
    d_stem = upstream_wide + inv_rms * (
        gated - unit_rows * jnp.mean(gated * unit_rows, axis=1, keepdims=True)
    )
    d_stem_low = d_stem.astype(jnp.bfloat16)
    grad_rows = jnp.dot(d_stem_low, weight_full, preferred_element_type=jnp.float32).astype(
        jnp.bfloat16
    )
    gain_part = jnp.sum(d_normed * unit_rows, axis=0)
    slope_blocks = slope_padded[2 : 2 + slot_count]
    kernel_part = kernel_sums(slope_blocks, padded, clip_mask, slot_count)
    chan_terms = jnp.concatenate([gain_part[None, :], kernel_part], axis=0).T
    weight_block = lax.dot_general(
        d_stem_low, packed, (((0,), (0,)), ((), ())), preferred_element_type=jnp.float32
    )
    grad_shard = lax.psum_scatter(
        jnp.concatenate([weight_block, chan_terms], axis=1), "fsdp", scatter_dimension=0, tiled=True
    )
    summed = lax.psum(grad_shard, "seq")
    grad_scale = 1.0 / math.sqrt(tokens * seq_size * fsdp_size)
    grad_weight = (summed[:, :pixel_width] * grad_scale).astype(jnp.bfloat16)
    grad_channels = (summed[:, pixel_width:] * grad_scale).T
    return (features[None], grad_rows[None], grad_weight, grad_channels)


def solution(mesh):
    in_specs = (
        P("fsdp", "seq", None),
        P("fsdp", "seq"),
        P("fsdp", None),
        P("fsdp", None),
        P("fsdp"),
        P(None, "fsdp"),
        P("fsdp", "seq", None),
    )
    out_specs = (P("fsdp", "seq", None), P("fsdp", "seq", None), P("fsdp", None), P(None, "fsdp"))
    return jax.shard_map(shards, mesh=mesh, in_specs=in_specs, out_specs=out_specs, check_vma=False)
```

profile of v0, /device:TPU:0, one launch (start us, length us, event | category | flops | bytes accessed | tf_op | source)
XLA Modules:
  0.0 526.9 jit_solution(14682402449252586406)
XLA Ops:
  12.2 5.2 all-to-all-start
  21.0 14.8 %all-gather = bf16[8,448,5]{1,2,0:T(8,128)(2,1)S(1)} all-gather(bf16[1,448,5]{1,2,0:T(8,128)(2,1)} %bitcast.136), channel_id=1, replica_groups=mesh['seq'=4,'fsdp'=8] {'fsdp'}, dimensions={0}, use_global_device_ids=true | all-gather | bytes 40320 | tf_op jit(solution)/shard_map/all_gather | solution.py:127
  41.3 5.8 %scatter_fusion = bf16[32,32,1176]{2,1,0:T(8,128)(2,1)} fusion(bf16[32,32,1176]{2,1,0:T(8,128)(2,1)} %broadcast_in_dim.19, s32[17]{0:T(128)S(1)} %fusion.26, bf16[17,32,1176]{2,1,0:T(8,128)(2,1)S(1)} %bitcast.131), kind=kCustom, calls=%fused_computation.11 | custom fusion | bytes 3838532 | tf_op jit(solution)/shard_map/scatter | solution.py:104
  49.3 4.6 all-to-all-start.1
  56.4 19.1 %all-reduce = bf16[3584]{0:T(1024)(128)(2,1)S(1)} all-reduce(bf16[3584]{0:T(1024)(128)(2,1)S(1)} %dynamic-update-slice), channel_id=1, replica_groups=mesh['seq'=4,'fsdp'=8] {'fsdp'}, use_global_device_ids=true, to_apply=%add | all-reduce | flops 3584 | bytes 14336
  76.7 8.5 %all-to-all-done.1 = bf16[32,32,1176]{2,1,0:T(8,128)(2,1)} async-done(((bf16[32,32,1176]{2,1,0:T(8,128)(2,1)}), bf16[32,32,1176]{2,1,0:T(8,128)(2,1)}, u32[]{:S(2)}, u32[]{:S(2)}) %all-to-all-start.1) | async-done | bytes 2408480 | tf_op jit(solution)/shard_map/all_to_all | solution.py:113
  89.7 12.3 %all-gather.3.cloned.1.call-done = bf16[3584,1176]{1,0:T(8,128)(2,1)} async-done(((bf16[448,1176]{1,0:T(8,128)(2,1)}), bf16[3584,1176]{1,0:T(8,128)(2,1)}) %all-gather.3.cloned.1.call-update) | async-done | bytes 8429584 | tf_op jit(solution)/shard_map/all_gather | solution.py:125
  101.9 8.0 %multiply_reduce_fusion.2 = (f32[544]{0:T(1024)S(1)}, f32[544,3584]{1,0:T(8,128)S(1)}) fusion(bf16[544,1176]{1,0:T(8,128)(2,1)S(1)} %bitcast.132, bf16[3584,1176]{1,0:T(8,128)(2,1)} %all-gather.3.cloned.1.call-done), kind=kOutput, calls=%fused_computation.47 | convolution fusion | flops 4589583872 | bytes 17510016 | tf_op jit(solution)/shard_map/dot_general | solution.py:131
  113.0 5.0 collective-permute-start
  118.8 8.2 %collective-permute-done.1 = bf16[64,3584]{1,0:T(8,128)(2,1)S(1)} collective-permute-done((bf16[64,3584]{1,0:T(8,128)(2,1)S(1)}, bf16[64,3584]{1,0:T(8,128)(2,1)S(1)}, u32[]{:S(2)}, u32[]{:S(2)}) %collective-permute-start.1) | collective-permute-done | bytes 458784 | tf_op jit(solution)/shard_map/ppermute | solution.py:21
  127.8 8.3 %convert_multiply_fusion = (f32[544,3584]{1,0:T(8,128)}, bf16[544,3584]{1,0:T(8,128)(2,1)S(1)}, f32[544,3584]{1,0:T(8,128)}) fusion(bf16[64,3584]{1,0:T(8,128)(2,1)S(1)} %collective-permute-done.1, bf16[544,3584]{1,0:T(8,128)(2,1)S(1)} %multiply_convert_fusion, bf16[1,544,3584]{2,1,0:T(8,128)(2,1)S(1)} %copy-done.5, f32[17,3584]{1,0:T(8,128)S(1)} %copy-done.7, ...), kind=kLoop, calls=%fused_computation.13 | loop fusion | flops 74088448 | bytes 29431808 | tf_op jit(solution)/shard_map/mul | solution.py:73
  138.9 10.7 %collective-permute-start.3 = (bf16[64,3584]{1,0:T(8,128)(2,1)}, bf16[64,3584]{1,0:T(8,128)(2,1)}, u32[]{:S(2)}, u32[]{:S(2)}) collective-permute-start(bf16[64,3584]{1,0:T(8,128)(2,1)} %get-tuple-element.45), channel_id=1, source_target_pairs={{0,8},{8,16},{16,24},{1,9},{9,17},{17,25},{2,10},{10,18},{18,26},{... | collective-permute-start | bytes 1376264 | tf_op jit(solution)/shard_map/ppermute | solution.py:19
  151.0 15.1 %convert_multiply_fusion.1 = (f32[544,3584]{1,0:T(8,128)}, f32[544,3584]{1,0:T(8,128)}, f32[544,3584]{1,0:T(8,128)}, f32[544,3584]{1,0:T(8,128)}) fusion(bf16[544,3584]{1,0:T(8,128)(2,1)} %copy-done.3, bf16[64,3584]{1,0:T(8,128)(2,1)S(1)} %collective-permute-done.1, bf16[544,3584]{1,0:T(8,128)(2,1)} %copy-done.4, bf16[64,3584]{1,0:T(8,128)(2,1)S(1)} %collective-permute-done), kind=kLoop, calls=%fused_computation.14 | loop fusion | flops 35094528 | bytes 39911424 | tf_op jit(solution)/shard_map/mul | solution.py:73
  170.6 4.4 reduce_sum.135
  175.1 4.4 reduce_sum.137
  179.6 4.4 reduce_sum.139
  188.7 10.2 %fusion.9 = f32[544,3584]{1,0:T(8,128)S(1)} fusion(bf16[544,3584]{1,0:T(8,128)(2,1)} %copy-done.3, bf16[64,3584]{1,0:T(8,128)(2,1)} %collective-permute-done.3, bf16[64,3584]{1,0:T(8,128)(2,1)} %collective-permute-done.2, f32[17,3584]{1,0:T(8,128)S(1)} %get-tuple-element.56, f32[17,3584]{1,0:T(8,128)} %get-tuple-element.54, ...), kind=kLoop, calls=%fused_computation.36 | loop fusion | flops 50692096 | bytes 13834240 | tf_op jit(solution)/shard_map/add | solution.py:63
  201.0 9.9 %fusion.6 = (bf16[544,3584]{1,0:T(8,128)(2,1)}, bf16[1,544,3584]{2,1,0:T(8,128)(2,1)}) fusion(f32[544,3584]{1,0:T(8,128)S(1)} %fusion.9, f32[544,3584]{1,0:T(8,128)S(1)} %bitcast.125, bf16[1,544,3584]{2,1,0:T(8,128)(2,1)} %param.13, f32[544]{0:T(1024)S(1)} %broadcast_multiply_fusion.10, f32[3584]{0:T(1024)S(1)} %convert_element_type.185, ...), kind=kLoop, calls=%fused_computation.33 | loop fusion | flops 27295744 | bytes 35113216 | tf_op jit(solution)/shard_map/convert_element_type | solution.py:158
  210.9 12.7 %fusion.47 = f32[3584,1176]{0,1:T(8,128)} fusion(bf16[544,3584]{1,0:T(8,128)(2,1)} %get-tuple-element.42, bf16[544,1176]{1,0:T(8,128)(2,1)S(1)} %bitcast.133), kind=kOutput, calls=%fused_computation.172 | convolution fusion | flops 4585684992 | bytes 22038016 | tf_op jit(solution)/shard_map/dot_general | solution.py:166
  223.7 11.5 %pad_maximum_fusion = f32[3584,1182]{0,1:T(8,128)} fusion(f32[3584,6]{0,1:T(8,128)S(1)} %bitcast.134, f32[3584,1176]{0,1:T(8,128)} %fusion.47), kind=kLoop, calls=%fused_computation.19 | loop fusion | flops 4236288 | bytes 33890304 | tf_op jit(solution)/shard_map/concatenate | solution.py:170
  235.3 18.8 %copy.23 = f32[3584,1182]{1,0:T(8,128)} copy(f32[3584,1182]{0,1:T(8,128)} %pad_maximum_fusion) | data formatting | bytes 33890304
  254.2 184.6 %reduce-scatter.4.cloned.1.call-done = f32[448,1182]{1,0:T(8,128)} async-done(((f32[3584,1182]{1,0:T(8,128)}), f32[448,1182]{1,0:T(8,128)}) %reduce-scatter.4.cloned.1.call-update) | async-done | bytes 2118160
  441.9 10.8 %fusion.16 = bf16[1,544,1176]{2,1,0:T(8,128)(2,1)} fusion(bf16[544,3584]{1,0:T(8,128)(2,1)} %get-tuple-element.42, bf16[3584,1176]{1,0:T(8,128)(2,1)} %all-gather.3.cloned.1.call-done), kind=kOutput, calls=%fused_computation.66 | convolution fusion | flops 4586324992 | bytes 13608448 | tf_op jit(solution)/shard_map/dot_general | solution.py:159
  452.7 62.9 %all-reduce.3.cloned.1.call-done = f32[448,1182]{0,1:T(8,128)} async-done(((f32[448,1182]{0,1:T(8,128)}), f32[448,1182]{0,1:T(8,128)}) %all-reduce.3.cloned.1.call-update) | async-done | bytes 2118160 | tf_op jit(solution)/shard_map/psum | solution.py:172
  (130 shorter events, 52.1 us)
Async XLA Ops:
  7.2 10.2 %copy-start = (s32[1,68]{1,0:T(1,128)S(1)}, s32[1,68]{1,0:T(1,128)}, u32[]{:S(2)}) copy-start(s32[1,68]{1,0:T(1,128)} %param.9) | copy-start | bytes 820
  7.2 34.1 %copy-start.6 = (bf16[1,544,1176]{2,1,0:T(8,128)(2,1)S(1)}, bf16[1,544,1176]{2,1,0:T(8,128)(2,1)}, u32[]{:S(2)}) copy-start(bf16[1,544,1176]{2,1,0:T(8,128)(2,1)} %param.7) | copy-start | bytes 3838468
  7.2 94.7 %all-gather.3.cloned.1.call-start = ((), (), s32[]{:S(2)}) async-start(), calls=%async_computation.3 | async-start | bytes 10321920 | tf_op jit(solution)/shard_map/all_gather | solution.py:125
  12.2 37.1 %all-to-all-start = ((bf16[4,8,1]{1,2,0:T(2,128)(2,1)}), bf16[4,8,1]{1,2,0:T(2,128)(2,1)S(1)}, u32[]{:S(2)}, u32[]{:S(2)}) async-start(bf16[4,8,1]{1,2,0:T(2,128)(2,1)} %all_to_all.12), calls=%async_computation | async-start | bytes 4096 | tf_op jit(solution)/shard_map/all_to_all | solution.py:114
  38.0 16.9 %copy-start.12 = (u32[32]{0:T(128)S(1)}, u32[32]{0:T(128)}, u32[]{:S(2)}) copy-start(u32[32]{0:T(128)} %constant.81) | copy-start | bytes 388
  38.0 18.1 %copy-start.11 = (bf16[448]{0:T(512)(128)(2,1)S(1)}, bf16[448]{0:T(512)(128)(2,1)}, u32[]{:S(2)}) copy-start(bf16[448]{0:T(512)(128)(2,1)} %param.11) | copy-start | bytes 2692
  49.3 35.9 %all-to-all-start.1 = ((bf16[32,32,1176]{2,1,0:T(8,128)(2,1)}), bf16[32,32,1176]{2,1,0:T(8,128)(2,1)}, u32[]{:S(2)}, u32[]{:S(2)}) async-start(bf16[32,32,1176]{2,1,0:T(8,128)(2,1)} %scatter_fusion), calls=%async_computation.1 | async-start | bytes 5242880 | tf_op jit(solution)/shard_map/all_to_all | solution.py:113
  53.8 384.9 %reduce-scatter.4.cloned.1.call-start = ((), (), s32[]{:S(2)}) async-start(), calls=%async_computation.5 | async-start | bytes 20643840
  109.9 26.2 %copy-start.2 = (f32[544,3584]{1,0:T(8,128)}, f32[544,3584]{1,0:T(8,128)S(1)}, u32[]{:S(2)}) copy-start(f32[544,3584]{1,0:T(8,128)S(1)} %get-tuple-element.69) | copy-start | bytes 23396356
  109.9 17.9 %copy-start.5 = (bf16[1,544,3584]{2,1,0:T(8,128)(2,1)S(1)}, bf16[1,544,3584]{2,1,0:T(8,128)(2,1)}, u32[]{:S(2)}) copy-start(bf16[1,544,3584]{2,1,0:T(8,128)(2,1)} %param.13) | copy-start | bytes 11698180
  109.9 17.9 %copy-start.7 = (f32[17,3584]{1,0:T(8,128)S(1)}, f32[17,3584]{1,0:T(8,128)}, u32[]{:S(2)}) copy-start(f32[17,3584]{1,0:T(8,128)} %get-tuple-element.57) | copy-start | bytes 731140
  110.0 17.9 %copy-start.8 = (f32[17,3584]{1,0:T(8,128)S(1)}, f32[17,3584]{1,0:T(8,128)}, u32[]{:S(2)}) copy-start(f32[17,3584]{1,0:T(8,128)} %get-tuple-element.55) | copy-start | bytes 731140
  110.0 17.9 %copy-start.9 = (f32[17,3584]{1,0:T(8,128)S(1)}, f32[17,3584]{1,0:T(8,128)}, u32[]{:S(2)}) copy-start(f32[17,3584]{1,0:T(8,128)} %get-tuple-element.53) | copy-start | bytes 731140
  110.0 17.8 %copy-start.10 = (f32[17,3584]{1,0:T(8,128)S(1)}, f32[17,3584]{1,0:T(8,128)}, u32[]{:S(2)}) copy-start(f32[17,3584]{1,0:T(8,128)} %get-tuple-element.51) | copy-start | bytes 731140
  111.3 24.8 %copy-start.4 = (bf16[544,3584]{1,0:T(8,128)(2,1)}, bf16[544,3584]{1,0:T(8,128)(2,1)S(1)}, u32[]{:S(2)}) copy-start(bf16[544,3584]{1,0:T(8,128)(2,1)S(1)} %multiply_convert_fusion) | copy-start | bytes 11698180
  111.4 15.6 %collective-permute-start.1 = (bf16[64,3584]{1,0:T(8,128)(2,1)S(1)}, bf16[64,3584]{1,0:T(8,128)(2,1)S(1)}, u32[]{:S(2)}, u32[]{:S(2)}) collective-permute-start(bf16[64,3584]{1,0:T(8,128)(2,1)S(1)} %get-tuple-element.47), channel_id=1, source_target_pairs={{8,0},{16,8},{24,16},{9,1},{17,9},{25,17},{10,2},{18,10},{26,18},{... | collective-permute-start | bytes 1376264 | tf_op jit(solution)/shard_map/ppermute | solution.py:21
  113.0 14.8 %collective-permute-start = (bf16[64,3584]{1,0:T(8,128)(2,1)S(1)}, bf16[64,3584]{1,0:T(8,128)(2,1)S(1)}, u32[]{:S(2)}, u32[]{:S(2)}) collective-permute-start(bf16[64,3584]{1,0:T(8,128)(2,1)S(1)} %get-tuple-element.46), channel_id=1, source_target_pairs={{0,8},{8,16},{16,24},{1,9},{9,17},{17,25},{2,10},{10,18},{18,26},{... | collective-permute-start | bytes 1376264 | tf_op jit(solution)/shard_map/ppermute | solution.py:19
  136.2 1.9 copy-start.3
  138.9 49.7 %collective-permute-start.3 = (bf16[64,3584]{1,0:T(8,128)(2,1)}, bf16[64,3584]{1,0:T(8,128)(2,1)}, u32[]{:S(2)}, u32[]{:S(2)}) collective-permute-start(bf16[64,3584]{1,0:T(8,128)(2,1)} %get-tuple-element.45), channel_id=1, source_target_pairs={{0,8},{8,16},{16,24},{1,9},{9,17},{17,25},{2,10},{10,18},{18,26},{... | collective-permute-start | bytes 1376264 | tf_op jit(solution)/shard_map/ppermute | solution.py:19
  149.6 39.1 %collective-permute-start.2 = (bf16[64,3584]{1,0:T(8,128)(2,1)S(1)}, bf16[64,3584]{1,0:T(8,128)(2,1)}, u32[]{:S(2)}, u32[]{:S(2)}) collective-permute-start(bf16[64,3584]{1,0:T(8,128)(2,1)S(1)} %get-tuple-element.44), channel_id=1, source_target_pairs={{8,0},{16,8},{24,16},{9,1},{17,9},{25,17},{10,2},{18,10},{26,18},{... | collective-permute-start | bytes 1376264 | tf_op jit(solution)/shard_map/ppermute | solution.py:21
  188.5 10.4 %slice-start = ((s8[7798784]{0:T(1024)(128)(4,1)}), s8[4194304]{0:T(1024)(128)(4,1)S(1)}, s32[]{:S(2)}) async-start(s8[7798784]{0:T(1024)(128)(4,1)} %bitcast.124), calls=%async_computation.6 | async-start | bytes 8388608
  188.7 10.3 %slice-start.1 = ((s8[7798784]{0:T(1024)(128)(4,1)}), s8[3604480]{0:T(1024)(128)(4,1)S(1)}, s32[]{:S(2)}) async-start(s8[7798784]{0:T(1024)(128)(4,1)} %bitcast.124), calls=%async_computation.7 | async-start | bytes 7208960
  254.1 261.4 %all-reduce.3.cloned.1.call-start = ((), (), s32[]{:S(2)}) async-start(), calls=%async_computation.4 | async-start | bytes 4849664 | tf_op jit(solution)/shard_map/psum | solution.py:172
  441.9 78.5 %copy-start.1 = (s32[1,68]{1,0:T(1,128)S(1)}, s32[1,68]{1,0:T(1,128)}, u32[]{:S(2)}) copy-start(s32[1,68]{1,0:T(1,128)} %param.9) | copy-start | bytes 820
Sparse Core Ops, SparseCore 0:
  9.7 92.2 all-gather.2
  254.2 184.5 reduce-scatter.3
  442.0 73.4 all-reduce.2
where the time goes:
time: 528 us; the launch traced here: 527 us
  waiting for transfers between devices  278 us (53%)
  other arithmetic  92.2 us (17%)
  local copies, waits for them, and re-layouts  48 us (9%)
  blocking collectives  33.8 us (6%)
  matrix products  31.5 us (6%)
  starting transfers between devices  28.5 us (5%)
  between operations  15 us (3%)
    unnamed x4, waiting for transfers between devices  185 us
    psum x1, waiting for transfers between devices, shards(): summed = lax.psum(grad_shard, 'seq')  62.9 us
    unnamed x36, local copies, waits for them, and re-layouts  26.3 us
    mul x2, other arithmetic, kernel_sums(): slope_blocks.astype(jnp.float32)  23.4 us
    reduce_sum x5, other arithmetic, kernel_sums(): jnp.sum(slope_blocks.astype(jnp.float32) * padded[offset:offset + slot_to...  21.8 us
    unnamed x1, blocking collectives  19.1 us
    ppermute x2, starting transfers between devices, extended_2(): lax.ppermute(tail, axis, [(i, (i + 1) % count) for i in range(ends)])  15.6 us
    all_gather x1, blocking collectives, shards(): lax.all_gather(conv_kernel, 'fsdp', axis=1, tiled=True)  14.8 us
  transfers between devices with their start and end apart: 9, of which 6 were waited for; matrix products, arithmetic and copies ran while one was open for 15% of the time, Pallas kernels for 0%

commit v1 on v0

v1 whole, which is shorter than its diff:
```python
import functools
import math

import jax
import jax.numpy as jnp
from jax import lax
from jax.experimental import pallas as pl
from jax.experimental.pallas import tpu as pltpu
from jax.sharding import PartitionSpec as P

EPSILON = 1e-06
BF16 = jnp.bfloat16
F32 = jnp.float32
LANES = 128
AXES = ("seq", "fsdp")
VMEM_BYTES = 56 * 1024 * 1024


def round_up(value, unit):
    return (value + unit - 1) // unit * unit


def kernel_params(**more):
    return pltpu.CompilerParams(vmem_limit_bytes=VMEM_BYTES, **more)


def sent(value, route):
    seq_size, fsdp_size = lax.axis_size("seq"), lax.axis_size("fsdp")
    pairs = []
    for s in range(seq_size):
        for f in range(fsdp_size):
            target = route(s, f)
            if target is not None:
                pairs.append((s * fsdp_size + f, target[0] * fsdp_size + target[1]))
    return lax.ppermute(value, AXES, pairs)


def swapped(value, seq_bits, fsdp_bits):
    return sent(value, lambda s, f: (s ^ seq_bits, f ^ fsdp_bits))


def bits_of(size):
    return [1 << i for i in range(size.bit_length() - 1)]


def by_position(pieces, me):
    stack = jnp.stack(pieces, axis=0)
    count = len(pieces)
    tail = stack.shape[1:]
    for bit in bits_of(count):
        view = stack.reshape((count // (2 * bit), 2, bit) + tail)
        flipped = jnp.concatenate([view[:, 1:], view[:, :1]], axis=1)
        stack = jnp.where((me & bit) != 0, flipped, view).reshape((count,) + tail)
    return stack


def outbox_kernel(order_ref, frames_ref, *out_refs):
    width = frames_ref.shape[2]
    for peer, out in enumerate(out_refs):
        capacity, rows, padded = out.shape
        out[:, :, padded - LANES :] = jnp.zeros((capacity, rows, LANES), out.dtype)
        for k in range(capacity):
            out[k, :, :width] = frames_ref[order_ref[peer * capacity + k]]


def place_kernel(pick_ref, frames_ref, *refs):
    inbox, out = refs[:-1], refs[-1]
    slots, _, width = frames_ref.shape
    padded = out.shape[2]
    capacity = inbox[0].shape[0]
    out[:, :, padded - LANES :] = jnp.zeros((slots, out.shape[1], LANES), out.dtype)

    def one(p, carry):
        index = pick_ref[p]

        @pl.when(index < slots)
        def _():
            out[p, :, :width] = frames_ref[index]

        for peer, box in enumerate(inbox):
            first = slots + peer * capacity

            @pl.when((index >= first) & (index < first + capacity))
            def _():
                out[p] = box[index - first]

        return carry

    lax.fori_loop(0, slots, one, 0)


def scalar_call(kernel, out_shape, scalars, arrays):
    return pl.pallas_call(
        kernel,
        grid_spec=pltpu.PrefetchScalarGridSpec(
            num_scalar_prefetch=1,
            grid=(),
            in_specs=[pl.BlockSpec(memory_space=pltpu.VMEM)] * len(arrays),
            out_specs=jax.tree.map(lambda _: pl.BlockSpec(memory_space=pltpu.VMEM), out_shape),
        ),
        out_shape=out_shape,
        compiler_params=kernel_params(),
    )(scalars, *arrays)


def pack_slots(frames, destination, seq_index, seq_size, padded):
    slots, rows, width = frames.shape
    capacity = 2 * slots // seq_size
    owner = (destination // slots) ^ seq_index
    rank = jnp.sum(
        ((owner[:, None] == owner[None, :]) & (destination[None, :] < destination[:, None])).astype(
            jnp.int32
        ),
        axis=1,
    )
    peers = jnp.arange(1, seq_size, dtype=jnp.int32)
    places = jnp.arange(capacity, dtype=jnp.int32)
    hit = (owner[None, None, :] == peers[:, None, None]) & (
        rank[None, None, :] == places[None, :, None]
    )
    numbers = jnp.arange(slots, dtype=jnp.int32)
    order = jnp.sum(jnp.where(hit, numbers, 0), axis=2).reshape(-1)
    outbox = scalar_call(
        outbox_kernel,
        [jax.ShapeDtypeStruct((capacity, rows, padded), BF16)] * (seq_size - 1),
        order,
        [frames],
    )
    inbox = [swapped(box, o + 1, 0) for o, box in enumerate(outbox)]
    rows_of = jnp.stack(
        [destination] + [swapped(destination, o, 0) for o in range(1, seq_size)], axis=0
    )
    match = rows_of[:, :, None] == (seq_index * slots + numbers)[None, None, :]
    source = jnp.sum(
        jnp.where(match, jnp.arange(seq_size, dtype=jnp.int32)[:, None, None], 0), axis=(0, 1)
    )
    local = jnp.sum(jnp.where(match, numbers[None, :, None], 0), axis=(0, 1))
    arrival = jnp.sum(
        ((source[:, None] == source[None, :]) & (numbers[None, :] < numbers[:, None])).astype(
            jnp.int32
        ),
        axis=1,
    )
    pick = jnp.where(source == 0, local, slots + (source - 1) * capacity + arrival)
    return scalar_call(
        place_kernel,
        jax.ShapeDtypeStruct((slots, rows, padded), BF16),
        pick,
        [frames] + inbox,
    )


def gather_weights(own, seq_index, chip, chips, seq_size):
    shard = own.shape[0]
    shared = shard * 4 // 7 // seq_size // 8 * 8
    whole = shard - seq_size * shared
    piece = jnp.concatenate(
        [own[:whole], lax.dynamic_slice_in_dim(own, whole + seq_index * shared, shared, axis=0)],
        axis=0,
    )
    rising, falling = {0: piece}, {0: piece}
    for k in range(1, chips):
        rising[k] = sent(
            rising[k - 1], lambda s, f: (s, f + 2) if k - 1 <= f // 2 < chips - 1 else None
        )
        falling[k] = sent(
            falling[k - 1], lambda s, f: (s, f - 2) if 0 < f // 2 <= chips - k else None
        )
    low = chip < chips // 2
    far = jnp.maximum(chip, chips - 1 - chip)
    towards = jnp.where(low, 1, -1)
    shards, chip_of = [own], [chip]
    for k in range(1, chips):
        value = jnp.where(low, falling[k], rising[k])
        origin = chip + towards * k
        for reach in range(chips // 2, k):
            near = jnp.where(low, rising[k - reach], falling[k - reach])
            value = jnp.where(far == reach, near, value)
            origin = jnp.where(far == reach, chip - towards * (k - reach), origin)
        part = value[whole:]
        parts = [part] + [swapped(part, o, 0) for o in range(1, seq_size)]
        ordered = by_position(parts, seq_index).reshape(seq_size * shared, -1)
        shards.append(jnp.concatenate([value[:whole], ordered], axis=0))
        chip_of.append(origin)
    return shards, chip_of


def load_weights(place_ref, shard_refs, weights, sems):
    chips = len(shard_refs) // 2
    shard = shard_refs[0].shape[0]
    core = place_ref[chips]
    for k in range(chips):
        for h in range(2):
            lane = core if h == 0 else 1 - core
            first = pl.multiple_of((2 * place_ref[k] + lane) * shard, 16)
            pltpu.make_async_copy(
                shard_refs[2 * k + h],
                weights.at[pl.ds(first, shard), :],
                sems.at[2 * place_ref[k] + lane],
            ).start()


def wait_weights(shard_ref, weights, sems, f):
    shard = shard_ref.shape[0]
    pltpu.make_async_copy(
        shard_ref, weights.at[pl.ds(f * shard, shard), :], sems.at[f]
    ).wait()


def stem_kernel(
    place_ref, packed_ref, low_ref, high_ref, *refs, chips, channels, tile
):
    shard_refs = refs[: 2 * chips]
    normed_ref, inv_ref, chan_ref, stem_ref = refs[2 * chips : 2 * chips + 4]
    inputs, weights, acc, squares, inverse, sems, out_sems = refs[2 * chips + 4 :]
    tokens, padded = packed_ref.shape
    edge = low_ref.shape[0]
    width = padded - LANES + 24
    load_weights(place_ref, shard_refs, weights, sems)
    inputs[0:edge] = low_ref[...]
    inputs[edge : edge + tokens] = packed_ref[...]
    inputs[edge + tokens : 2 * edge + tokens] = high_ref[...]
    extra = inputs.shape[0] - 2 * edge - tokens
    row = lax.broadcasted_iota(jnp.int32, (extra, padded), 0)
    column = lax.broadcasted_iota(jnp.int32, (extra, padded), 1)
    inputs[2 * edge + tokens :] = jnp.where(
        (column == row + width) & (row < 6), 1.0, 0.0
    ).astype(BF16)
    squares[...] = jnp.zeros_like(squares)

    def one(j, carry):
        first = pl.multiple_of(j * tile, tile)
        result = lax.dot_general(
            inputs[...],
            weights[pl.ds(first, tile), :],
            (((1,), (1,)), ((), ())),
            preferred_element_type=F32,
        )
        acc[:, pl.ds(first, tile)] = result
        total = squares[...]
        for t in range(tile // LANES):
            part = result[:, t * LANES : (t + 1) * LANES]
            total = total + part * part
        squares[...] = total
        return carry

    group = channels // chips
    steps = channels // tile
    begin, copies = 0, []
    for z in range(chips):
        wait_weights(shard_refs[0], weights, sems, 2 * z)
        wait_weights(shard_refs[0], weights, sems, 2 * z + 1)
        end = (z + 1) * group // tile
        lax.fori_loop(begin, end, one, 0)
        lanes = pl.ds(begin * tile, (end - begin) * tile)
        copy = pltpu.make_async_copy(
            acc.at[pl.ds(edge, tokens), lanes], stem_ref.at[:, lanes], out_sems.at[z]
        )
        copy.start()
        copies.append(copy)
        begin = end
    rows = 2 * edge + tokens
    mean = jnp.sum(squares[...], axis=1, keepdims=True) / channels
    inverse[...] = jnp.broadcast_to(lax.rsqrt(mean + EPSILON), inverse.shape)
    inv_ref[...] = inverse[edge : edge + tokens]
    chan_ref[...] = acc[rows : rows + 8, :]

    def norm(t, carry):
        lanes = pl.ds(pl.multiple_of(t * LANES, LANES), LANES)
        gain = acc[rows : rows + 1, lanes]
        normed_ref[:, lanes] = (acc[0:rows, lanes] * inverse[0:rows] * gain).astype(BF16)
        return carry

    lax.fori_loop(0, channels // LANES, norm, 0)
    for copy in copies:
        copy.wait()


def stem(packed, low, high, shards, places, channels):
    tokens, padded = packed.shape
    edge = low.shape[0]
    chips = len(shards) // 2
    rows = 2 * edge + tokens
    return pl.pallas_call(
        functools.partial(stem_kernel, chips=chips, channels=channels, tile=256),
        grid_spec=pltpu.PrefetchScalarGridSpec(
            num_scalar_prefetch=1,
            grid=(),
            in_specs=[pl.BlockSpec(memory_space=pltpu.VMEM)] * 3
            + [pl.BlockSpec(memory_space=pl.ANY)] * len(shards),
            out_specs=[pl.BlockSpec(memory_space=pltpu.VMEM)] * 3
            + [pl.BlockSpec(memory_space=pl.ANY)],
            scratch_shapes=[
                pltpu.VMEM((rows + 16, padded), BF16),
                pltpu.VMEM((channels, padded), BF16),
                pltpu.VMEM((rows + 16, channels), F32),
                pltpu.VMEM((rows + 16, LANES), F32),
                pltpu.VMEM((rows + 16, LANES), F32),
                pltpu.SemaphoreType.DMA((2 * chips,)),
                pltpu.SemaphoreType.DMA((chips,)),
            ],
        ),
        out_shape=[
            jax.ShapeDtypeStruct((rows, channels), BF16),
            jax.ShapeDtypeStruct((tokens, LANES), F32),
            jax.ShapeDtypeStruct((8, channels), F32),
            jax.ShapeDtypeStruct((tokens, channels), F32),
        ],
        compiler_params=kernel_params(),
    )(places, packed, low, high, *shards)


def gate_of(value):
    return 0.5 * jnp.tanh(0.5 * value) + 0.5


def mixed_at(window, taps, mask_ref, g):
    total = window[0] * (taps[0] * mask_ref[5 * g])
    for k in range(1, 5):
        total = total + window[k] * (taps[k] * mask_ref[5 * g + k])
    return total


def edge_kernel(mask_ref, normed_ref, cot_ref, chan_ref, out_ref, *, slots, rows):
    edges = (0, 1, slots - 2, slots - 1)

    def one(t, carry):
        lanes = pl.ds(pl.multiple_of(t * LANES, LANES), LANES)
        taps = [chan_ref[1 + k : 2 + k, lanes] for k in range(5)]
        for i, g in enumerate(edges):
            window = [
                normed_ref[(g + k) * rows : (g + k + 1) * rows, lanes].astype(F32) for k in range(5)
            ]
            mixed = mixed_at(window, taps, mask_ref, g)
            gate = gate_of(mixed)
            up = cot_ref[g * rows : (g + 1) * rows, lanes].astype(F32)
            slope = up * gate * (1.0 + mixed * (1.0 - gate))
            out_ref[i * rows : (i + 1) * rows, lanes] = slope.astype(BF16)
        return carry

    lax.fori_loop(0, out_ref.shape[1] // LANES, one, 0)


def forward_kernel(
    mask_ref, normed_ref, stem_ref, cot_ref, chan_ref, feat_ref, slope_ref, part_ref, *, slots, rows
):
    def one(t, carry):
        lanes = pl.ds(pl.multiple_of(t * LANES, LANES), LANES)
        taps = [chan_ref[1 + k : 2 + k, lanes] for k in range(5)]

        def slot(i):
            return normed_ref[i * rows : (i + 1) * rows, lanes].astype(F32)

        window = [slot(i) for i in range(4)]
        sums = [jnp.zeros((8, LANES), F32) for _ in range(5)]
        for g in range(slots):
            window.append(slot(g + 4))
            mixed = mixed_at(window, taps, mask_ref, g)
            gate = gate_of(mixed)
            here = slice(g * rows, (g + 1) * rows)
            feat_ref[here, lanes] = (stem_ref[here, lanes] + mixed * gate).astype(BF16)
            up = cot_ref[here, lanes].astype(F32)
            slope = (up * gate * (1.0 + mixed * (1.0 - gate))).astype(BF16)
            slope_ref[here, lanes] = slope
            wide = slope.astype(F32)
            for k in range(5):
                product = (wide * window[k]).reshape(rows // 8, 8, LANES)
                sums[k] = sums[k] + jnp.sum(product, axis=0) * mask_ref[5 * g + k]
            window = window[1:]
        part_ref[0:1, lanes] = jnp.zeros((1, LANES), F32)
        for k in range(5):
            part_ref[1 + k : 2 + k, lanes] = jnp.sum(sums[k], axis=0, keepdims=True)
        part_ref[6:8, lanes] = jnp.zeros((2, LANES), F32)
        return carry

    lax.fori_loop(0, feat_ref.shape[1] // LANES, one, 0)


def column_call(kernel, scalars, arrays, out_rows, block):
    channels = arrays[0].shape[1]

    def spec(count):
        return pl.BlockSpec((count, block), lambda j, *_: (0, j))

    return pl.pallas_call(
        kernel,
        grid_spec=pltpu.PrefetchScalarGridSpec(
            num_scalar_prefetch=1,
            grid=(channels // block,),
            in_specs=[spec(a.shape[0]) for a in arrays],
            out_specs=[spec(count) for count, _ in out_rows],
        ),
        out_shape=[jax.ShapeDtypeStruct((count, channels), kind) for count, kind in out_rows],
        compiler_params=kernel_params(),
    )(scalars, *arrays)


def backward_kernel(
    mask_ref,
    core_ref,
    slope_ref,
    low_ref,
    high_ref,
    stem_ref,
    inv_ref,
    cot_ref,
    chan_ref,
    give_ref,
    keep_ref,
    part_ref,
    gated,
    row_sums,
    *,
    slots,
    rows,
    channels,
):
    phase, j = pl.program_id(0), pl.program_id(1)
    blocks = pl.num_programs(1)
    block = stem_ref.shape[1]

    @pl.when(phase == 0)
    def _():
        @pl.when(j == 0)
        def _():
            row_sums[...] = jnp.zeros_like(row_sums)

        def one(t, carry):
            lanes = pl.ds(pl.multiple_of(t * LANES, LANES), LANES)
            taps = [chan_ref[5 - k : 6 - k, lanes] for k in range(5)]
            gain = chan_ref[0:1, lanes]

            def slot(i):
                if i < 2:
                    return low_ref[i * rows : (i + 1) * rows, lanes].astype(F32)
                if i < slots + 2:
                    return slope_ref[(i - 2) * rows : (i - 1) * rows, lanes].astype(F32)
                first = (i - slots - 2) * rows
                return high_ref[first : first + rows, lanes].astype(F32)

            window = [slot(i) for i in range(4)]
            total = jnp.zeros((8, LANES), F32)
            for g in range(slots):
                window.append(slot(g + 4))
                here = slice(g * rows, (g + 1) * rows)
                d_normed = mixed_at(window, taps, mask_ref, g)
                unit = stem_ref[here, lanes] * inv_ref[here, :]
                product = d_normed * unit
                total = total + jnp.sum(product.reshape(rows // 8, 8, LANES), axis=0)
                gated[j, here, lanes] = d_normed * gain
                row_sums[here, :] = row_sums[here, :] + product * gain
                window = window[1:]
            part_ref[0:1, lanes] = jnp.sum(total, axis=0, keepdims=True)
            return carry

        lax.fori_loop(0, block // LANES, one, 0)
        part_ref[1:8, :] = jnp.zeros((7, block), F32)

    @pl.when(phase == 1)
    def _():
        @pl.when(j == 0)
        def _():
            mean = jnp.sum(row_sums[...], axis=1, keepdims=True) / channels
            row_sums[...] = jnp.broadcast_to(mean, row_sums.shape)

        def fill(out_ref):
            def one(t, carry):
                lanes = pl.ds(pl.multiple_of(t * LANES, LANES), LANES)
                inv = inv_ref[...]
                unit = stem_ref[:, lanes] * inv
                d_stem = cot_ref[:, lanes].astype(F32) + inv * (
                    gated[j, :, lanes] - unit * row_sums[...]
                )
                out_ref[:, lanes] = d_stem.astype(BF16)
                return carry

            lax.fori_loop(0, block // LANES, one, 0)

        @pl.when(j < blocks // 2)
        def _():
            fill(give_ref)

        @pl.when(j >= blocks // 2)
        def _():
            fill(keep_ref)


def backward(mask, core, slope, low, high, stem_out, inv, cot, chan, slots, blocks):
    tokens, channels = slope.shape
    block = channels // blocks
    half = blocks // 2

    def column(phase, j, mask_ref, core_ref):
        return (j + (1 - core_ref[0]) * half) % blocks

    def always(count):
        return pl.BlockSpec((count, block), lambda p, j, m, c: (0, column(p, j, m, c)))

    def first(count):
        return pl.BlockSpec(
            (count, block), lambda p, j, m, c: (0, column(p, jnp.where(p == 0, j, blocks - 1), m, c))
        )

    def second(count):
        return pl.BlockSpec(
            (count, block), lambda p, j, m, c: (0, column(p, jnp.where(p == 0, 0, j), m, c))
        )

    fixed = pl.BlockSpec((tokens, LANES), lambda p, j, m, c: (0, 0))
    return pl.pallas_call(
        functools.partial(
            backward_kernel, slots=slots, rows=tokens // slots, channels=channels
        ),
        grid_spec=pltpu.PrefetchScalarGridSpec(
            num_scalar_prefetch=2,
            grid=(2, blocks),
            in_specs=[
                first(tokens),
                first(low.shape[0]),
                first(high.shape[0]),
                always(tokens),
                fixed,
                second(tokens),
                first(8),
            ],
            out_specs=[
                pl.BlockSpec(
                    (tokens, block),
                    lambda p, j, m, c: (0, jnp.where(p == 0, 0, jnp.minimum(j, half - 1))),
                ),
                pl.BlockSpec(
                    (tokens, block),
                    lambda p, j, m, c: (0, jnp.where(p == 0, 0, jnp.maximum(j - half, 0))),
                ),
                first(8),
            ],
            scratch_shapes=[
                pltpu.VMEM((blocks, tokens, block), F32),
                pltpu.VMEM((tokens, LANES), F32),
            ],
        ),
        out_shape=[
            jax.ShapeDtypeStruct((tokens, channels // 2), BF16),
            jax.ShapeDtypeStruct((tokens, channels // 2), BF16),
            jax.ShapeDtypeStruct((8, channels), F32),
        ],
        compiler_params=kernel_params(),
    )(mask, core, slope, low, high, stem_out, inv, cot, chan)


def pixel_kernel(place_ref, keep_ref, give_ref, *refs, chips, width):
    shard_refs = refs[: 2 * chips]
    out_ref, weights, sems = refs[2 * chips :]
    core = place_ref[chips]
    half = keep_ref.shape[1]
    load_weights(place_ref, shard_refs, weights, sems)
    for f in range(2 * chips):
        wait_weights(shard_refs[0], weights, sems, f)
    own = pl.multiple_of(core * half, LANES)
    other = pl.multiple_of((1 - core) * half, LANES)
    tile = 256

    def product(lanes):
        return jnp.dot(
            keep_ref[...], weights[pl.ds(own, half), lanes], preferred_element_type=F32
        ) + jnp.dot(give_ref[...], weights[pl.ds(other, half), lanes], preferred_element_type=F32)

    def one(j, carry):
        lanes = pl.ds(pl.multiple_of(j * tile, tile), tile)
        out_ref[:, lanes] = product(lanes).astype(BF16)
        return carry

    full = width // tile
    lax.fori_loop(0, full, one, 0)
    last = round_up(width - full * tile, LANES)
    rest = product(slice(full * tile, full * tile + last))
    out_ref[:, full * tile :] = rest[:, : width - full * tile].astype(BF16)


def pixel_grads(keep, give, shards, places, width):
    tokens, half = keep.shape
    chips = len(shards) // 2
    padded = shards[0].shape[1]
    return pl.pallas_call(
        functools.partial(pixel_kernel, chips=chips, width=width),
        grid_spec=pltpu.PrefetchScalarGridSpec(
            num_scalar_prefetch=1,
            grid=(),
            in_specs=[pl.BlockSpec(memory_space=pltpu.VMEM)] * 2
            + [pl.BlockSpec(memory_space=pl.ANY)] * len(shards),
            out_specs=pl.BlockSpec(memory_space=pltpu.VMEM),
            scratch_shapes=[
                pltpu.VMEM((2 * half, padded), BF16),
                pltpu.SemaphoreType.DMA((2 * chips,)),
            ],
        ),
        out_shape=jax.ShapeDtypeStruct((tokens, width), BF16),
        compiler_params=kernel_params(),
    )(places, keep, give, *shards)


def weight_kernel(packed_ref, packed_other_ref, keep_ref, got_ref, out_ref):
    groups, height, group = out_ref.shape
    tile = 256
    for m in range(0, height, tile):
        count = min(tile, height - m)
        lanes = slice(m, m + round_up(count, LANES))
        mine = packed_ref[:, lanes].T
        theirs = packed_other_ref[:, lanes].T
        for g in range(groups):
            columns = slice(g * group, (g + 1) * group)
            total = jnp.dot(mine, keep_ref[:, columns], preferred_element_type=F32) + jnp.dot(
                theirs, got_ref[:, columns], preferred_element_type=F32
            )
            out_ref[g, m : m + count, :] = total[:count].astype(BF16)


def weight_partial(packed, packed_other, keep, got, groups, height):
    half = keep.shape[1]
    return pl.pallas_call(
        weight_kernel,
        in_specs=[pl.BlockSpec(memory_space=pltpu.VMEM)] * 4,
        out_specs=pl.BlockSpec(memory_space=pltpu.VMEM),
        out_shape=jax.ShapeDtypeStruct((groups, height, half // groups), BF16),
        compiler_params=kernel_params(),
    )(packed, packed_other, keep, got)


def wide_sum(a, b):
    return a.astype(F32) + b.astype(F32)


def halved(value, axis, bit_set, seq_bits, fsdp_bits):
    keep = lax.dynamic_index_in_dim(value, bit_set, axis, keepdims=False)
    give = lax.dynamic_index_in_dim(value, 1 - bit_set, axis, keepdims=False)
    return wide_sum(keep, swapped(give, seq_bits, fsdp_bits)).astype(BF16)


def scatter_weight(partial, seq_index, chip, core, chips, seq_size, scale):
    groups, height, group = partial.shape
    seq_bits = bits_of(seq_size)
    reduced = []
    for g in range(groups):
        order = seq_bits[::-1] if g % 2 == 0 else seq_bits
        left = list(seq_bits[::-1])
        value = partial[g].reshape((2,) * len(seq_bits) + (height // seq_size, group))
        for bit in order:
            axis = left.index(bit)
            left.pop(axis)
            value = halved(value, axis, (seq_index & bit) // bit, bit, 0)
        reduced.append(value)
    value = jnp.stack(reduced, axis=0)
    low_bits = bits_of(chips)[:-1]
    for bit in low_bits:
        count = value.shape[0]
        value = value.reshape((count // 2, 2) + value.shape[1:])
        value = halved(value, 1, (chip & bit) // bit, 0, 2 * bit)
    value = value[0]
    top = chips // 2
    arrived = sent(
        value, lambda s, f: (s, f ^ (2 * top)) if (f // 2) // top != f % 2 else None
    )
    total = (wide_sum(value, arrived) * scale).astype(BF16)
    shard = group // 2
    mine = lax.dynamic_slice_in_dim(total, core * shard, shard, axis=1)
    other = lax.dynamic_slice_in_dim(total, (1 - core) * shard, shard, axis=1)
    from_core = swapped(other, 0, 1)
    return jnp.where(chip // top == core, mine, from_core)


def shards(patches, send_slot, segments, stem_weight, norm_gain, conv_kernel, cotangent):
    seq_size, fsdp_size = lax.axis_size("seq"), lax.axis_size("fsdp")
    seq_index, fsdp_index = lax.axis_index("seq"), lax.axis_index("fsdp")
    chips, chip, core = fsdp_size // 2, fsdp_index // 2, fsdp_index % 2
    slots = send_slot.shape[1]
    tokens, width = patches.shape[1], patches.shape[2]
    rows = tokens // slots
    edge = 2 * rows
    shard = stem_weight.shape[0]
    channels = shard * fsdp_size
    padded = round_up(width + 6, LANES)
    cot = cotangent[0]

    own = jnp.concatenate(
        [
            stem_weight,
            norm_gain[:, None],
            conv_kernel.T,
            jnp.zeros((shard, padded - width - 6), BF16),
        ],
        axis=1,
    )
    lane_shards, chip_of = gather_weights(own, seq_index, chip, chips, seq_size)
    all_shards = []
    for piece in lane_shards:
        all_shards += [piece, swapped(piece, 0, 1)]
    places = jnp.stack(chip_of + [core]).astype(jnp.int32)

    packed = pack_slots(
        patches[0].reshape(slots, rows, width), send_slot[0], seq_index, seq_size, padded
    ).reshape(tokens, padded)
    packed_other = swapped(packed, 0, 1)

    def following(s, f):
        return (s + 1, f) if s + 1 < seq_size else None

    def preceding(s, f):
        return (s - 1, f) if s > 0 else None

    packed_low = sent(packed[tokens - edge :], following)
    packed_high = sent(packed[:edge], preceding)
    normed, inv, chan, stem_out = stem(
        packed, packed_low, packed_high, all_shards, places, channels
    )

    ids = segments[0]
    total_slots = ids.shape[0]
    centre = seq_index * slots + jnp.arange(slots, dtype=jnp.int32)
    near = centre[:, None] + jnp.arange(-2, 3, dtype=jnp.int32)[None, :]
    inside = (near >= 0) & (near < total_slots)
    same = ids[jnp.clip(near, 0, total_slots - 1)] == ids[centre][:, None]
    mask = (inside & same).astype(F32).reshape(-1)

    (slope_edge,) = column_call(
        functools.partial(edge_kernel, slots=slots, rows=rows),
        mask,
        [normed, cot, chan],
        [(4 * rows, BF16)],
        512,
    )
    slope_low = sent(slope_edge[edge:], following)
    slope_high = sent(slope_edge[:edge], preceding)
    features, slope, kernel_part = column_call(
        functools.partial(forward_kernel, slots=slots, rows=rows),
        mask,
        [normed, stem_out, cot, chan],
        [(tokens, BF16), (tokens, BF16), (8, F32)],
        512,
    )
    give, keep, gain_part = backward(
        mask,
        core.astype(jnp.int32).reshape(1),
        slope,
        slope_low,
        slope_high,
        stem_out,
        inv,
        cot,
        chan,
        slots,
        4,
    )
    got = swapped(give, 0, 1)
    height = round_up(width, 64)
    partial = weight_partial(packed, packed_other, keep, got, chips // 2, height)
    grad_rows = pixel_grads(keep, give, all_shards, places, width)

    scale = 1.0 / math.sqrt(tokens * seq_size * fsdp_size)
    rows_mine = scatter_weight(partial, seq_index, chip, core, chips, seq_size, scale)
    pieces = [rows_mine] + [swapped(rows_mine, o, 0) for o in range(1, seq_size)]
    grad_weight = by_position(pieces, seq_index).reshape(height, shard)[:width].T

    chan_sum = kernel_part + gain_part
    for bit in bits_of(fsdp_size):
        chan_sum = chan_sum + swapped(chan_sum, 0, bit)
    for bit in bits_of(seq_size):
        chan_sum = chan_sum + swapped(chan_sum, bit, 0)
    grad_channels = (
        lax.dynamic_slice_in_dim(chan_sum, fsdp_index * shard, shard, axis=1)[:6] * scale
    )
    return (features[None], grad_rows[None], grad_weight, grad_channels)


def solution(mesh):
    in_specs = (
        P("fsdp", "seq", None),
        P("fsdp", "seq"),
        P("fsdp", None),
        P("fsdp", None),
        P("fsdp"),
        P(None, "fsdp"),
        P("fsdp", "seq", None),
    )
    out_specs = (P("fsdp", "seq", None), P("fsdp", "seq", None), P("fsdp", None), P(None, "fsdp"))
    return jax.shard_map(shards, mesh=mesh, in_specs=in_specs, out_specs=out_specs, check_vma=False)
```

time: 528 us -> 361 us (0.68)
  waiting for transfers between devices: 278 us -> 175 us
  Pallas kernels: 0 us -> 91.2 us
  other arithmetic: 92.2 us -> 14.7 us
  blocking collectives: 33.8 us -> 0 us
  matrix products: 31.5 us -> 0 us
  starting transfers between devices: 28.5 us -> 52.9 us
  local copies, waits for them, and re-layouts: 48 us -> 24 us
  between operations: 15 us -> 1.52 us
    unnamed x4 -> x0, waiting for transfers between devices: 185 us -> none
    ppermute x4 -> x46, waiting for transfers between devices: 9 us -> 175 us  [sent(): return lax.ppermute(value, AXES, pairs)]
    pallas_call x0 -> x8, Pallas kernels: none -> 91.2 us  [the longest x2 23.4 us: column_call(): pl.pallas_call(kernel, grid_spec=pltpu.PrefetchScalarGridSpec(num_scalar_...]
    psum x1 -> x0, waiting for transfers between devices: 62.9 us -> none  [shards(): summed = lax.psum(grad_shard, 'seq')]
    ppermute x4 -> x46, starting transfers between devices: 18.6 us -> 52.9 us  [sent(): return lax.ppermute(value, AXES, pairs)]
    dot_general x3 -> x0, matrix products: 31.5 us -> none  [the longest x1 12.7 us: shards(): lax.dot_general(d_stem_low, packed, (((0,), (0,)), ((), ())), preferred_e...]
    mul x7 -> x1, other arithmetic: 28 us -> 0.69 us  [shards(): lax.dynamic_slice_in_dim(chan_sum, fsdp_index * shard, shard, axis=1)[:6]]
    reduce_sum x12 -> x4, other arithmetic: 25.3 us -> 0.61 us  [the longest x1 0.18 us: pack_slots(): jnp.sum(((owner[:, None] == owner[None, :]) & (destination[None, :] < des...]
  transfers between devices with their start and end apart: 9 -> 46, of which waited for: 6 -> 23; matrix products, arithmetic and copies ran while one was open for 15% -> 6% of each run, Pallas kernels for 0% -> 10%
where the time goes in v1:
time: 361 us; the launch traced here: 359 us
  waiting for transfers between devices  175 us (48%)
  Pallas kernels  91.2 us (25%)
  starting transfers between devices  52.9 us (15%)
  local copies, waits for them, and re-layouts  24 us (7%)
  other arithmetic  14.7 us (4%)
    ppermute x46, waiting for transfers between devices, sent(): return lax.ppermute(value, AXES, pairs)  175 us
    ppermute x46, starting transfers between devices, sent(): return lax.ppermute(value, AXES, pairs)  52.9 us
    pallas_call x2, Pallas kernels, column_call(): pl.pallas_call(kernel, grid_spec=pltpu.PrefetchScalarGridSpec(num_scalar_...  23.4 us
    pallas_call x1, Pallas kernels, stem(): pl.pallas_call(functools.partial(stem_kernel, chips=chips, channels=chann...  17.6 us
    pallas_call x1, Pallas kernels, backward(): pl.pallas_call(functools.partial(backward_kernel, slots=slots, rows=token...  16 us
    pallas_call x1, Pallas kernels, pixel_grads(): pl.pallas_call(functools.partial(pixel_kernel, chips=chips, width=width),...  13.5 us
    pallas_call x1, Pallas kernels, weight_partial(): pl.pallas_call(weight_kernel, in_specs=[pl.BlockSpec(memory_space=pltpu.V...  13.1 us
    pallas_call x2, Pallas kernels, scalar_call(): pl.pallas_call(kernel, grid_spec=pltpu.PrefetchScalarGridSpec(num_scalar_...  7.69 us
  transfers between devices with their start and end apart: 46, of which 23 were waited for; matrix products, arithmetic and copies ran while one was open for 6% of the time, Pallas kernels for 10%

profile of v1, /device:TPU:0, one launch (start us, length us, event | category | flops | bytes accessed | tf_op | source)
XLA Modules:
  0.0 359.4 jit_solution(2926565614403267367)
XLA Ops:
  6.2 6.4 %collective-permute-start.10 = (bf16[256,1280]{1,0:T(8,128)(2,1)S(1)}, bf16[256,1280]{1,0:T(8,128)(2,1)}, u32[]{:S(2)}, u32[]{:S(2)}) collective-permute-start(bf16[256,1280]{1,0:T(8,128)(2,1)S(1)} %pad_maximum_fusion.6), channel_id=1, source_target_pairs={{0,2},{1,3},{2,4},{3,5},{4,6},{5,7},{8,10},{9,11},{10,12},{11,13},... | collective-permute-start | bytes 1966088 | tf_op jit(solution)/shard_map/ppermute | solution.py:35
  16.4 8.1 %collective-permute-done.9 = bf16[256,1280]{1,0:T(8,128)(2,1)S(1)} collective-permute-done((bf16[256,1280]{1,0:T(8,128)(2,1)S(1)}, bf16[256,1280]{1,0:T(8,128)(2,1)S(1)}, u32[]{:S(2)}, u32[]{:S(2)}) %collective-permute-start.9) | collective-permute-done | bytes 655392 | tf_op jit(solution)/shard_map/ppermute | solution.py:35
  31.7 10.7 %collective-permute-done.15 = bf16[256,1280]{1,0:T(8,128)(2,1)} collective-permute-done((bf16[256,1280]{1,0:T(8,128)(2,1)S(1)}, bf16[256,1280]{1,0:T(8,128)(2,1)}, u32[]{:S(2)}, u32[]{:S(2)}) %collective-permute-start.15) | collective-permute-done | bytes 655392 | tf_op jit(solution)/shard_map/ppermute | solution.py:35
  48.9 14.9 %collective-permute-done.17 = bf16[64,1280]{1,0:T(8,128)(2,1)S(1)} collective-permute-done((bf16[64,1280]{1,0:T(8,128)(2,1)S(1)}, bf16[64,1280]{1,0:T(8,128)(2,1)S(1)}, u32[]{:S(2)}, u32[]{:S(2)}) %collective-permute-start.17) | collective-permute-done | bytes 163872 | tf_op jit(solution)/shard_map/ppermute | solution.py:35
  69.1 12.6 %collective-permute-done.21 = bf16[256,1280]{1,0:T(8,128)(2,1)S(1)} collective-permute-done((bf16[256,1280]{1,0:T(8,128)(2,1)}, bf16[256,1280]{1,0:T(8,128)(2,1)S(1)}, u32[]{:S(2)}, u32[]{:S(2)}) %collective-permute-start.21) | collective-permute-done | bytes 655392 | tf_op jit(solution)/shard_map/ppermute | solution.py:35
  98.5 9.6 %collective-permute-done.12 = bf16[64,1280]{1,0:T(8,128)(2,1)S(1)} collective-permute-done((bf16[64,1280]{1,0:T(8,128)(2,1)S(1)}, bf16[64,1280]{1,0:T(8,128)(2,1)S(1)}, u32[]{:S(2)}, u32[]{:S(2)}) %collective-permute-start.12) | collective-permute-done | bytes 163872 | tf_op jit(solution)/shard_map/ppermute | solution.py:35
  110.9 16.5 %collective-permute-done.4.refs_1_ = bf16[8,32,1280]{2,1,0:T(8,128)(2,1)S(1)} collective-permute-done((bf16[8,32,1280]{2,1,0:T(8,128)(2,1)S(1)}, bf16[8,32,1280]{2,1,0:T(8,128)(2,1)S(1)}, u32[]{:S(2)}, u32[]{:S(2)}) %collective-permute-start.4) | collective-permute-done | bytes 655392 | tf_op jit(solution)/shard_map/ppermute | solution.py:35
  129.1 4.3 %shard_map.103 = bf16[17,32,1280]{2,1,0:T(8,128)(2,1)} custom-call(s32[17]{0:T(128)} %compare_select_fusion.4.pick_ref, bf16[17,32,1176]{2,1,0:T(8,128)(2,1)} %bitcast.161, bf16[8,32,1280]{2,1,0:T(8,128)(2,1)} %collective-permute-done.3.refs_0_, bf16[8,32,1280]{2,1,0:T(8,128)(2,1)} %copy-done.10, bf16[8,32,1280]{2,1,0:T(8,128)(2,1)} %copy-done.11), custom_call_target="tpu_custom_call" | custom-call | tf_op jit(solution)/shard_map/pallas_call | solution.py:93
  144.5 6.0 %collective-permute-done.7.high_ref = bf16[64,1280]{1,0:T(8,128)(2,1)} collective-permute-done((bf16[64,1280]{1,0:T(8,128)(2,1)}, bf16[64,1280]{1,0:T(8,128)(2,1)}, u32[]{:S(2)}, u32[]{:S(2)}) %collective-permute-start.7) | collective-permute-done | bytes 163872 | tf_op jit(solution)/shard_map/ppermute | solution.py:35
  150.5 17.6 %shard_map.104 = (bf16[672,3584]{1,0:T(8,128)(2,1)}, f32[544,128]{1,0:T(8,128)}, f32[8,3584]{1,0:T(8,128)}, f32[544,3584]{1,0:T(8,128)}) custom-call(s32[5]{0:T(128)} %stack.104.place_ref, bf16[544,1280]{1,0:T(8,128)(2,1)} %bitcast.147, bf16[64,1280]{1,0:T(8,128)(2,1)} %collective-permute-done.6.low_ref, bf16[64,1280]{1,0:T(8,128)(2,1)} %collective-permute-done.7.high_ref, ...), custom_call_target="tpu_custom_call" | custom-call | tf_op jit(solution)/shard_map/pallas_call | solution.py:284
  168.1 7.9 %shard_map.106 = bf16[128,3584]{1,0:T(8,128)(2,1)} custom-call(f32[85]{0:T(128)} %reshape.534.mask_ref, bf16[672,3584]{1,0:T(8,128)(2,1)} %get-tuple-element.20.normed_ref, bf16[544,3584]{1,0:T(8,128)(2,1)} %bitcast.141, f32[8,3584]{1,0:T(8,128)} %get-tuple-element.22.chan_ref), custom_call_target="tpu_custom_call" | custom-call | tf_op jit(solution)/shard_map/pallas_call | solution.py:385
  177.2 4.9 %collective-permute-start.27 = (bf16[64,3584]{1,0:T(8,128)(2,1)S(1)}, bf16[64,3584]{1,0:T(8,128)(2,1)S(1)}, u32[]{:S(2)}, u32[]{:S(2)}) collective-permute-start(bf16[64,3584]{1,0:T(8,128)(2,1)S(1)} %get-tuple-element.57), channel_id=1, source_target_pairs={{0,8},{1,9},{2,10},{3,11},{4,12},{5,13},{6,14},{7,15},{8,16},{9,17... | collective-permute-start | bytes 1376264 | tf_op jit(solution)/shard_map/ppermute | solution.py:35
  183.6 15.5 %shard_map.105 = (bf16[544,3584]{1,0:T(8,128)(2,1)}, bf16[544,3584]{1,0:T(8,128)(2,1)}, f32[8,3584]{1,0:T(8,128)}) custom-call(f32[85]{0:T(128)} %reshape.534.mask_ref, bf16[672,3584]{1,0:T(8,128)(2,1)} %get-tuple-element.20.normed_ref, f32[544,3584]{1,0:T(8,128)} %get-tuple-element.21.stem_ref, bf16[544,3584]{1,0:T(8,128)(2,1)} %bitcast.142, ...), custom_call_target="tpu_custom_call" | custom-call | tf_op jit(solution)/shard_map/pallas_call | solution.py:385
  199.1 3.5 collective-permute-done.28.high_ref
  203.5 16.0 %shard_map.107 = (bf16[544,1792]{1,0:T(8,128)(2,1)}, bf16[544,1792]{1,0:T(8,128)(2,1)}, f32[8,3584]{1,0:T(8,128)}) custom-call(f32[85]{0:T(128)} %reshape.534.mask_ref, s32[1]{0:T(128)} %bitcast.6.core_ref, bf16[544,3584]{1,0:T(8,128)(2,1)} %get-tuple-element.24.slope_ref, bf16[64,3584]{1,0:T(8,128)(2,1)} %copy-done.14, bf16[64,3584]{1,0:T(8,128)(2,1)} %copy-done.15, ...), custom_call_target="tpu_custom_call" | custom-call | tf_op jit(solution)/shard_map/pallas_call | solution.py:510
  220.1 5.6 %collective-permute-done.29.packed_other_ref = bf16[544,1280]{1,0:T(8,128)(2,1)} collective-permute-done((bf16[544,1280]{1,0:T(8,128)(2,1)S(1)}, bf16[544,1280]{1,0:T(8,128)(2,1)}, u32[]{:S(2)}, u32[]{:S(2)}) %collective-permute-start.29) | collective-permute-done | bytes 1392672 | tf_op jit(solution)/shard_map/ppermute | solution.py:35
  225.8 13.1 %shard_map.109 = bf16[2,1216,896]{2,1,0:T(8,128)(2,1)} custom-call(bf16[544,1280]{1,0:T(8,128)(2,1)} %bitcast.148, bf16[544,1280]{1,0:T(8,128)(2,1)} %collective-permute-done.29.packed_other_ref, bf16[544,1792]{1,0:T(8,128)(2,1)} %get-tuple-element.26.keep_ref, bf16[544,1792]{1,0:T(8,128)(2,1)} %collective-permute-done.30.got_ref), custom_call_target="tpu_custom_call" | custom-call | tf_op jit(solution)/shard_map/pallas_call | solution.py:620
  244.5 24.7 %collective-permute-done.33 = bf16[2,304,896]{2,1,0:T(8,128)(2,1)} collective-permute-done((bf16[2,304,896]{2,1,0:T(8,128)(2,1)S(1)}, bf16[2,304,896]{2,1,0:T(8,128)(2,1)}, u32[]{:S(2)}, u32[]{:S(2)}) %collective-permute-start.33) | collective-permute-done | bytes 1089568 | tf_op jit(solution)/shard_map/ppermute | solution.py:35
  275.1 10.6 %collective-permute-done.34 = bf16[304,896]{1,0:T(8,128)(2,1)} collective-permute-done((bf16[304,896]{1,0:T(8,128)(2,1)}, bf16[304,896]{1,0:T(8,128)(2,1)}, u32[]{:S(2)}, u32[]{:S(2)}) %collective-permute-start.34) | collective-permute-done | bytes 544800 | tf_op jit(solution)/shard_map/ppermute | solution.py:35
  291.5 10.7 %collective-permute-done.35 = bf16[1,304,896]{2,1,0:T(8,128)(2,1)S(1)} collective-permute-done((bf16[1,304,896]{2,1,0:T(8,128)(2,1)S(1)}, bf16[1,304,896]{2,1,0:T(8,128)(2,1)S(1)}, u32[]{:S(2)}, u32[]{:S(2)}) %collective-permute-start.35) | collective-permute-done | bytes 544800 | tf_op jit(solution)/shard_map/ppermute | solution.py:35
  304.1 16.4 %collective-permute-done.36 = bf16[304,896]{1,0:T(8,128)(2,1)S(1)} collective-permute-done((bf16[304,896]{1,0:T(8,128)(2,1)S(1)}, bf16[304,896]{1,0:T(8,128)(2,1)S(1)}, u32[]{:S(2)}, u32[]{:S(2)}) %collective-permute-start.36) | collective-permute-done | bytes 544800 | tf_op jit(solution)/shard_map/ppermute | solution.py:35
  321.0 5.5 %collective-permute-done.42 = f32[8,3584]{1,0:T(8,128)S(1)} collective-permute-done((f32[8,3584]{1,0:T(8,128)S(1)}, f32[8,3584]{1,0:T(8,128)S(1)}, u32[]{:S(2)}, u32[]{:S(2)}) %collective-permute-start.42) | collective-permute-done | bytes 114720 | tf_op jit(solution)/shard_map/ppermute | solution.py:35
  326.7 8.0 %collective-permute-done.43 = f32[8,3584]{1,0:T(8,128)S(1)} collective-permute-done((f32[8,3584]{1,0:T(8,128)S(1)}, f32[8,3584]{1,0:T(8,128)S(1)}, u32[]{:S(2)}, u32[]{:S(2)}) %collective-permute-start.43) | collective-permute-done | bytes 114720 | tf_op jit(solution)/shard_map/ppermute | solution.py:35
  342.4 13.5 %shard_map.108 = bf16[544,1176]{1,0:T(8,128)(2,1)} custom-call(s32[5]{0:T(128)} %stack.104.place_ref, bf16[544,1792]{1,0:T(8,128)(2,1)} %get-tuple-element.26.keep_ref, bf16[544,1792]{1,0:T(8,128)(2,1)} %get-tuple-element.27.give_ref, bf16[448,1280]{1,0:T(8,128)(2,1)} %copy-done.2, bf16[448,1280]{1,0:T(8,128)(2,1)} %collective-permute-done.8.refs_1_, ...), custom_call_target="tpu_custom_call" | custom-call | tf_op jit(solution)/shard_map/pallas_call | solution.py:584
  (212 shorter events, 95.4 us)
Async XLA Ops:
  4.9 19.7 %collective-permute-start.9 = (bf16[256,1280]{1,0:T(8,128)(2,1)S(1)}, bf16[256,1280]{1,0:T(8,128)(2,1)S(1)}, u32[]{:S(2)}, u32[]{:S(2)}) collective-permute-start(bf16[256,1280]{1,0:T(8,128)(2,1)S(1)} %pad_maximum_fusion.6), channel_id=1, source_target_pairs={{2,0},{3,1},{4,2},{5,3},{6,4},{7,5},{10,8},{11,9},{12,10},{13,11},... | collective-permute-start | bytes 1966088 | tf_op jit(solution)/shard_map/ppermute | solution.py:35
  6.2 19.6 %collective-permute-start.10 = (bf16[256,1280]{1,0:T(8,128)(2,1)S(1)}, bf16[256,1280]{1,0:T(8,128)(2,1)}, u32[]{:S(2)}, u32[]{:S(2)}) collective-permute-start(bf16[256,1280]{1,0:T(8,128)(2,1)S(1)} %pad_maximum_fusion.6), channel_id=1, source_target_pairs={{0,2},{1,3},{2,4},{3,5},{4,6},{5,7},{8,10},{9,11},{10,12},{11,13},... | collective-permute-start | bytes 1966088 | tf_op jit(solution)/shard_map/ppermute | solution.py:35
  12.6 32.5 %collective-permute-start.2 = (s32[17]{0:T(128)S(1)}, s32[17]{0:T(128)S(1)}, u32[]{:S(2)}, u32[]{:S(2)}) collective-permute-start(s32[17]{0:T(128)S(1)} %bitcast.180), channel_id=1, source_target_pairs={{0,24},{1,25},{2,26},{3,27},{4,28},{5,29},{6,30},{7,31},{8,16},{9,... | collective-permute-start | bytes 212 | tf_op jit(solution)/shard_map/ppermute | solution.py:35
  15.5 30.4 %collective-permute-start = (s32[17]{0:T(128)S(1)}, s32[17]{0:T(128)S(1)}, u32[]{:S(2)}, u32[]{:S(2)}) collective-permute-start(s32[17]{0:T(128)S(1)} %bitcast.181), channel_id=1, source_target_pairs={{0,8},{1,9},{2,10},{3,11},{4,12},{5,13},{6,14},{7,15},{8,0},{9,1},... | collective-permute-start | bytes 212 | tf_op jit(solution)/shard_map/ppermute | solution.py:35
  16.0 31.2 %collective-permute-start.1 = (s32[17]{0:T(128)S(1)}, s32[17]{0:T(128)S(1)}, u32[]{:S(2)}, u32[]{:S(2)}) collective-permute-start(s32[17]{0:T(128)S(1)} %bitcast.182), channel_id=1, source_target_pairs={{0,16},{1,17},{2,18},{3,19},{4,20},{5,21},{6,22},{7,23},{8,24},{9,... | collective-permute-start | bytes 212 | tf_op jit(solution)/shard_map/ppermute | solution.py:35
  42.5 108.0 %collective-permute-start.8 = (bf16[448,1280]{1,0:T(8,128)(2,1)S(1)}, bf16[448,1280]{1,0:T(8,128)(2,1)}, u32[]{:S(2)}, u32[]{:S(2)}) collective-permute-start(bf16[448,1280]{1,0:T(8,128)(2,1)S(1)} %concatenate.123.refs_0_), channel_id=1, source_target_pairs={{0,1},{1,0},{2,3},{3,2},{4,5},{5,4},{6,7},{7,6},{8,9},{9,8},{10,11... | collective-permute-start | bytes 3440648 | tf_op jit(solution)/shard_map/ppermute | solution.py:35
  42.5 68.0 %collective-permute-start.3 = (bf16[8,32,1280]{2,1,0:T(8,128)(2,1)}, bf16[8,32,1280]{2,1,0:T(8,128)(2,1)}, u32[]{:S(2)}, u32[]{:S(2)}) collective-permute-start(bf16[8,32,1280]{2,1,0:T(8,128)(2,1)} %get-tuple-element.17), channel_id=1, source_target_pairs={{0,8},{1,9},{2,10},{3,11},{4,12},{5,13},{6,14},{7,15},{8,0},{9,1},... | collective-permute-start | bytes 1966088 | tf_op jit(solution)/shard_map/ppermute | solution.py:35
  45.1 18.7 %collective-permute-start.17 = (bf16[64,1280]{1,0:T(8,128)(2,1)S(1)}, bf16[64,1280]{1,0:T(8,128)(2,1)S(1)}, u32[]{:S(2)}, u32[]{:S(2)}) collective-permute-start(bf16[64,1280]{1,0:T(8,128)(2,1)S(1)} %get-tuple-element.73), channel_id=1, source_target_pairs={{0,8},{1,9},{2,10},{3,11},{4,12},{5,13},{6,14},{7,15},{8,0},{9,1},... | collective-permute-start | bytes 491528 | tf_op jit(solution)/shard_map/ppermute | solution.py:35
  45.8 19.2 %collective-permute-start.18 = (bf16[64,1280]{1,0:T(8,128)(2,1)S(1)}, bf16[64,1280]{1,0:T(8,128)(2,1)S(1)}, u32[]{:S(2)}, u32[]{:S(2)}) collective-permute-start(bf16[64,1280]{1,0:T(8,128)(2,1)S(1)} %get-tuple-element.73), channel_id=1, source_target_pairs={{0,16},{1,17},{2,18},{3,19},{4,20},{5,21},{6,22},{7,23},{8,24},{9,... | collective-permute-start | bytes 491528 | tf_op jit(solution)/shard_map/ppermute | solution.py:35
  47.2 20.4 %collective-permute-start.19 = (bf16[64,1280]{1,0:T(8,128)(2,1)S(1)}, bf16[64,1280]{1,0:T(8,128)(2,1)S(1)}, u32[]{:S(2)}, u32[]{:S(2)}) collective-permute-start(bf16[64,1280]{1,0:T(8,128)(2,1)S(1)} %get-tuple-element.73), channel_id=1, source_target_pairs={{0,24},{1,25},{2,26},{3,27},{4,28},{5,29},{6,30},{7,31},{8,16},{9,... | collective-permute-start | bytes 491528 | tf_op jit(solution)/shard_map/ppermute | solution.py:35
  63.8 17.9 %collective-permute-start.21 = (bf16[256,1280]{1,0:T(8,128)(2,1)}, bf16[256,1280]{1,0:T(8,128)(2,1)S(1)}, u32[]{:S(2)}, u32[]{:S(2)}) collective-permute-start(bf16[256,1280]{1,0:T(8,128)(2,1)} %collective-permute-done.15), channel_id=1, source_target_pairs={{2,0},{3,1},{10,8},{11,9},{18,16},{19,17},{26,24},{27,25}} | collective-permute-start | bytes 1966088 | tf_op jit(solution)/shard_map/ppermute | solution.py:35
  97.2 30.2 %collective-permute-start.4 = (bf16[8,32,1280]{2,1,0:T(8,128)(2,1)S(1)}, bf16[8,32,1280]{2,1,0:T(8,128)(2,1)S(1)}, u32[]{:S(2)}, u32[]{:S(2)}) collective-permute-start(bf16[8,32,1280]{2,1,0:T(8,128)(2,1)S(1)} %copy-done.20), channel_id=1, source_target_pairs={{0,16},{1,17},{2,18},{3,19},{4,20},{5,21},{6,22},{7,23},{8,24},{9,... | collective-permute-start | bytes 1966088 | tf_op jit(solution)/shard_map/ppermute | solution.py:35
  108.1 20.0 %collective-permute-start.5 = (bf16[8,32,1280]{2,1,0:T(8,128)(2,1)S(1)}, bf16[8,32,1280]{2,1,0:T(8,128)(2,1)S(1)}, u32[]{:S(2)}, u32[]{:S(2)}) collective-permute-start(bf16[8,32,1280]{2,1,0:T(8,128)(2,1)S(1)} %copy-done.19), channel_id=1, source_target_pairs={{0,24},{1,25},{2,26},{3,27},{4,28},{5,29},{6,30},{7,31},{8,16},{9,... | collective-permute-start | bytes 1966088 | tf_op jit(solution)/shard_map/ppermute | solution.py:35
  108.2 42.3 %collective-permute-start.20 = (bf16[448,1280]{1,0:T(8,128)(2,1)S(1)}, bf16[448,1280]{1,0:T(8,128)(2,1)}, u32[]{:S(2)}, u32[]{:S(2)}) collective-permute-start(bf16[448,1280]{1,0:T(8,128)(2,1)S(1)} %pad_maximum_fusion.4.refs_4_), channel_id=1, source_target_pairs={{0,1},{1,0},{2,3},{3,2},{4,5},{5,4},{6,7},{7,6},{8,9},{9,8},{10,11... | collective-permute-start | bytes 3440648 | tf_op jit(solution)/shard_map/ppermute | solution.py:35
  110.4 40.1 %collective-permute-start.26 = (bf16[448,1280]{1,0:T(8,128)(2,1)S(1)}, bf16[448,1280]{1,0:T(8,128)(2,1)}, u32[]{:S(2)}, u32[]{:S(2)}) collective-permute-start(bf16[448,1280]{1,0:T(8,128)(2,1)S(1)} %pad_maximum_fusion.5.refs_6_), channel_id=1, source_target_pairs={{0,1},{1,0},{2,3},{3,2},{4,5},{5,4},{6,7},{7,6},{8,9},{9,8},{10,11... | collective-permute-start | bytes 3440648 | tf_op jit(solution)/shard_map/ppermute | solution.py:35
  127.4 23.1 %collective-permute-start.14 = (bf16[448,1280]{1,0:T(8,128)(2,1)}, bf16[448,1280]{1,0:T(8,128)(2,1)}, u32[]{:S(2)}, u32[]{:S(2)}) collective-permute-start(bf16[448,1280]{1,0:T(8,128)(2,1)} %pad_maximum_fusion.3.refs_2_), channel_id=1, source_target_pairs={{0,1},{1,0},{2,3},{3,2},{4,5},{5,4},{6,7},{7,6},{8,9},{9,8},{10,11... | collective-permute-start | bytes 3440648 | tf_op jit(solution)/shard_map/ppermute | solution.py:35
  177.2 21.9 %collective-permute-start.27 = (bf16[64,3584]{1,0:T(8,128)(2,1)S(1)}, bf16[64,3584]{1,0:T(8,128)(2,1)S(1)}, u32[]{:S(2)}, u32[]{:S(2)}) collective-permute-start(bf16[64,3584]{1,0:T(8,128)(2,1)S(1)} %get-tuple-element.57), channel_id=1, source_target_pairs={{0,8},{1,9},{2,10},{3,11},{4,12},{5,13},{6,14},{7,15},{8,16},{9,17... | collective-permute-start | bytes 1376264 | tf_op jit(solution)/shard_map/ppermute | solution.py:35
  182.1 20.6 %collective-permute-start.28 = (bf16[64,3584]{1,0:T(8,128)(2,1)S(1)}, bf16[64,3584]{1,0:T(8,128)(2,1)S(1)}, u32[]{:S(2)}, u32[]{:S(2)}) collective-permute-start(bf16[64,3584]{1,0:T(8,128)(2,1)S(1)} %get-tuple-element.56), channel_id=1, source_target_pairs={{8,0},{9,1},{10,2},{11,3},{12,4},{13,5},{14,6},{15,7},{16,8},{17,9... | collective-permute-start | bytes 1376264 | tf_op jit(solution)/shard_map/ppermute | solution.py:35
  242.9 26.2 %collective-permute-start.33 = (bf16[2,304,896]{2,1,0:T(8,128)(2,1)S(1)}, bf16[2,304,896]{2,1,0:T(8,128)(2,1)}, u32[]{:S(2)}, u32[]{:S(2)}) collective-permute-start(bf16[2,304,896]{2,1,0:T(8,128)(2,1)S(1)} %dynamic-slice_bitcast_fusion), channel_id=1, source_target_pairs={{0,8},{1,9},{2,10},{3,11},{4,12},{5,13},{6,14},{7,15},{8,0},{9,1},... | collective-permute-start | bytes 3268616 | tf_op jit(solution)/shard_map/ppermute | solution.py:35
  244.3 27.9 %collective-permute-start.31 = (bf16[2,304,896]{2,1,0:T(8,128)(2,1)}, bf16[2,304,896]{2,1,0:T(8,128)(2,1)}, u32[]{:S(2)}, u32[]{:S(2)}) collective-permute-start(bf16[2,304,896]{2,1,0:T(8,128)(2,1)} %dynamic-slice_bitcast_fusion.1), channel_id=1, source_target_pairs={{0,16},{1,17},{2,18},{3,19},{4,20},{5,21},{6,22},{7,23},{8,24},{9,... | collective-permute-start | bytes 3268616 | tf_op jit(solution)/shard_map/ppermute | solution.py:35
  302.4 18.0 %collective-permute-start.36 = (bf16[304,896]{1,0:T(8,128)(2,1)S(1)}, bf16[304,896]{1,0:T(8,128)(2,1)S(1)}, u32[]{:S(2)}, u32[]{:S(2)}) collective-permute-start(bf16[304,896]{1,0:T(8,128)(2,1)S(1)} %fusion.8), channel_id=1, source_target_pairs={{1,5},{3,7},{4,0},{6,2},{9,13},{11,15},{12,8},{14,10},{17,21},{19,... | collective-permute-start | bytes 1634312 | tf_op jit(solution)/shard_map/ppermute | solution.py:35
  335.9 20.7 %collective-permute-start.38 = (bf16[304,448]{1,0:T(8,128)(2,1)S(1)}, bf16[304,448]{1,0:T(8,128)(2,1)S(1)}, u32[]{:S(2)}, u32[]{:S(2)}) collective-permute-start(bf16[304,448]{1,0:T(8,128)(2,1)S(1)} %dynamic-slice_select_fusion), channel_id=1, source_target_pairs={{0,8},{1,9},{2,10},{3,11},{4,12},{5,13},{6,14},{7,15},{8,0},{9,1},... | collective-permute-start | bytes 817160 | tf_op jit(solution)/shard_map/ppermute | solution.py:35
  337.0 19.6 %collective-permute-start.39 = (bf16[304,448]{1,0:T(8,128)(2,1)S(1)}, bf16[304,448]{1,0:T(8,128)(2,1)S(1)}, u32[]{:S(2)}, u32[]{:S(2)}) collective-permute-start(bf16[304,448]{1,0:T(8,128)(2,1)S(1)} %dynamic-slice_select_fusion), channel_id=1, source_target_pairs={{0,16},{1,17},{2,18},{3,19},{4,20},{5,21},{6,22},{7,23},{8,24},{9,... | collective-permute-start | bytes 817160 | tf_op jit(solution)/shard_map/ppermute | solution.py:35
  338.6 18.0 %collective-permute-start.40 = (bf16[304,448]{1,0:T(8,128)(2,1)S(1)}, bf16[304,448]{1,0:T(8,128)(2,1)S(1)}, u32[]{:S(2)}, u32[]{:S(2)}) collective-permute-start(bf16[304,448]{1,0:T(8,128)(2,1)S(1)} %dynamic-slice_select_fusion), channel_id=1, source_target_pairs={{0,24},{1,25},{2,26},{3,27},{4,28},{5,29},{6,30},{7,31},{8,16},{9,... | collective-permute-start | bytes 817160 | tf_op jit(solution)/shard_map/ppermute | solution.py:35
  (44 other events, 629.3 us)

commit v2 on v0

v2 whole, which is shorter than its diff:
```python
import functools
import math

import jax
import jax.numpy as jnp
from jax import lax
from jax.experimental import pallas as pl
from jax.experimental.pallas import tpu as pltpu
from jax.sharding import PartitionSpec as P

EPSILON = 1e-06
BF16 = jnp.bfloat16
F32 = jnp.float32
LANES = 128
AXES = ("seq", "fsdp")
VMEM_BYTES = 60 * 1024 * 1024


def round_up(value, unit):
    return (value + unit - 1) // unit * unit


def kernel_params(**more):
    return pltpu.CompilerParams(vmem_limit_bytes=VMEM_BYTES, **more)


def sent(value, route):
    seq_size, fsdp_size = lax.axis_size("seq"), lax.axis_size("fsdp")
    pairs = []
    for s in range(seq_size):
        for f in range(fsdp_size):
            target = route(s, f)
            if target is not None:
                pairs.append((s * fsdp_size + f, target[0] * fsdp_size + target[1]))
    return lax.ppermute(value, AXES, pairs)


def swapped(value, seq_bits, fsdp_bits):
    return sent(value, lambda s, f: (s ^ seq_bits, f ^ fsdp_bits))


def together(*values):
    flat, tree = jax.tree.flatten(values)
    return jax.tree.unflatten(tree, lax.optimization_barrier(tuple(flat)))


def bits_of(size):
    return [1 << i for i in range(size.bit_length() - 1)]


def by_position(pieces, me):
    stack = jnp.stack(pieces, axis=0)
    count = len(pieces)
    tail = stack.shape[1:]
    for bit in bits_of(count):
        view = stack.reshape((count // (2 * bit), 2, bit) + tail)
        flipped = jnp.concatenate([view[:, 1:], view[:, :1]], axis=1)
        stack = jnp.where((me & bit) != 0, flipped, view).reshape((count,) + tail)
    return stack


def outbox_kernel(order_ref, spot_ref, frames_ref, *out_refs):
    rows, width = frames_ref.shape[1:]
    for peer, out in enumerate(out_refs):
        capacity, _, padded = out.shape
        lane = lax.broadcasted_iota(jnp.int32, (rows, LANES), 1) + (padded - LANES)
        for k in range(capacity):
            spot = spot_ref[peer * capacity + k]
            out[k, :, padded - LANES :] = jnp.where(lane == width, spot, 0.0).astype(BF16)
            out[k, :, :width] = frames_ref[order_ref[peer * capacity + k]]


def place_kernel(pick_ref, frames_ref, *refs):
    inbox, out = refs[:-1], refs[-1]
    slots, rows, width = frames_ref.shape
    total, padded = out.shape
    tokens = slots * rows
    capacity = inbox[0].shape[0]
    out[:tokens, padded - LANES :] = jnp.zeros((tokens, LANES), out.dtype)
    row = lax.broadcasted_iota(jnp.int32, (total - tokens, padded), 0)
    column = lax.broadcasted_iota(jnp.int32, (total - tokens, padded), 1)
    out[tokens:, :] = jnp.where((column == row + width) & (row < 6), 1.0, 0.0).astype(BF16)

    def one(p, carry):
        index = pick_ref[p]
        here = pl.ds(pl.multiple_of(p * rows, 16), rows)

        @pl.when(index < slots)
        def _():
            out[here, :width] = frames_ref[index]

        for peer, box in enumerate(inbox):
            first = slots + peer * capacity

            @pl.when((index >= first) & (index < first + capacity))
            def _():
                out[here, :width] = box[index - first, :, :width]

        return carry

    lax.fori_loop(0, slots, one, 0)


def scalar_call(kernel, out_shape, scalars, arrays):
    return pl.pallas_call(
        kernel,
        grid_spec=pltpu.PrefetchScalarGridSpec(
            num_scalar_prefetch=len(scalars),
            grid=(),
            in_specs=[pl.BlockSpec(memory_space=pltpu.VMEM)] * len(arrays),
            out_specs=jax.tree.map(lambda _: pl.BlockSpec(memory_space=pltpu.VMEM), out_shape),
        ),
        out_shape=out_shape,
        compiler_params=kernel_params(),
    )(*scalars, *arrays)


def outgoing(frames, destination, seq_index, seq_size, padded):
    slots, rows, _ = frames.shape
    capacity = 2 * slots // seq_size
    owner = (destination // slots) ^ seq_index
    rank = jnp.sum(
        ((owner[:, None] == owner[None, :]) & (destination[None, :] < destination[:, None])).astype(
            jnp.int32
        ),
        axis=1,
    )
    peers = jnp.arange(1, seq_size, dtype=jnp.int32)
    places = jnp.arange(capacity, dtype=jnp.int32)
    hit = (owner[None, None, :] == peers[:, None, None]) & (
        rank[None, None, :] == places[None, :, None]
    )
    order = jnp.sum(jnp.where(hit, jnp.arange(slots, dtype=jnp.int32), 0), axis=2).reshape(-1)
    spot = jnp.sum(jnp.where(hit, destination % slots + 1, 0), axis=2).reshape(-1) - 1
    return scalar_call(
        outbox_kernel,
        [jax.ShapeDtypeStruct((capacity, rows, padded), BF16)] * (seq_size - 1),
        [order, spot.astype(F32)],
        [frames],
    )


def arrivals(destination, spots, seq_index):
    slots = destination.shape[0]
    numbers = jnp.arange(slots, dtype=jnp.int32)
    local = (destination == seq_index * slots + numbers[:, None]).astype(jnp.int32)
    boxed = (spots.astype(jnp.int32).reshape(-1) == numbers[:, None]).astype(jnp.int32)
    places = slots + jnp.arange(boxed.shape[1], dtype=jnp.int32)
    return jnp.sum(local * numbers, axis=1) + jnp.sum(boxed * places, axis=1)


def chain_step(rising, falling, k, chips):
    return (
        sent(rising, lambda s, f: (s, f + 2) if k - 1 <= f // 2 < chips - 1 else None),
        sent(falling, lambda s, f: (s, f - 2) if 0 < f // 2 <= chips - k else None),
    )


def chain_slot(rising, falling, k, chip, chips):
    low = chip < chips // 2
    far = jnp.maximum(chip, chips - 1 - chip)
    towards = jnp.where(low, 1, -1)
    options = [falling[k], rising[k]]
    which = jnp.where(low, 0, 1)
    origin = chip + towards * k
    for reach in range(chips // 2, k):
        which = jnp.where(far == reach, len(options) + jnp.where(low, 1, 0), which)
        options += [falling[k - reach], rising[k - reach]]
        origin = jnp.where(far == reach, chip - towards * (k - reach), origin)
    return options, which, origin


def chosen(options, which):
    value = options[0]
    for i, option in enumerate(options[1:], 1):
        value = jnp.where(which == i, option, value)
    return value


def load_weights(place_ref, shard_refs, weights, sems, by_chip):
    pairs = len(shard_refs) // 2
    shard = shard_refs[0].shape[0]
    core = place_ref[0]
    for k in range(pairs):
        for h in range(2):
            lane = core if h == 0 else 1 - core
            row = 2 * (place_ref[1 + k] if by_chip else k) + lane
            first = pl.multiple_of(row * shard, 16)
            pltpu.make_async_copy(
                shard_refs[2 * k + h], weights.at[pl.ds(first, shard), :], sems.at[row]
            ).start()


def wait_weights(shard_ref, weights, sems, pair):
    shard = shard_ref.shape[0]
    for row in (2 * pair, 2 * pair + 1):
        pltpu.make_async_copy(
            shard_ref, weights.at[pl.ds(row * shard, shard), :], sems.at[row]
        ).wait()


def pair_product(inputs, weights, first, count, store, squares):
    total = squares[...]
    for begin in range(0, count, 256):
        size = min(256, count - begin)
        result = lax.dot_general(
            inputs[...],
            weights[first + begin : first + begin + size, :],
            (((1,), (1,)), ((), ())),
            preferred_element_type=F32,
        )
        store(begin, size, result)
        for t in range(0, size, LANES):
            part = result[:, t : t + LANES]
            total = total + part * part
    squares[...] = total


def early_kernel(place_ref, *refs, count, pairs):
    row_refs, shard_refs = refs[:count], refs[count : count + 2 * pairs]
    acc_ref, squares, weights, rows_all, sems = refs[count + 2 * pairs :]
    group = acc_ref.shape[2]
    load_weights(place_ref, shard_refs, weights, sems, False)
    begin = 0
    for ref in row_refs:
        rows_all[begin : begin + ref.shape[0]] = ref[...]
        begin += ref.shape[0]
    squares[...] = jnp.zeros_like(squares)
    for k in range(pairs):
        wait_weights(shard_refs[0], weights, sems, k)

        def store(begin, size, result, k=k):
            acc_ref[k, :, begin : begin + size] = result

        pair_product(rows_all, weights, k * group, group, store, squares)


VMEM_SPEC = pl.BlockSpec(memory_space=pltpu.VMEM)
ANY_SPEC = pl.BlockSpec(memory_space=pl.ANY)


def stem_early(row_arrays, shards, core_id):
    padded = row_arrays[0].shape[1]
    rows = sum(a.shape[0] for a in row_arrays)
    pairs = len(shards) // 2
    group = 2 * shards[0].shape[0]
    return pl.pallas_call(
        functools.partial(early_kernel, count=len(row_arrays), pairs=pairs),
        grid_spec=pltpu.PrefetchScalarGridSpec(
            num_scalar_prefetch=1,
            grid=(),
            in_specs=[VMEM_SPEC] * len(row_arrays) + [ANY_SPEC] * len(shards),
            out_specs=[VMEM_SPEC] * 2,
            scratch_shapes=[
                pltpu.VMEM((pairs * group, padded), BF16),
                pltpu.VMEM((rows, padded), BF16),
                pltpu.SemaphoreType.DMA((2 * pairs,)),
            ],
        ),
        out_shape=[
            jax.ShapeDtypeStruct((pairs, rows, group), F32),
            jax.ShapeDtypeStruct((rows, LANES), F32),
        ],
        compiler_params=kernel_params(),
    )(core_id, *row_arrays, *shards)


def gate_of(value):
    return 0.5 * jnp.tanh(0.5 * value) + 0.5


def mixed_at(window, taps, mask_ref, first):
    total = window[0] * (taps[0] * mask_ref[first])
    for k in range(1, 5):
        total = total + window[k] * (taps[k] * mask_ref[first + k])
    return total


def layer_kernel(
    place_ref, mask_ref, main_ref, low_ref, high_ref, cot_ref, cot_low_ref, cot_high_ref, *refs,
    pairs, late, slots, channels
):
    shard_refs, refs = refs[: 2 * late], refs[2 * late :]
    if pairs:
        early_main, early_halo, main_squares, halo_squares = refs[:4]
        refs = refs[4:]
    part_ref, feat_ref, stem_ref, give_ref, keep_ref = refs[:5]
    weights, rows_all, acc, cots, feats, d_stem, lanes_of_core, gated, slopes, squares, inverse = refs[5:16]
    sems, in_sems, cot_sems, out_sems = refs[16:]
    group = 2 * shard_refs[0].shape[0]
    tokens = cot_ref.shape[0]
    rows = tokens // slots
    halo, edge = low_ref.shape[0], cot_low_ref.shape[0]
    extra = main_ref.shape[0] - tokens
    body = tokens + 2 * halo
    core = place_ref[0]
    load_weights(place_ref, shard_refs, weights, sems, not pairs)
    loads = [
        pltpu.make_async_copy(cot_low_ref, cots.at[pl.ds(0, edge), :], cot_sems.at[0]),
        pltpu.make_async_copy(cot_ref, cots.at[pl.ds(edge, tokens), :], cot_sems.at[1]),
        pltpu.make_async_copy(cot_high_ref, cots.at[pl.ds(edge + tokens, edge), :], cot_sems.at[2]),
    ]
    if pairs:
        for k in range(pairs):
            lanes = pl.ds(pl.multiple_of(place_ref[1 + k] * group, LANES), group)
            for i, (ref, src, dst, size) in enumerate(
                (
                    (early_main, 0, halo, tokens),
                    (early_main, tokens, body, extra),
                    (early_halo, 0, 0, halo),
                    (early_halo, halo, halo + tokens, halo),
                )
            ):
                loads.append(
                    pltpu.make_async_copy(
                        ref.at[k, pl.ds(src, size), :],
                        acc.at[pl.ds(dst, size), lanes],
                        in_sems.at[k, i],
                    )
                )
    for copy in loads:
        copy.start()
    rows_all[0:halo] = low_ref[...]
    rows_all[halo : halo + tokens] = main_ref[0:tokens]
    rows_all[halo + tokens : body] = high_ref[...]
    rows_all[body : body + extra] = main_ref[tokens:]
    if pairs:
        squares[0:halo] = halo_squares[0:halo]
        squares[halo : halo + tokens] = main_squares[0:tokens]
        squares[halo + tokens : body] = halo_squares[halo:]
        squares[body:] = main_squares[tokens:]
        wait_weights(shard_refs[0], weights, sems, 0)

        def store(begin, size, result):
            first = pl.multiple_of(place_ref[1 + pairs] * group + begin, LANES)
            acc[:, pl.ds(first, size)] = result

        pair_product(rows_all, weights, 0, group, store, squares)
    else:
        squares[...] = jnp.zeros_like(squares)
        for z in range(late):
            wait_weights(shard_refs[0], weights, sems, z)
        tile = 256

        def one(j, carry):
            first = pl.multiple_of(j * tile, tile)
            result = lax.dot_general(
                rows_all[...],
                weights[pl.ds(first, tile), :],
                (((1,), (1,)), ((), ())),
                preferred_element_type=F32,
            )
            acc[:, pl.ds(first, tile)] = result
            total = squares[...]
            for t in range(0, tile, LANES):
                total = total + result[:, t : t + LANES] * result[:, t : t + LANES]
            squares[...] = total
            return carry

        lax.fori_loop(0, channels // tile, one, 0)
    mean = jnp.sum(squares[...], axis=1, keepdims=True) / channels
    inverse[...] = jnp.broadcast_to(lax.rsqrt(mean + EPSILON), inverse.shape)
    squares[...] = jnp.zeros_like(squares)
    for copy in loads:
        copy.wait()

    def columns(t, carry):
        lanes = pl.ds(pl.multiple_of(t * LANES, LANES), LANES)
        gain = acc[body : body + 1, lanes]
        taps = [acc[body + 1 + k : body + 2 + k, lanes] for k in range(5)]

        def normed(i):
            here = slice(i * rows, (i + 1) * rows)
            return (acc[here, lanes] * inverse[here] * gain).astype(BF16).astype(F32)

        window = [normed(i) for i in range(4)]
        sums = [jnp.zeros((8, LANES), F32) for _ in range(5)]
        for i in range(slots + 4):
            window.append(normed(i + 4))
            mixed = mixed_at(window, taps, mask_ref, 5 * i)
            gate = gate_of(mixed)
            smooth = mixed * gate
            here = slice(i * rows, (i + 1) * rows)
            up = cots[here, lanes].astype(F32)
            slope = (up * (gate + smooth - smooth * gate)).astype(BF16).astype(F32)
            slopes[here] = slope
            if 2 <= i < slots + 2:
                own = slice((i - 2) * rows, (i - 1) * rows)
                stem = acc[halo + (i - 2) * rows : halo + (i - 1) * rows, lanes]
                feats[own, lanes] = (stem + smooth).astype(BF16)
                for k in range(5):
                    product = (slope * window[k]).reshape(rows // 8, 8, LANES)
                    sums[k] = sums[k] + jnp.sum(product, axis=0) * mask_ref[5 * i + k]
            window = window[1:]
        for k in range(5):
            part_ref[1 + k : 2 + k, lanes] = jnp.sum(sums[k], axis=0, keepdims=True)
        part_ref[6:8, lanes] = jnp.zeros((2, LANES), F32)
        total = jnp.zeros((8, LANES), F32)
        for p in range(slots):
            window = [slopes[(p + o) * rows : (p + o + 1) * rows] for o in range(5)]
            own = slice(p * rows, (p + 1) * rows)
            here = slice(halo + p * rows, halo + (p + 1) * rows)
            d_normed = mixed_at(window, taps[::-1], mask_ref, 5 * (p + 2))
            product = d_normed * (acc[here, lanes] * inverse[here])
            total = total + jnp.sum(product.reshape(rows // 8, 8, LANES), axis=0)
            gated[own, lanes] = d_normed * gain
            squares[own] = squares[own] + product * gain
        part_ref[0:1, lanes] = jnp.sum(total, axis=0, keepdims=True)
        return carry

    copies = []
    parts = 4
    size = channels // parts
    for i in range(parts):
        lax.fori_loop(i * size // LANES, (i + 1) * size // LANES, columns, 0)
        lanes = pl.ds(i * size, size)
        copy = pltpu.make_async_copy(feats.at[:, lanes], feat_ref.at[:, lanes], out_sems.at[i])
        copy.start()
        copies.append(copy)
    mean = jnp.sum(squares[0:tokens], axis=1, keepdims=True) / channels
    squares[0:tokens] = jnp.broadcast_to(mean, (tokens, LANES))

    def finish_columns(t, carry):
        lanes = pl.ds(pl.multiple_of(t * LANES, LANES), LANES)
        inv = inverse[halo : halo + tokens]
        unit = acc[halo : halo + tokens, lanes] * inv
        value = cots[edge : edge + tokens, lanes].astype(F32) + inv * (
            gated[:, lanes] - unit * squares[0:tokens]
        )
        d_stem[:, lanes] = value.astype(BF16)
        return carry

    lax.fori_loop(0, channels // LANES, finish_columns, 0)
    copies.append(pltpu.make_async_copy(d_stem, stem_ref, out_sems.at[parts]))
    copies[-1].start()
    shard = group // 2
    room = lanes_of_core.shape[2] // (channels // group)
    for f in range(channels // shard):
        first = f // 2 * room
        lanes_of_core[f % 2, :, first : first + shard] = d_stem[:, f * shard : (f + 1) * shard]
        if room > shard:
            lanes_of_core[f % 2, :, first + shard : first + room] = jnp.zeros(
                (tokens, room - shard), BF16
            )
    for h, ref in enumerate((keep_ref, give_ref)):
        copy = pltpu.make_async_copy(
            lanes_of_core.at[(core + h) % 2], ref, out_sems.at[parts + 1 + h]
        )
        copy.start()
        copies.append(copy)
    for copy in copies:
        copy.wait()


def layer(main, low, high, cot, cot_low, cot_high, shards, early, places, mask, slots, channels):
    tokens = cot.shape[0]
    padded = main.shape[1]
    halo, edge = low.shape[0], cot_low.shape[0]
    total = main.shape[0] + 2 * halo
    late = len(shards) // 2
    pairs = early[0].shape[0] if early else 0
    shard = shards[0].shape[0]
    half = channels // (2 * shard) * round_up(shard, LANES)
    return pl.pallas_call(
        functools.partial(layer_kernel, pairs=pairs, late=late, slots=slots, channels=channels),
        grid_spec=pltpu.PrefetchScalarGridSpec(
            num_scalar_prefetch=2,
            grid=(),
            in_specs=[VMEM_SPEC] * 3
            + [ANY_SPEC] * 3
            + [ANY_SPEC] * len(shards)
            + ([ANY_SPEC] * 2 + [VMEM_SPEC] * 2 if pairs else []),
            out_specs=[VMEM_SPEC] + [ANY_SPEC] * 4,
            scratch_shapes=[
                pltpu.VMEM((late * 2 * shards[0].shape[0], padded), BF16),
                pltpu.VMEM((total, padded), BF16),
                pltpu.VMEM((total, channels), F32),
                pltpu.VMEM((tokens + 2 * edge, channels), BF16),
                pltpu.VMEM((tokens, channels), BF16),
                pltpu.VMEM((tokens, channels), BF16),
                pltpu.VMEM((2, tokens, half), BF16),
                pltpu.VMEM((tokens, channels), F32),
                pltpu.VMEM((tokens + 2 * edge, LANES), F32),
                pltpu.VMEM((total, LANES), F32),
                pltpu.VMEM((total, LANES), F32),
                pltpu.SemaphoreType.DMA((2 * late,)),
                pltpu.SemaphoreType.DMA((max(pairs, 1), 4)),
                pltpu.SemaphoreType.DMA((3,)),
                pltpu.SemaphoreType.DMA((7,)),
            ],
        ),
        out_shape=[
            jax.ShapeDtypeStruct((8, channels), F32),
            jax.ShapeDtypeStruct((tokens, channels), BF16),
            jax.ShapeDtypeStruct((tokens, channels), BF16),
            jax.ShapeDtypeStruct((tokens, half), BF16),
            jax.ShapeDtypeStruct((tokens, half), BF16),
        ],
        compiler_params=kernel_params(),
    )(places, mask, main, low, high, cot, cot_low, cot_high, *shards, *early)


def pixel_kernel(place_ref, d_stem_ref, *refs, chips, begin, tile):
    shard_refs, refs = refs[: 2 * chips], refs[2 * chips :]
    before = refs[0] if begin else None
    out_ref, weights, sems = refs[1:] if begin else refs
    width = out_ref.shape[1] - begin
    lanes = pl.ds(begin, weights.shape[1])
    load_weights(place_ref, [r.at[:, lanes] for r in shard_refs], weights, sems, True)
    for z in range(chips):
        wait_weights(shard_refs[0].at[:, lanes], weights, sems, z)
    if begin:
        out_ref[:, :begin] = before[...]
    for first in range(0, width, tile):
        size = min(tile, width - first)
        columns = slice(first, first + round_up(size, LANES))
        value = jnp.dot(d_stem_ref[...], weights[:, columns], preferred_element_type=F32)
        out_ref[:, begin + first : begin + first + size] = value[:, :size].astype(BF16)


def pixel_grads(d_stem, shards, places, begin, end, before=None):
    tokens, channels = d_stem.shape
    chips = len(shards) // 2
    lanes = round_up(end - begin, LANES)
    return pl.pallas_call(
        functools.partial(pixel_kernel, chips=chips, begin=begin, tile=256),
        grid_spec=pltpu.PrefetchScalarGridSpec(
            num_scalar_prefetch=1,
            grid=(),
            in_specs=[VMEM_SPEC]
            + [ANY_SPEC] * len(shards)
            + ([VMEM_SPEC] if begin else []),
            out_specs=VMEM_SPEC,
            scratch_shapes=[
                pltpu.VMEM((channels, lanes), BF16),
                pltpu.SemaphoreType.DMA((2 * chips,)),
            ],
        ),
        out_shape=jax.ShapeDtypeStruct((tokens, end), BF16),
        compiler_params=kernel_params(),
    )(places, d_stem, *shards, *([before] if begin else []))


def turn_kernel(first_ref, second_ref, out_ref, *, tokens):
    height, depth = out_ref.shape
    out_ref[:, 2 * tokens :] = jnp.zeros((height, depth - 2 * tokens), BF16)
    both = jnp.concatenate([first_ref[:tokens], second_ref[:tokens]], axis=0)
    for m in range(0, first_ref.shape[1], LANES):
        count = min(LANES, height - m)
        if count > 0:
            out_ref[m : m + count, : 2 * tokens] = both[:, m : m + LANES].T[:count]


def turned(packed, packed_other, height, tokens):
    return pl.pallas_call(
        functools.partial(turn_kernel, tokens=tokens),
        in_specs=[VMEM_SPEC] * 2,
        out_specs=VMEM_SPEC,
        out_shape=jax.ShapeDtypeStruct((height, round_up(2 * tokens, LANES)), BF16),
        compiler_params=kernel_params(),
    )(packed, packed_other)


def halves_beside(value, shard):
    rows = value.shape[0] // 2
    return value[:rows, :shard], value[rows:, :shard]


def weight_kernel(where_ref, pixels_ref, keep_ref, got_ref, *refs, bits, share, line_share, shard, give):
    outs, (d_stem, left, line, sems, left_sems) = refs[:3], refs[3:]
    tokens = keep_ref.shape[0]
    seq_index, chip = where_ref[0], where_ref[1]
    seq_size = 2 * outs[0].shape[1]
    half = seq_size // 2
    chips = 2 * outs[0].shape[0]
    room = d_stem.shape[1] // chips
    arrive = [[] for _ in range(chips + 1)]
    for g, bit in enumerate(bits):
        mine = (seq_index // bit) % 2
        wanted = 1 - mine if give else mine
        for i in range(half):
            p = (i // bit) * (2 * bit) + i % bit + bit * wanted
            arrive[g * (chips // 2)].append(
                pltpu.make_async_copy(
                    pixels_ref.at[pl.ds(pl.multiple_of(p * share, 16), share), :],
                    left.at[g, pl.ds(i * share, share), :],
                    left_sems.at[g, i],
                )
            )
        for z in range(g * (chips // 2), (g + 1) * (chips // 2)):
            lanes = pl.ds(z * room, room)
            for h, ref in enumerate((keep_ref, got_ref)):
                arrive[z].append(
                    pltpu.make_async_copy(
                        ref.at[:, lanes],
                        d_stem.at[pl.ds(h * tokens, tokens), lanes],
                        sems.at[2 * z + h],
                    )
                )
    arrive[chips].append(
        pltpu.make_async_copy(
            pixels_ref.at[pl.ds(seq_size * share, line.shape[0]), :], line, sems.at[2 * chips]
        )
    )
    for copy in sum(arrive, []):
        copy.start()
    extra = d_stem.shape[0] - 2 * tokens
    d_stem[2 * tokens :, :] = jnp.zeros((extra, d_stem.shape[1]), BF16)

    def fill(out, value, count, rows):
        for i in range(count):
            low, high = halves_beside(value[i * rows : (i + 1) * rows], shard)
            out[i, :, :shard] = low.astype(out.dtype)
            out[i, :, shard:] = high.astype(out.dtype)

    for g in range(2):
        for z in range(chips // 2):
            for copy in arrive[g * (chips // 2) + z]:
                copy.wait()
            first = (g * (chips // 2) + z) * room
            value = jnp.dot(
                left[g], d_stem[:, first : first + room], preferred_element_type=F32
            )
            fill(outs[g].at[z], value, half, share)
    for copy in arrive[chips]:
        copy.wait()
    mine = chip % 2
    wanted = 1 - mine if give else mine
    for i in range(chips // 2):
        columns = pl.ds(pl.multiple_of((2 * i + wanted) * room, LANES), room)
        value = jnp.dot(line[...], d_stem[:, columns], preferred_element_type=F32)
        fill(outs[2].at[i], value, seq_size, line_share)


def weight_part(pixels, keep, got, where, chips, seq_size, shard, share, line_share, bits, give):
    half = keep.shape[1]
    height, depth = pixels.shape
    kind = BF16 if give else F32
    plane = jax.ShapeDtypeStruct((chips // 2, seq_size // 2, share // 2, 2 * shard), kind)
    line = jax.ShapeDtypeStruct((chips // 2, seq_size, line_share // 2, 2 * shard), kind)
    return pl.pallas_call(
        functools.partial(
            weight_kernel, bits=bits, share=share, line_share=line_share, shard=shard, give=give
        ),
        grid_spec=pltpu.PrefetchScalarGridSpec(
            num_scalar_prefetch=1,
            grid=(),
            in_specs=[ANY_SPEC] * 3,
            out_specs=[VMEM_SPEC] * 3,
            scratch_shapes=[
                pltpu.VMEM((depth, half), BF16),
                pltpu.VMEM((2, seq_size // 2 * share, depth), BF16),
                pltpu.VMEM((seq_size * line_share, depth), BF16),
                pltpu.SemaphoreType.DMA((2 * chips + 1,)),
                pltpu.SemaphoreType.DMA((2, seq_size // 2)),
            ],
        ),
        out_shape=[plane, plane, line],
        compiler_params=kernel_params(),
    )(where, pixels, keep, got)


def bit_at(index, bit):
    return (index // bit) % 2


def sums_kernel(at_ref, *refs, plan):
    count = sum(n for alternatives, _, _ in plan for n in alternatives)
    ins, outs = list(refs[:count]), list(refs[count:])
    for alternatives, selector, keep in plan:
        totals = []
        for n in alternatives:
            terms, ins = ins[:n], ins[n:]
            total = terms[0][...].astype(F32)
            for term in terms[1:]:
                total = total + term[...].astype(F32)
            totals.append(total)
        if selector is None:
            give = kept = totals[0]
        else:
            upper = at_ref[selector] == 1
            give = jnp.where(upper, totals[0], totals[1])
            kept = jnp.where(upper, totals[1], totals[0])
        out = outs.pop(0)
        out[...] = give.astype(out.dtype)
        if keep:
            outs.pop(0)[...] = kept


def sums(units):
    scalars, arrays, in_specs, outs, plan = [], [], [], [], []

    def scalar(value):
        scalars.append(value)
        return len(scalars) - 1

    def spec(array, places):
        lead = [None if at is not None else array.shape[d] for d, at in enumerate(places)]
        return pl.BlockSpec(
            tuple(lead) + tuple(array.shape[-2:]),
            lambda i, at_ref: tuple(0 if p is None else at_ref[p] for p in places) + (0, 0),
        )

    for alternatives, selector, kind in units:
        for terms in alternatives:
            for array, index in terms:
                places = [None if at is None else scalar(at) for at in index]
                arrays.append(array)
                in_specs.append(spec(array, places))
                shape = tuple(
                    array.shape[d] for d, at in enumerate(index) if at is None
                ) + tuple(array.shape[-2:])
        keep = len(alternatives) > 1
        plan.append(
            ([len(t) for t in alternatives], scalar(selector) if keep else None, keep)
        )
        outs.append(jax.ShapeDtypeStruct(shape, kind))
        if keep:
            outs.append(jax.ShapeDtypeStruct(shape, F32))
    if not scalars:
        scalars = [jnp.int32(0)]

    def whole(shape):
        return pl.BlockSpec(shape, lambda i, at_ref: (0,) * len(shape))

    results = list(
        pl.pallas_call(
            functools.partial(sums_kernel, plan=plan),
            grid_spec=pltpu.PrefetchScalarGridSpec(
                num_scalar_prefetch=1,
                grid=(1,),
                in_specs=in_specs,
                out_specs=[whole(o.shape) for o in outs],
            ),
            out_shape=outs,
            compiler_params=kernel_params(),
        )(jnp.stack([jnp.asarray(s, jnp.int32) for s in scalars]), *arrays)
    )
    return [(results.pop(0), results.pop(0) if keep else None) for _, _, keep in plan]


def at_own(terms, mine, done, label=None):
    return [
        (array, [1 - mine[b] if b == label else mine[b] if b in done else None for b in labels])
        for array, labels in terms
    ]


def split_view(array, labels):
    return array.reshape((2,) * len(labels) + tuple(array.shape[-2:]))


def route_of(label):
    axis, bit = label
    if axis == "seq":
        return lambda s, f: (s ^ bit, f)
    return lambda s, f: (s, f ^ (2 * bit))


def without(labels, done):
    return [label for label in labels if label not in done]


def halving(gives, keeps, labels, orders, mine, last=None):
    came = yield gives, [route_of(order[0]) for order in orders]
    terms = []
    for keep, (arrived, _, _), order in zip(keeps, came, orders):
        rest = without(labels, order[:1])
        terms.append([(split_view(keep, rest), rest), (split_view(arrived, rest), rest)])
    for i in range(1, len(orders[0])):
        units = [
            ([at_own(t, mine, order[:i], order[i])], None, BF16) for t, order in zip(terms, orders)
        ]
        came = yield units, [route_of(order[i]) for order in orders]
        for t, (arrived, _, _), order in zip(terms, came, orders):
            rest = without(labels, order[: i + 1])
            t.append((split_view(arrived, rest), rest))
    final = [at_own(t, mine, order) for t, order in zip(terms, orders)]
    if last is not None:
        ((arrived, kept, _),) = yield [(final, mine[last], BF16)], [route_of(last)]
        final = [[(kept, []), (arrived, [])]]
    yield final[0], None


def all_sum(value, routes):
    ((came, _, give),) = yield [value], routes[:1]
    for route in routes[1:]:
        ((came, _, give),) = yield [([[(give, []), (came, [])]], None, F32)], [route]
    yield (give, came), None


def in_rounds(chains, beside):
    waiting = [next(chain) for chain in chains]
    first, done = True, None
    while any(routes is not None for _, routes in waiting):
        units = [u for values, routes in waiting if routes is not None for u in values]
        routes = [r for _, some in waiting if some is not None for r in some]
        ready = [(value, None) for value in units] if first else sums(units)
        first = False
        came = [sent(give, route) for (give, _), route in zip(ready, routes)]
        if beside:
            if done is not None:
                ready, done = together(ready, done)
            done = beside[0](done)
            beside = beside[1:]
            came, done = together(came, done)
        else:
            (came,) = together(came)
        arrived = [(value, kept, give) for value, (give, kept) in zip(came, ready)]
        for i, (values, some) in enumerate(waiting):
            if some is not None:
                mine, arrived = arrived[: len(values)], arrived[len(values) :]
                waiting[i] = chains[i].send(mine)
    return [values for values, _ in waiting], done


def finish_kernel(at_ref, *refs, counts, scale):
    ins, out_ref = list(refs[:-1]), refs[-1]
    shard = out_ref.shape[1]
    begin = 0
    for n in counts:
        terms, ins = ins[:n], ins[n:]
        total = terms[0][...].astype(F32)
        for term in terms[1:]:
            total = total + term[...].astype(F32)
        total = (total * scale).astype(BF16)
        for part in (total[:, :shard], total[:, shard:]):
            out_ref[begin : begin + part.shape[0], :] = part
            begin += part.shape[0]


def finish(chains, scale):
    scalars, arrays, in_specs, height = [], [], [], 0
    for terms in chains:
        for array, index in terms:
            first = len(scalars)
            scalars += index
            arrays.append(array)
            in_specs.append(
                pl.BlockSpec(
                    (None,) * len(index) + tuple(array.shape[-2:]),
                    lambda i, at_ref, first=first, n=len(index): tuple(
                        at_ref[first + d] for d in range(n)
                    )
                    + (0, 0),
                )
            )
        height += 2 * terms[0][0].shape[-2]
    shard = arrays[0].shape[-1] // 2
    return pl.pallas_call(
        functools.partial(finish_kernel, counts=[len(t) for t in chains], scale=scale),
        grid_spec=pltpu.PrefetchScalarGridSpec(
            num_scalar_prefetch=1,
            grid=(1,),
            in_specs=in_specs,
            out_specs=pl.BlockSpec((height, shard), lambda i, at_ref: (0, 0)),
        ),
        out_shape=jax.ShapeDtypeStruct((height, shard), BF16),
        compiler_params=kernel_params(),
    )(jnp.stack([jnp.asarray(s, jnp.int32) for s in scalars]), *arrays)


def shards(patches, send_slot, segments, stem_weight, norm_gain, conv_kernel, cotangent):
    seq_size, fsdp_size = lax.axis_size("seq"), lax.axis_size("fsdp")
    seq_index, fsdp_index = lax.axis_index("seq"), lax.axis_index("fsdp")
    chips, chip, core = fsdp_size // 2, fsdp_index // 2, fsdp_index % 2
    slots = send_slot.shape[1]
    tokens, width = patches.shape[1], patches.shape[2]
    rows = tokens // slots
    edge = 2 * rows
    shard = stem_weight.shape[0]
    channels = shard * fsdp_size
    padded = round_up(width + 6, LANES)
    capacity = 2 * slots // seq_size
    cot = cotangent[0]
    core_id = core.astype(jnp.int32).reshape(1)

    def following(s, f):
        return (s + 1, f) if s + 1 < seq_size else None

    def preceding(s, f):
        return (s - 1, f) if s > 0 else None

    tail, head = cot[tokens - edge :], cot[:edge]
    own = jnp.concatenate(
        [
            stem_weight,
            norm_gain[:, None],
            conv_kernel.T,
            jnp.zeros((shard, padded - width - 6), BF16),
        ],
        axis=1,
    )
    own, tail, patches = together(own, tail, patches)
    frames = patches[0].reshape(slots, rows, width)
    boxes = outgoing(frames, send_slot[0], seq_index, seq_size, padded)
    rising, falling = {0: own}, {0: own}
    own_core = swapped(own, 0, 1)
    boxes, own_core = together(boxes, own_core)
    inbox = [None] * (seq_size - 1)
    direct = [o for o in range(1, seq_size) if o.bit_count() % 2 == 1]
    others = [o for o in range(1, seq_size) if o.bit_count() % 2 == 0]
    split = 2 * shard % LANES == 0 and chips == 4
    lane_shards, core_shards, chip_of = [own], [own_core], [chip]
    early = []
    spots = [None] * (seq_size - 1)

    def arrive(numbers, boxes):
        for o, box in zip(numbers, boxes):
            inbox[o - 1], spots[o - 1] = box, box[:, 0, width]

    def add_shard(k):
        options, which, origin = chain_slot(rising, falling, k, chip, chips)
        lane_shards.append(chosen(options, which))
        core_shards.append(swapped(lane_shards[-1], 0, 1))
        chip_of.append(origin)

    for k in range(1, chips):
        rising[k], falling[k] = chain_step(rising[k - 1], falling[k - 1], k, chips)
        if k == 1:
            came = [swapped(boxes[o - 1], o, 0) for o in direct]
            rising, falling, came, boxes, tail, head = together(
                rising, falling, came, boxes, tail, head
            )
            arrive(direct, came)
        elif k == 2:
            came = [swapped(boxes[o - 1], o, 0) for o in others]
            cot_low = sent(tail, following)
            if split:
                add_shard(1)
            rising, falling, cot_low, came, core_shards, lane_shards, spots, head = together(
                rising, falling, cot_low, came, core_shards, lane_shards, spots, head
            )
            arrive(others, came)
            cot_high = sent(head, preceding)
            pick = arrivals(send_slot[0], jnp.stack(spots, axis=0), seq_index)
            main = scalar_call(
                place_kernel,
                jax.ShapeDtypeStruct((tokens + 16, padded), BF16),
                [pick],
                [frames] + inbox,
            )
            if split:
                add_shard(2)
                main, lane_shards, core_shards = together(main, lane_shards, core_shards)
            low = sent(main[tokens - 2 * edge : tokens], following)
            high = sent(main[: 2 * edge], preceding)
        elif k == 3 and split:
            pairs = [v for both in zip(lane_shards, core_shards) for v in both]
            early_main, main_squares = stem_early([main], pairs, core_id)
            rising, falling, early_main, low, high, cot_high, main = together(
                rising, falling, early_main, low, high, cot_high, main
            )
        else:
            rising, falling = together(rising, falling)
    for k in range(len(lane_shards), chips):
        add_shard(k)
    height = round_up(width, 64 * seq_size)
    main_other = swapped(main, 0, 1)
    places = jnp.stack([core] + chip_of).astype(jnp.int32)
    all_pairs = [v for both in zip(lane_shards, core_shards) for v in both]
    late_pairs = all_pairs
    if split:
        late_pairs = all_pairs[len(pairs) :]
        early_halo, halo_squares = stem_early([low, high], pairs, core_id)
        early_halo, main_other = together(early_halo, main_other)
        early = [early_main, early_halo, main_squares, halo_squares]

    ids = segments[0]
    total_slots = ids.shape[0]
    centre = seq_index * slots + jnp.arange(-2, slots + 2, dtype=jnp.int32)
    near = centre[:, None] + jnp.arange(-2, 3, dtype=jnp.int32)[None, :]
    inside = (near >= 0) & (near < total_slots) & ((centre >= 0) & (centre < total_slots))[:, None]
    same = (
        ids[jnp.clip(near, 0, total_slots - 1)] == ids[jnp.clip(centre, 0, total_slots - 1)][:, None]
    )
    mask = (inside & same).astype(F32).reshape(-1)
    chan_part, features, d_stem, give, keep = layer(
        main, low, high, cot, cot_low, cot_high, late_pairs, early, places, mask, slots, channels
    )
    chan_part = chan_part + swapped(chan_part, 0, 1)
    got = swapped(give, 0, 1)
    pixels = turned(main, main_other, height, tokens)
    middle = round_up(width // 2, LANES)

    seq_bits = bits_of(seq_size)
    chip_bits = bits_of(chips)
    line_share = height // seq_size // 4 // 32 * 32
    share = height // seq_size - line_share
    where = jnp.stack([seq_index, chip]).astype(jnp.int32)
    first_bits = [seq_bits[0], seq_bits[-1]]
    sizes = (chips, seq_size, shard, share, line_share, first_bits)
    gives = weight_part(pixels, keep, got, where, *sizes, True)
    keeps = weight_part(pixels, keep, got, where, *sizes, False)
    scale = 1.0 / math.sqrt(tokens * seq_size * fsdp_size)
    mine = {("seq", b): bit_at(seq_index, b) for b in seq_bits}
    mine |= {("chip", b): bit_at(chip, b) for b in chip_bits}
    seq_labels = [("seq", b) for b in seq_bits]
    chip_labels = [("chip", b) for b in chip_bits]
    orders = [order + chip_labels[:-1] for order in (seq_labels, seq_labels[::-1])]
    chains = [
        halving(
            gives[:2],
            keeps[:2],
            chip_labels[:-1][::-1] + seq_labels[::-1],
            orders,
            mine,
            chip_labels[-1],
        ),
        halving(
            gives[2:],
            keeps[2:],
            chip_labels[::-1] + seq_labels[::-1],
            [chip_labels + seq_labels],
            mine,
        ),
        all_sum(chan_part, [route_of(label) for label in seq_labels + chip_labels]),
    ]
    (plane, line, chan), grad_rows = in_rounds(
        chains,
        [
            lambda _: pixel_grads(d_stem, all_pairs, places, 0, middle),
            lambda before: pixel_grads(d_stem, all_pairs, places, middle, width, before),
        ],
    )
    rows_mine = finish([plane, line], scale)
    pieces = [rows_mine] + [swapped(rows_mine, o, 0) for o in range(1, seq_size)]
    stack = by_position(pieces, seq_index)
    grad_weight = jnp.concatenate(
        [stack[:, :share].reshape(-1, shard), stack[:, share:].reshape(-1, shard)], axis=0
    )[:width].T
    first = fsdp_index * shard
    grad_channels = scale * (
        lax.dynamic_slice_in_dim(chan[0], first, shard, axis=1)[:6]
        + lax.dynamic_slice_in_dim(chan[1], first, shard, axis=1)[:6]
    )
    return (features[None], grad_rows[None], grad_weight, grad_channels)


def solution(mesh):
    in_specs = (
        P("fsdp", "seq", None),
        P("fsdp", "seq"),
        P("fsdp", None),
        P("fsdp", None),
        P("fsdp"),
        P(None, "fsdp"),
        P("fsdp", "seq", None),
    )
    out_specs = (P("fsdp", "seq", None), P("fsdp", "seq", None), P("fsdp", None), P(None, "fsdp"))
    return jax.shard_map(shards, mesh=mesh, in_specs=in_specs, out_specs=out_specs, check_vma=False)
```

time: 528 us -> 298 us (0.56)
  waiting for transfers between devices: 278 us -> 87.2 us
  Pallas kernels: 0 us -> 116 us
  other arithmetic: 92.2 us -> 10.9 us
  blocking collectives: 33.8 us -> 0 us
  matrix products: 31.5 us -> 0 us
  starting transfers between devices: 28.5 us -> 54.6 us
  local copies, waits for them, and re-layouts: 48 us -> 27.3 us
  between operations: 15 us -> 1.5 us
    unnamed x4 -> x0, waiting for transfers between devices: 185 us -> none
    pallas_call x0 -> x14, Pallas kernels: none -> 116 us  [the longest x1 35.8 us: layer(): pl.pallas_call(functools.partial(layer_kernel, pairs=pairs, late=late, sl...]
    ppermute x4 -> x38, waiting for transfers between devices: 9 us -> 87.2 us  [sent(): return lax.ppermute(value, AXES, pairs)]
    psum x1 -> x0, waiting for transfers between devices: 62.9 us -> none  [shards(): summed = lax.psum(grad_shard, 'seq')]
    ppermute x4 -> x38, starting transfers between devices: 18.6 us -> 54.6 us  [sent(): return lax.ppermute(value, AXES, pairs)]
    dot_general x3 -> x0, matrix products: 31.5 us -> none  [the longest x1 12.7 us: shards(): lax.dot_general(d_stem_low, packed, (((0,), (0,)), ((), ())), preferred_e...]
    mul x7 -> x1, other arithmetic: 28 us -> 1.41 us  [shards(): scale * (lax.dynamic_slice_in_dim(chan[0], first, shard, axis=1)[:6] + la...]
    reduce_sum x12 -> x3, other arithmetic: 25.3 us -> 0.49 us  [the longest x2 0.3 us: arrivals(): return jnp.sum(local * numbers, axis=1) + jnp.sum(boxed * places, axis=1)]
  transfers between devices with their start and end apart: 9 -> 38, of which waited for: 6 -> 14; matrix products, arithmetic and copies ran while one was open for 15% -> 6% of each run, Pallas kernels for 0% -> 19%
where the time goes in v2:
time: 298 us; the launch traced here: 297 us
  Pallas kernels  116 us (39%)
  waiting for transfers between devices  87.2 us (29%)
  starting transfers between devices  54.6 us (18%)
  local copies, waits for them, and re-layouts  27.3 us (9%)
  other arithmetic  10.9 us (4%)
    ppermute x38, waiting for transfers between devices, sent(): return lax.ppermute(value, AXES, pairs)  87.2 us
    ppermute x38, starting transfers between devices, sent(): return lax.ppermute(value, AXES, pairs)  54.6 us
    pallas_call x1, Pallas kernels, layer(): pl.pallas_call(functools.partial(layer_kernel, pairs=pairs, late=late, sl...  35.8 us
    pallas_call x2, Pallas kernels, pixel_grads(): pl.pallas_call(functools.partial(pixel_kernel, chips=chips, begin=begin,...  18.7 us
    pallas_call x2, Pallas kernels, stem_early(): pl.pallas_call(functools.partial(early_kernel, count=len(row_arrays), pai...  17.9 us
    pallas_call x2, Pallas kernels, weight_part(): pl.pallas_call(functools.partial(weight_kernel, bits=bits, share=share, l...  17.7 us
    pallas_call x3, Pallas kernels, sums(): pl.pallas_call(functools.partial(sums_kernel, plan=plan), grid_spec=pltpu...  10.9 us
    unnamed x83, local copies, waits for them, and re-layouts  10.6 us
  transfers between devices with their start and end apart: 38, of which 14 were waited for; matrix products, arithmetic and copies ran while one was open for 6% of the time, Pallas kernels for 19%

profile of v2, /device:TPU:0, one launch (start us, length us, event | category | flops | bytes accessed | tf_op | source)
XLA Modules:
  0.0 296.9 jit_solution(10998912119063462990)
XLA Ops:
  5.1 4.6 %collective-permute-start = (bf16[448,1280]{1,0:T(8,128)(2,1)S(1)}, bf16[448,1280]{1,0:T(8,128)(2,1)S(1)}, u32[]{:S(2)}, u32[]{:S(2)}) collective-permute-start(bf16[448,1280]{1,0:T(8,128)(2,1)S(1)} %concatenate.33.refs_1_.refs_2_.refs_0_), channel_id=1, source_target_pairs={{0,2},{1,3},{2,4},{3,5},{4,6},{5,7},{8,10},{9,11},{10,12},{11,13},... | collective-permute-start | bytes 3440648 | tf_op jit(solution)/shard_map/ppermute | solution.py:35
  19.2 15.6 %collective-permute-done = bf16[448,1280]{1,0:T(8,128)(2,1)S(1)} collective-permute-done((bf16[448,1280]{1,0:T(8,128)(2,1)S(1)}, bf16[448,1280]{1,0:T(8,128)(2,1)S(1)}, u32[]{:S(2)}, u32[]{:S(2)}) %collective-permute-start) | collective-permute-done | bytes 1146912 | tf_op jit(solution)/shard_map/ppermute | solution.py:35
  34.8 4.3 %collective-permute-done.1 = bf16[448,1280]{1,0:T(8,128)(2,1)} collective-permute-done((bf16[448,1280]{1,0:T(8,128)(2,1)S(1)}, bf16[448,1280]{1,0:T(8,128)(2,1)}, u32[]{:S(2)}, u32[]{:S(2)}) %collective-permute-start.1) | collective-permute-done | bytes 1146912 | tf_op jit(solution)/shard_map/ppermute | solution.py:35
  50.6 20.1 %collective-permute-done.7.cot_low_ref = bf16[64,3584]{1,0:T(8,128)(2,1)S(1)} collective-permute-done((bf16[64,3584]{1,0:T(8,128)(2,1)S(1)}, bf16[64,3584]{1,0:T(8,128)(2,1)S(1)}, u32[]{:S(2)}, u32[]{:S(2)}) %collective-permute-start.7) | collective-permute-done | bytes 458784 | tf_op jit(solution)/shard_map/ppermute | solution.py:35
  80.0 4.3 %shard_map.103.refs_0_.main_ref.first_ref = bf16[560,1280]{1,0:T(8,128)(2,1)} custom-call(s32[17]{0:T(128)} %add.215.pick_ref, bf16[17,32,1176]{2,1,0:T(8,128)(2,1)} %bitcast.76, bf16[8,32,1280]{2,1,0:T(8,128)(2,1)} %collective-permute-done.3.refs_0_, bf16[8,32,1280]{2,1,0:T(8,128)(2,1)} %collective-permute-done.4.refs_1_, bf16[8,32,1280]{2,1,0:T(8,128)(2,1)} %copy-done.24), custom_call_target="tpu_custom_call" | custom-call | tf_op jit(solution)/shard_map/pallas_call | solution.py:105
  88.0 4.6 %collective-permute-start.13 = (bf16[128,1280]{1,0:T(8,128)(2,1)}, bf16[128,1280]{1,0:T(8,128)(2,1)S(1)}, u32[]{:S(2)}, u32[]{:S(2)}) collective-permute-start(bf16[128,1280]{1,0:T(8,128)(2,1)} %get-tuple-element.199), channel_id=1, source_target_pairs={{0,8},{1,9},{2,10},{3,11},{4,12},{5,13},{6,14},{7,15},{8,16},{9,17... | collective-permute-start | bytes 983048 | tf_op jit(solution)/shard_map/ppermute | solution.py:35
  94.1 10.8 %shard_map.104 = (f32[3,560,896]{2,1,0:T(8,128)}, f32[560,128]{1,0:T(8,128)}) custom-call(s32[1]{0:T(128)} %bitcast.place_ref, bf16[560,1280]{1,0:T(8,128)(2,1)} %shard_map.103.refs_0_.main_ref.first_ref, bf16[448,1280]{1,0:T(8,128)(2,1)} %copy-done.2, bf16[448,1280]{1,0:T(8,128)(2,1)} %copy-done.7, bf16[448,1280]{1,0:T(8,128)(2,1)} %copy-done.3, ...), custom_call_target="tpu_custom_call" | custom-call | tf_op jit(solution)/shard_map/pallas_call | solution.py:247
  107.6 5.7 %collective-permute-done.14.refs_1_.high_ref = bf16[128,1280]{1,0:T(8,128)(2,1)S(1)} collective-permute-done((bf16[128,1280]{1,0:T(8,128)(2,1)}, bf16[128,1280]{1,0:T(8,128)(2,1)S(1)}, u32[]{:S(2)}, u32[]{:S(2)}) %collective-permute-start.14) | collective-permute-done | bytes 327712 | tf_op jit(solution)/shard_map/ppermute | solution.py:35
  119.8 7.0 %shard_map.105 = (f32[3,256,896]{2,1,0:T(8,128)}, f32[256,128]{1,0:T(8,128)}) custom-call(s32[1]{0:T(128)} %bitcast.place_ref, bf16[128,1280]{1,0:T(8,128)(2,1)} %copy-done.21, bf16[128,1280]{1,0:T(8,128)(2,1)} %copy-done.22, bf16[448,1280]{1,0:T(8,128)(2,1)} %copy-done.2, bf16[448,1280]{1,0:T(8,128)(2,1)} %copy-done.7, bf16[448,1280]{1,0:T(8,128)(2,1)} %copy-done.3, ...), custom_call_target="tpu_custom_call" | custom-call | tf_op jit(solution)/shard_map/pallas_call | solution.py:247
  126.9 35.8 %shard_map.106 = (f32[8,3584]{1,0:T(8,128)}, bf16[544,3584]{1,0:T(8,128)(2,1)}, bf16[544,3584]{1,0:T(8,128)(2,1)}, bf16[544,2048]{1,0:T(8,128)(2,1)}, bf16[544,2048]{1,0:T(8,128)(2,1)}) custom-call(s32[5]{0:T(128)} %stack.61.place_ref, f32[105]{0:T(128)} %reshape.327.mask_ref, bf16[560,1280]{1,0:T(8,128)(2,1)} %shard_map.103.refs_0_.main_ref.first_ref, ...), custom_call_target="tpu_custom_call" | custom-call | tf_op jit(solution)/shard_map/pallas_call | solution.py:464
  163.4 4.2 %shard_map.107.pixels_ref = bf16[1280,1152]{1,0:T(8,128)(2,1)} custom-call(bf16[560,1280]{1,0:T(8,128)(2,1)} %shard_map.103.refs_0_.main_ref.first_ref, bf16[560,1280]{1,0:T(8,128)(2,1)} %collective-permute-done.17.second_ref), custom_call_target="tpu_custom_call" | custom-call | tf_op jit(solution)/shard_map/pallas_call | solution.py:555
  169.0 8.6 %shard_map.109 = (bf16[2,2,128,896]{3,2,1,0:T(8,128)(2,1)}, bf16[2,2,128,896]{3,2,1,0:T(8,128)(2,1)}, bf16[2,4,32,896]{3,2,1,0:T(8,128)(2,1)}) custom-call(s32[2]{0:T(128)} %pad_add_fusion.where_ref, bf16[1280,1152]{1,0:T(8,128)(2,1)} %shard_map.107.pixels_ref, bf16[544,2048]{1,0:T(8,128)(2,1)} %get-tuple-element.151.keep_ref, bf16[544,2048]{1,0:T(8,128)(2,1)} %copy-done.10), custom_call_target="tpu_custom_call" | custom-call | tf_op jit(solution)/shard_map/pallas_call | solution.py:641
  180.3 4.4 %collective-permute-start.21 = (bf16[2,4,32,896]{3,2,1,0:T(8,128)(2,1)}, bf16[2,4,32,896]{3,2,1,0:T(8,128)(2,1)S(1)}, u32[]{:S(2)}, u32[]{:S(2)}) collective-permute-start(bf16[2,4,32,896]{3,2,1,0:T(8,128)(2,1)} %get-tuple-element.156), channel_id=1, source_target_pairs={{0,2},{1,3},{2,0},{3,1},{4,6},{5,7},{6,4},{7,5},{8,10},{9,11},{10,... | collective-permute-start | bytes 1376264 | tf_op jit(solution)/shard_map/ppermute | solution.py:35
  186.9 9.2 %shard_map.110.refs_8_ = bf16[544,640]{1,0:T(8,128)(2,1)} custom-call(s32[5]{0:T(128)} %stack.61.place_ref, bf16[544,3584]{1,0:T(8,128)(2,1)} %get-tuple-element.158.d_stem_ref, bf16[448,1280]{1,0:T(8,128)(2,1)} %copy-done.2, bf16[448,1280]{1,0:T(8,128)(2,1)} %copy-done.7, bf16[448,1280]{1,0:T(8,128)(2,1)} %copy-done.3, bf16[448,1280]{1,0:T(8,128)(2,1)} %copy-done.8, ...), custom_call_target="tpu_custom_call" | custom-call | tf_op jit(solution)/shard_map/pallas_call | solution.py:525
  196.1 9.0 %shard_map.108 = (f32[2,2,128,896]{3,2,1,0:T(8,128)}, f32[2,2,128,896]{3,2,1,0:T(8,128)}, f32[2,4,32,896]{3,2,1,0:T(8,128)}) custom-call(s32[2]{0:T(128)} %pad_add_fusion.where_ref, bf16[1280,1152]{1,0:T(8,128)(2,1)} %shard_map.107.pixels_ref, bf16[544,2048]{1,0:T(8,128)(2,1)} %get-tuple-element.151.keep_ref, bf16[544,2048]{1,0:T(8,128)(2,1)} %copy-done.10), custom_call_target="tpu_custom_call" | custom-call | tf_op jit(solution)/shard_map/pallas_call | solution.py:641
  206.6 3.8 %shard_map.111 = (bf16[2,128,896]{2,1,0:T(8,128)(2,1)}, bf16[2,128,896]{2,1,0:T(8,128)(2,1)}, bf16[2,2,32,896]{3,2,1,0:T(8,128)(2,1)}, f32[8,3584]{1,0:T(8,128)}) custom-call(s32[6]{0:T(128)} %stack.68.at_ref, f32[2,2,128,896]{3,2,1,0:T(8,128)} %get-tuple-element.153.refs_0_, bf16[2,2,128,896]{3,2,1,0:T(8,128)(2,1)} %copy-done.11, ...), custom_call_target="tpu_custom_call" | custom-call | tf_op jit(solution)/shard_map/pallas_call | solution.py:727
  220.2 9.5 %shard_map.112 = bf16[544,1176]{1,0:T(8,128)(2,1)} custom-call(s32[5]{0:T(128)} %stack.61.place_ref, bf16[544,3584]{1,0:T(8,128)(2,1)} %get-tuple-element.158.d_stem_ref, bf16[448,1280]{1,0:T(8,128)(2,1)} %copy-done.2, bf16[448,1280]{1,0:T(8,128)(2,1)} %copy-done.7, bf16[448,1280]{1,0:T(8,128)(2,1)} %copy-done.3, bf16[448,1280]{1,0:T(8,128)(2,1)} %copy-done.8, ...), custom_call_target="tpu_custom_call" | custom-call | tf_op jit(solution)/shard_map/pallas_call | solution.py:525
  231.4 3.5 %shard_map.113 = (bf16[128,896]{1,0:T(8,128)(2,1)}, bf16[128,896]{1,0:T(8,128)(2,1)}, bf16[2,32,896]{2,1,0:T(8,128)(2,1)}, f32[8,3584]{1,0:T(8,128)}) custom-call(s32[15]{0:T(128)} %stack.149.at_ref, f32[2,2,128,896]{3,2,1,0:T(8,128)} %get-tuple-element.153.refs_0_, bf16[2,2,128,896]{3,2,1,0:T(8,128)(2,1)} %copy-done.11, bf16[2,128,896]{2,1,0:T(8,128)(2,1)} %copy-done.19, ...), custom_call_target="tpu_custom_call" | custom-call | tf_op jit(solution)/shard_map/pallas_call | solution.py:727
  237.9 4.0 %collective-permute-done.30.refs_11_.refs_5_ = bf16[2,32,896]{2,1,0:T(8,128)(2,1)S(1)} collective-permute-done((bf16[2,32,896]{2,1,0:T(8,128)(2,1)}, bf16[2,32,896]{2,1,0:T(8,128)(2,1)S(1)}, u32[]{:S(2)}, u32[]{:S(2)}) %collective-permute-start.30) | collective-permute-done | bytes 114720 | tf_op jit(solution)/shard_map/ppermute | solution.py:35
  241.9 6.6 %collective-permute-done.31.refs_13_ = f32[8,3584]{1,0:T(8,128)S(1)} collective-permute-done((f32[8,3584]{1,0:T(8,128)}, f32[8,3584]{1,0:T(8,128)S(1)}, u32[]{:S(2)}, u32[]{:S(2)}) %collective-permute-start.31) | collective-permute-done | bytes 114720 | tf_op jit(solution)/shard_map/ppermute | solution.py:35
  250.0 3.6 %shard_map.114 = (bf16[128,896]{1,0:T(8,128)(2,1)}, f32[128,896]{1,0:T(8,128)}, bf16[32,896]{1,0:T(8,128)(2,1)}, f32[8,3584]{1,0:T(8,128)}) custom-call(s32[20]{0:T(128)} %stack.147.at_ref, f32[2,2,128,896]{3,2,1,0:T(8,128)} %get-tuple-element.153.refs_0_, bf16[2,2,128,896]{3,2,1,0:T(8,128)(2,1)} %copy-done.11, bf16[2,128,896]{2,1,0:T(8,128)(2,1)} %copy-done.19, ...), custom_call_target="tpu_custom_call" | custom-call | tf_op jit(solution)/shard_map/pallas_call | solution.py:727
  260.9 8.8 %collective-permute-done.34 = f32[8,3584]{1,0:T(8,128)S(1)} collective-permute-done((f32[8,3584]{1,0:T(8,128)}, f32[8,3584]{1,0:T(8,128)S(1)}, u32[]{:S(2)}, u32[]{:S(2)}) %collective-permute-start.34) | collective-permute-done | bytes 114720 | tf_op jit(solution)/shard_map/ppermute | solution.py:35
  278.0 5.9 %collective-permute-done.35 = bf16[320,448]{1,0:T(8,128)(2,1)S(1)} collective-permute-done((bf16[320,448]{1,0:T(8,128)(2,1)}, bf16[320,448]{1,0:T(8,128)(2,1)S(1)}, u32[]{:S(2)}, u32[]{:S(2)}) %collective-permute-start.35) | collective-permute-done | bytes 286752 | tf_op jit(solution)/shard_map/ppermute | solution.py:35
  283.9 5.4 %collective-permute-done.36 = bf16[320,448]{1,0:T(8,128)(2,1)S(1)} collective-permute-done((bf16[320,448]{1,0:T(8,128)(2,1)}, bf16[320,448]{1,0:T(8,128)(2,1)S(1)}, u32[]{:S(2)}, u32[]{:S(2)}) %collective-permute-start.36) | collective-permute-done | bytes 286752 | tf_op jit(solution)/shard_map/ppermute | solution.py:35
  (208 shorter events, 96.1 us)
Async XLA Ops:
  5.1 29.7 %collective-permute-start = (bf16[448,1280]{1,0:T(8,128)(2,1)S(1)}, bf16[448,1280]{1,0:T(8,128)(2,1)S(1)}, u32[]{:S(2)}, u32[]{:S(2)}) collective-permute-start(bf16[448,1280]{1,0:T(8,128)(2,1)S(1)} %concatenate.33.refs_1_.refs_2_.refs_0_), channel_id=1, source_target_pairs={{0,2},{1,3},{2,4},{3,5},{4,6},{5,7},{8,10},{9,11},{10,12},{11,13},... | collective-permute-start | bytes 3440648 | tf_op jit(solution)/shard_map/ppermute | solution.py:35
  9.7 29.4 %collective-permute-start.1 = (bf16[448,1280]{1,0:T(8,128)(2,1)S(1)}, bf16[448,1280]{1,0:T(8,128)(2,1)}, u32[]{:S(2)}, u32[]{:S(2)}) collective-permute-start(bf16[448,1280]{1,0:T(8,128)(2,1)S(1)} %concatenate.33.refs_1_.refs_2_.refs_0_), channel_id=1, source_target_pairs={{2,0},{3,1},{4,2},{5,3},{6,4},{7,5},{10,8},{11,9},{12,10},{13,11},... | collective-permute-start | bytes 3440648 | tf_op jit(solution)/shard_map/ppermute | solution.py:35
  16.2 22.9 %collective-permute-start.3 = (bf16[8,32,1280]{2,1,0:T(8,128)(2,1)}, bf16[8,32,1280]{2,1,0:T(8,128)(2,1)}, u32[]{:S(2)}, u32[]{:S(2)}) collective-permute-start(bf16[8,32,1280]{2,1,0:T(8,128)(2,1)} %get-tuple-element.103), channel_id=1, source_target_pairs={{0,8},{1,9},{2,10},{3,11},{4,12},{5,13},{6,14},{7,15},{8,0},{9,1},... | collective-permute-start | bytes 1966088 | tf_op jit(solution)/shard_map/ppermute | solution.py:35
  17.7 21.4 %collective-permute-start.4 = (bf16[8,32,1280]{2,1,0:T(8,128)(2,1)}, bf16[8,32,1280]{2,1,0:T(8,128)(2,1)}, u32[]{:S(2)}, u32[]{:S(2)}) collective-permute-start(bf16[8,32,1280]{2,1,0:T(8,128)(2,1)} %get-tuple-element.104), channel_id=1, source_target_pairs={{0,16},{1,17},{2,18},{3,19},{4,20},{5,21},{6,22},{7,23},{8,24},{9,... | collective-permute-start | bytes 1966088 | tf_op jit(solution)/shard_map/ppermute | solution.py:35
  40.7 30.1 %collective-permute-start.9 = (bf16[448,1280]{1,0:T(8,128)(2,1)S(1)}, bf16[448,1280]{1,0:T(8,128)(2,1)S(1)}, u32[]{:S(2)}, u32[]{:S(2)}) collective-permute-start(bf16[448,1280]{1,0:T(8,128)(2,1)S(1)} %broadcast_select_fusion.2.refs_3_.refs_4_.refs_2_), channel_id=1, source_target_pairs={{0,1},{1,0},{2,3},{3,2},{4,5},{5,4},{6,7},{7,6},{8,9},{9,8},{10,11... | collective-permute-start | bytes 3440648 | tf_op jit(solution)/shard_map/ppermute | solution.py:35
  40.8 30.0 %collective-permute-start.5 = (bf16[448,1280]{1,0:T(8,128)(2,1)S(1)}, bf16[448,1280]{1,0:T(8,128)(2,1)}, u32[]{:S(2)}, u32[]{:S(2)}) collective-permute-start(bf16[448,1280]{1,0:T(8,128)(2,1)S(1)} %copy-done.16), channel_id=1, source_target_pairs={{2,4},{3,5},{4,6},{5,7},{10,12},{11,13},{12,14},{13,15},{18,20},{1... | collective-permute-start | bytes 3440648 | tf_op jit(solution)/shard_map/ppermute | solution.py:35
  42.5 32.2 %collective-permute-start.6 = (bf16[448,1280]{1,0:T(8,128)(2,1)}, bf16[448,1280]{1,0:T(8,128)(2,1)}, u32[]{:S(2)}, u32[]{:S(2)}) collective-permute-start(bf16[448,1280]{1,0:T(8,128)(2,1)} %collective-permute-done.1), channel_id=1, source_target_pairs={{2,0},{3,1},{4,2},{5,3},{10,8},{11,9},{12,10},{13,11},{18,16},{19,... | collective-permute-start | bytes 3440648 | tf_op jit(solution)/shard_map/ppermute | solution.py:35
  43.8 27.0 %collective-permute-start.8 = (bf16[8,32,1280]{2,1,0:T(8,128)(2,1)S(1)}, bf16[8,32,1280]{2,1,0:T(8,128)(2,1)S(1)}, u32[]{:S(2)}, u32[]{:S(2)}) collective-permute-start(bf16[8,32,1280]{2,1,0:T(8,128)(2,1)S(1)} %copy-done.40), channel_id=1, source_target_pairs={{0,24},{1,25},{2,26},{3,27},{4,28},{5,29},{6,30},{7,31},{8,16},{9,... | collective-permute-start | bytes 1966088 | tf_op jit(solution)/shard_map/ppermute | solution.py:35
  46.3 24.5 %collective-permute-start.7 = (bf16[64,3584]{1,0:T(8,128)(2,1)S(1)}, bf16[64,3584]{1,0:T(8,128)(2,1)S(1)}, u32[]{:S(2)}, u32[]{:S(2)}) collective-permute-start(bf16[64,3584]{1,0:T(8,128)(2,1)S(1)} %copy-done.27), channel_id=1, source_target_pairs={{0,8},{1,9},{2,10},{3,11},{4,12},{5,13},{6,14},{7,15},{8,16},{9,17... | collective-permute-start | bytes 1376264 | tf_op jit(solution)/shard_map/ppermute | solution.py:35
  76.1 28.8 %collective-permute-start.10 = (bf16[448,1280]{1,0:T(8,128)(2,1)}, bf16[448,1280]{1,0:T(8,128)(2,1)}, u32[]{:S(2)}, u32[]{:S(2)}) collective-permute-start(bf16[448,1280]{1,0:T(8,128)(2,1)} %collective-permute-done.5), channel_id=1, source_target_pairs={{4,6},{5,7},{12,14},{13,15},{20,22},{21,23},{28,30},{29,31}} | collective-permute-start | bytes 3440648 | tf_op jit(solution)/shard_map/ppermute | solution.py:35
  77.8 29.8 %collective-permute-start.11 = (bf16[448,1280]{1,0:T(8,128)(2,1)}, bf16[448,1280]{1,0:T(8,128)(2,1)}, u32[]{:S(2)}, u32[]{:S(2)}) collective-permute-start(bf16[448,1280]{1,0:T(8,128)(2,1)} %collective-permute-done.6), channel_id=1, source_target_pairs={{2,0},{3,1},{10,8},{11,9},{18,16},{19,17},{26,24},{27,25}} | collective-permute-start | bytes 3440648 | tf_op jit(solution)/shard_map/ppermute | solution.py:35
  84.3 20.6 %collective-permute-start.15 = (bf16[64,3584]{1,0:T(8,128)(2,1)}, bf16[64,3584]{1,0:T(8,128)(2,1)}, u32[]{:S(2)}, u32[]{:S(2)}) collective-permute-start(bf16[64,3584]{1,0:T(8,128)(2,1)} %get-tuple-element.134), channel_id=1, source_target_pairs={{8,0},{9,1},{10,2},{11,3},{12,4},{13,5},{14,6},{15,7},{16,8},{17,9... | collective-permute-start | bytes 1376264 | tf_op jit(solution)/shard_map/ppermute | solution.py:35
  88.0 19.7 %collective-permute-start.13 = (bf16[128,1280]{1,0:T(8,128)(2,1)}, bf16[128,1280]{1,0:T(8,128)(2,1)S(1)}, u32[]{:S(2)}, u32[]{:S(2)}) collective-permute-start(bf16[128,1280]{1,0:T(8,128)(2,1)} %get-tuple-element.199), channel_id=1, source_target_pairs={{0,8},{1,9},{2,10},{3,11},{4,12},{5,13},{6,14},{7,15},{8,16},{9,17... | collective-permute-start | bytes 983048 | tf_op jit(solution)/shard_map/ppermute | solution.py:35
  92.5 20.8 %collective-permute-start.14 = (bf16[128,1280]{1,0:T(8,128)(2,1)}, bf16[128,1280]{1,0:T(8,128)(2,1)S(1)}, u32[]{:S(2)}, u32[]{:S(2)}) collective-permute-start(bf16[128,1280]{1,0:T(8,128)(2,1)} %get-tuple-element.198), channel_id=1, source_target_pairs={{8,0},{9,1},{10,2},{11,3},{12,4},{13,5},{14,6},{15,7},{16,8},{17,9... | collective-permute-start | bytes 983048 | tf_op jit(solution)/shard_map/ppermute | solution.py:35
  177.7 27.5 %collective-permute-start.19 = (bf16[2,2,128,896]{3,2,1,0:T(8,128)(2,1)}, bf16[2,2,128,896]{3,2,1,0:T(8,128)(2,1)S(1)}, u32[]{:S(2)}, u32[]{:S(2)}) collective-permute-start(bf16[2,2,128,896]{3,2,1,0:T(8,128)(2,1)} %get-tuple-element.154), channel_id=1, source_target_pairs={{0,8},{1,9},{2,10},{3,11},{4,12},{5,13},{6,14},{7,15},{8,0},{9,1},... | collective-permute-start | bytes 2752520 | tf_op jit(solution)/shard_map/ppermute | solution.py:35
  180.3 25.0 %collective-permute-start.20 = (bf16[2,2,128,896]{3,2,1,0:T(8,128)(2,1)}, bf16[2,2,128,896]{3,2,1,0:T(8,128)(2,1)S(1)}, u32[]{:S(2)}, u32[]{:S(2)}) collective-permute-start(bf16[2,2,128,896]{3,2,1,0:T(8,128)(2,1)} %get-tuple-element.155), channel_id=1, source_target_pairs={{0,16},{1,17},{2,18},{3,19},{4,20},{5,21},{6,22},{7,23},{8,24},{9,... | collective-permute-start | bytes 2752520 | tf_op jit(solution)/shard_map/ppermute | solution.py:35
  180.3 24.9 %collective-permute-start.21 = (bf16[2,4,32,896]{3,2,1,0:T(8,128)(2,1)}, bf16[2,4,32,896]{3,2,1,0:T(8,128)(2,1)S(1)}, u32[]{:S(2)}, u32[]{:S(2)}) collective-permute-start(bf16[2,4,32,896]{3,2,1,0:T(8,128)(2,1)} %get-tuple-element.156), channel_id=1, source_target_pairs={{0,2},{1,3},{2,0},{3,1},{4,6},{5,7},{6,4},{7,5},{8,10},{9,11},{10,... | collective-permute-start | bytes 1376264 | tf_op jit(solution)/shard_map/ppermute | solution.py:35
  186.0 19.1 %collective-permute-start.23 = (f32[8,3584]{1,0:T(8,128)S(1)}, f32[8,3584]{1,0:T(8,128)S(1)}, u32[]{:S(2)}, u32[]{:S(2)}) collective-permute-start(f32[8,3584]{1,0:T(8,128)S(1)} %add.220.refs_6_), channel_id=1, source_target_pairs={{0,8},{1,9},{2,10},{3,11},{4,12},{5,13},{6,14},{7,15},{8,0},{9,1},... | collective-permute-start | bytes 344072 | tf_op jit(solution)/shard_map/ppermute | solution.py:35
  210.4 19.4 %collective-permute-start.24 = (bf16[2,128,896]{2,1,0:T(8,128)(2,1)}, bf16[2,128,896]{2,1,0:T(8,128)(2,1)S(1)}, u32[]{:S(2)}, u32[]{:S(2)}) collective-permute-start(bf16[2,128,896]{2,1,0:T(8,128)(2,1)} %get-tuple-element.165), channel_id=1, source_target_pairs={{0,16},{1,17},{2,18},{3,19},{4,20},{5,21},{6,22},{7,23},{8,24},{9,... | collective-permute-start | bytes 1376264 | tf_op jit(solution)/shard_map/ppermute | solution.py:35
  212.5 17.3 %collective-permute-start.25 = (bf16[2,128,896]{2,1,0:T(8,128)(2,1)}, bf16[2,128,896]{2,1,0:T(8,128)(2,1)S(1)}, u32[]{:S(2)}, u32[]{:S(2)}) collective-permute-start(bf16[2,128,896]{2,1,0:T(8,128)(2,1)} %get-tuple-element.166), channel_id=1, source_target_pairs={{0,8},{1,9},{2,10},{3,11},{4,12},{5,13},{6,14},{7,15},{8,0},{9,1},... | collective-permute-start | bytes 1376264 | tf_op jit(solution)/shard_map/ppermute | solution.py:35
  214.3 15.5 %collective-permute-start.26 = (bf16[2,2,32,896]{3,2,1,0:T(8,128)(2,1)}, bf16[2,2,32,896]{3,2,1,0:T(8,128)(2,1)S(1)}, u32[]{:S(2)}, u32[]{:S(2)}) collective-permute-start(bf16[2,2,32,896]{3,2,1,0:T(8,128)(2,1)} %get-tuple-element.167), channel_id=1, source_target_pairs={{0,4},{1,5},{2,6},{3,7},{4,0},{5,1},{6,2},{7,3},{8,12},{9,13},{10,... | collective-permute-start | bytes 688136 | tf_op jit(solution)/shard_map/ppermute | solution.py:35
  253.6 16.1 %collective-permute-start.32 = (bf16[128,896]{1,0:T(8,128)(2,1)}, bf16[128,896]{1,0:T(8,128)(2,1)S(1)}, u32[]{:S(2)}, u32[]{:S(2)}) collective-permute-start(bf16[128,896]{1,0:T(8,128)(2,1)} %get-tuple-element.186), channel_id=1, source_target_pairs={{0,4},{1,5},{2,6},{3,7},{4,0},{5,1},{6,2},{7,3},{8,12},{9,13},{10,... | collective-permute-start | bytes 688136 | tf_op jit(solution)/shard_map/ppermute | solution.py:35
  273.8 15.5 %collective-permute-start.36 = (bf16[320,448]{1,0:T(8,128)(2,1)}, bf16[320,448]{1,0:T(8,128)(2,1)S(1)}, u32[]{:S(2)}, u32[]{:S(2)}) collective-permute-start(bf16[320,448]{1,0:T(8,128)(2,1)} %shard_map.115), channel_id=1, source_target_pairs={{0,16},{1,17},{2,18},{3,19},{4,20},{5,21},{6,22},{7,23},{8,24},{9,... | collective-permute-start | bytes 860168 | tf_op jit(solution)/shard_map/ppermute | solution.py:35
  275.1 15.6 %collective-permute-start.37 = (bf16[320,448]{1,0:T(8,128)(2,1)}, bf16[320,448]{1,0:T(8,128)(2,1)S(1)}, u32[]{:S(2)}, u32[]{:S(2)}) collective-permute-start(bf16[320,448]{1,0:T(8,128)(2,1)} %shard_map.115), channel_id=1, source_target_pairs={{0,24},{1,25},{2,26},{3,27},{4,28},{5,29},{6,30},{7,31},{8,16},{9,... | collective-permute-start | bytes 860168 | tf_op jit(solution)/shard_map/ppermute | solution.py:35
  (56 other events, 494.1 us)

commit v3 on v2

--- a/solution.py
+++ b/solution.py
@@ -13,15 +13,14 @@
 F32 = jnp.float32
 LANES = 128
 AXES = ("seq", "fsdp")
-VMEM_BYTES = 60 * 1024 * 1024
 
 
 def round_up(value, unit):
     return (value + unit - 1) // unit * unit
 
 
-def kernel_params(**more):
-    return pltpu.CompilerParams(vmem_limit_bytes=VMEM_BYTES, **more)
+def kernel_params(mebibytes):
+    return pltpu.CompilerParams(vmem_limit_bytes=mebibytes * 1024 * 1024)
 
 
 def sent(value, route):
@@ -71,7 +70,7 @@
 
 
 def place_kernel(pick_ref, frames_ref, *refs):
-    inbox, out = refs[:-1], refs[-1]
+    inbox, (out, head, tail) = refs[:-3], refs[-3:]
     slots, rows, width = frames_ref.shape
     total, padded = out.shape
     tokens = slots * rows
@@ -99,6 +98,8 @@
         return carry
 
     lax.fori_loop(0, slots, one, 0)
+    head[...] = out[: head.shape[0]]
+    tail[...] = out[tokens - tail.shape[0] : tokens]
 
 
 def scalar_call(kernel, out_shape, scalars, arrays):
@@ -111,7 +112,7 @@
             out_specs=jax.tree.map(lambda _: pl.BlockSpec(memory_space=pltpu.VMEM), out_shape),
         ),
         out_shape=out_shape,
-        compiler_params=kernel_params(),
+        compiler_params=kernel_params(60),
     )(*scalars, *arrays)
 
 
@@ -181,7 +182,7 @@
     pairs = len(shard_refs) // 2
     shard = shard_refs[0].shape[0]
     core = place_ref[0]
-    for k in range(pairs):
+    for k in range(pairs)[::-1]:
         for h in range(2):
             lane = core if h == 0 else 1 - core
             row = 2 * (place_ref[1 + k] if by_chip else k) + lane
@@ -216,15 +217,11 @@
     squares[...] = total
 
 
-def early_kernel(place_ref, *refs, count, pairs):
-    row_refs, shard_refs = refs[:count], refs[count : count + 2 * pairs]
-    acc_ref, squares, weights, rows_all, sems = refs[count + 2 * pairs :]
+def early_kernel(place_ref, rows_ref, *refs, pairs):
+    shard_refs = refs[: 2 * pairs]
+    acc_ref, squares, weights, sems = refs[2 * pairs :]
     group = acc_ref.shape[2]
     load_weights(place_ref, shard_refs, weights, sems, False)
-    begin = 0
-    for ref in row_refs:
-        rows_all[begin : begin + ref.shape[0]] = ref[...]
-        begin += ref.shape[0]
     squares[...] = jnp.zeros_like(squares)
     for k in range(pairs):
         wait_weights(shard_refs[0], weights, sems, k)
@@ -232,28 +229,26 @@
         def store(begin, size, result, k=k):
             acc_ref[k, :, begin : begin + size] = result
 
-        pair_product(rows_all, weights, k * group, group, store, squares)
+        pair_product(rows_ref, weights, k * group, group, store, squares)
 
 
 VMEM_SPEC = pl.BlockSpec(memory_space=pltpu.VMEM)
 ANY_SPEC = pl.BlockSpec(memory_space=pl.ANY)
 
 
-def stem_early(row_arrays, shards, core_id):
-    padded = row_arrays[0].shape[1]
-    rows = sum(a.shape[0] for a in row_arrays)
+def stem_early(rows_in, shards, core_id):
+    rows, padded = rows_in.shape
     pairs = len(shards) // 2
     group = 2 * shards[0].shape[0]
     return pl.pallas_call(
-        functools.partial(early_kernel, count=len(row_arrays), pairs=pairs),
+        functools.partial(early_kernel, pairs=pairs),
         grid_spec=pltpu.PrefetchScalarGridSpec(
             num_scalar_prefetch=1,
             grid=(),
-            in_specs=[VMEM_SPEC] * len(row_arrays) + [ANY_SPEC] * len(shards),
+            in_specs=[VMEM_SPEC] + [ANY_SPEC] * len(shards),
             out_specs=[VMEM_SPEC] * 2,
             scratch_shapes=[
                 pltpu.VMEM((pairs * group, padded), BF16),
-                pltpu.VMEM((rows, padded), BF16),
                 pltpu.SemaphoreType.DMA((2 * pairs,)),
             ],
         ),
@@ -261,8 +256,8 @@
             jax.ShapeDtypeStruct((pairs, rows, group), F32),
             jax.ShapeDtypeStruct((rows, LANES), F32),
         ],
-        compiler_params=kernel_params(),
-    )(core_id, *row_arrays, *shards)
+        compiler_params=kernel_params(24),
+    )(core_id, rows_in, *shards)
 
 
 def gate_of(value):
@@ -280,64 +275,63 @@
     place_ref, mask_ref, main_ref, low_ref, high_ref, cot_ref, cot_low_ref, cot_high_ref, *refs,
     pairs, late, slots, channels
 ):
-    shard_refs, refs = refs[: 2 * late], refs[2 * late :]
+    shard_refs, refs = refs[: 2 * (pairs + late)], refs[2 * (pairs + late) :]
     if pairs:
-        early_main, early_halo, main_squares, halo_squares = refs[:4]
-        refs = refs[4:]
+        early_ref, early_squares, refs = refs[0], refs[1], refs[2:]
     part_ref, feat_ref, stem_ref, give_ref, keep_ref = refs[:5]
     weights, rows_all, acc, cots, feats, d_stem, lanes_of_core, gated, slopes, squares, inverse = refs[5:16]
-    sems, in_sems, cot_sems, out_sems = refs[16:]
+    sems, in_sems, cot_sems, out_sems, stem_sems = refs[16:]
     group = 2 * shard_refs[0].shape[0]
+    chips = channels // group
     tokens = cot_ref.shape[0]
     rows = tokens // slots
     halo, edge = low_ref.shape[0], cot_low_ref.shape[0]
-    extra = main_ref.shape[0] - tokens
-    body = tokens + 2 * halo
+    own_row = 2 * halo
+    body = own_row + tokens
     core = place_ref[0]
     load_weights(place_ref, shard_refs, weights, sems, not pairs)
-    loads = [
-        pltpu.make_async_copy(cot_low_ref, cots.at[pl.ds(0, edge), :], cot_sems.at[0]),
-        pltpu.make_async_copy(cot_ref, cots.at[pl.ds(edge, tokens), :], cot_sems.at[1]),
-        pltpu.make_async_copy(cot_high_ref, cots.at[pl.ds(edge + tokens, edge), :], cot_sems.at[2]),
-    ]
     if pairs:
         for k in range(pairs):
             lanes = pl.ds(pl.multiple_of(place_ref[1 + k] * group, LANES), group)
-            for i, (ref, src, dst, size) in enumerate(
-                (
-                    (early_main, 0, halo, tokens),
-                    (early_main, tokens, body, extra),
-                    (early_halo, 0, 0, halo),
-                    (early_halo, halo, halo + tokens, halo),
+            pltpu.make_async_copy(
+                early_ref.at[k],
+                acc.at[pl.ds(own_row, early_ref.shape[1]), lanes],
+                in_sems.at[place_ref[1 + k]],
+            ).start()
+    parts = 4
+    size = channels // parts
+    cot_loads = []
+    for i in range(parts):
+        lanes = pl.ds(i * size, size)
+        first = 0
+        for h, ref in enumerate((cot_low_ref, cot_ref, cot_high_ref)):
+            count = ref.shape[0]
+            cot_loads.append(
+                pltpu.make_async_copy(
+                    ref.at[:, lanes], cots.at[pl.ds(first, count), lanes], cot_sems.at[i, h]
                 )
-            ):
-                loads.append(
-                    pltpu.make_async_copy(
-                        ref.at[k, pl.ds(src, size), :],
-                        acc.at[pl.ds(dst, size), lanes],
-                        in_sems.at[k, i],
-                    )
-                )
-    for copy in loads:
+            )
+            first += count
+    for copy in cot_loads:
         copy.start()
     rows_all[0:halo] = low_ref[...]
-    rows_all[halo : halo + tokens] = main_ref[0:tokens]
-    rows_all[halo + tokens : body] = high_ref[...]
-    rows_all[body : body + extra] = main_ref[tokens:]
+    rows_all[halo:own_row] = high_ref[...]
+    rows_all[own_row:] = main_ref[...]
+    squares[...] = jnp.zeros_like(squares)
     if pairs:
-        squares[0:halo] = halo_squares[0:halo]
-        squares[halo : halo + tokens] = main_squares[0:tokens]
-        squares[halo + tokens : body] = halo_squares[halo:]
-        squares[body:] = main_squares[tokens:]
-        wait_weights(shard_refs[0], weights, sems, 0)
-
-        def store(begin, size, result):
-            first = pl.multiple_of(place_ref[1 + pairs] * group + begin, LANES)
-            acc[:, pl.ds(first, size)] = result
-
-        pair_product(rows_all, weights, 0, group, store, squares)
+        squares[own_row:] = early_squares[...]
+        for k in [pairs] + list(range(pairs)):
+            count = rows_all.shape[0] if k == pairs else own_row
+            wait_weights(shard_refs[0], weights, sems, k)
+
+            def store(begin, width, result, k=k, count=count):
+                first = pl.multiple_of(place_ref[1 + k] * group + begin, LANES)
+                acc[0:count, pl.ds(first, width)] = result
+
+            pair_product(
+                rows_all.at[0:count], weights, k * group, group, store, squares.at[0:count]
+            )
     else:
-        squares[...] = jnp.zeros_like(squares)
         for z in range(late):
             wait_weights(shard_refs[0], weights, sems, z)
         tile = 256
@@ -361,8 +355,16 @@
     mean = jnp.sum(squares[...], axis=1, keepdims=True) / channels
     inverse[...] = jnp.broadcast_to(lax.rsqrt(mean + EPSILON), inverse.shape)
     squares[...] = jnp.zeros_like(squares)
-    for copy in loads:
-        copy.wait()
+
+    def rows_of_slot(i):
+        edge_slots = halo // rows
+        if i < edge_slots:
+            first = i * rows
+        elif i < edge_slots + slots:
+            first = own_row + (i - edge_slots) * rows
+        else:
+            first = halo + (i - edge_slots - slots) * rows
+        return slice(first, first + rows)
 
     def columns(t, carry):
         lanes = pl.ds(pl.multiple_of(t * LANES, LANES), LANES)
@@ -370,7 +372,7 @@
         taps = [acc[body + 1 + k : body + 2 + k, lanes] for k in range(5)]
 
         def normed(i):
-            here = slice(i * rows, (i + 1) * rows)
+            here = rows_of_slot(i)
             return (acc[here, lanes] * inverse[here] * gain).astype(BF16).astype(F32)
 
         window = [normed(i) for i in range(4)]
@@ -386,7 +388,7 @@
             slopes[here] = slope
             if 2 <= i < slots + 2:
                 own = slice((i - 2) * rows, (i - 1) * rows)
-                stem = acc[halo + (i - 2) * rows : halo + (i - 1) * rows, lanes]
+                stem = acc[rows_of_slot(i + 2), lanes]
                 feats[own, lanes] = (stem + smooth).astype(BF16)
                 for k in range(5):
                     product = (slope * window[k]).reshape(rows // 8, 8, LANES)
@@ -399,7 +401,7 @@
         for p in range(slots):
             window = [slopes[(p + o) * rows : (p + o + 1) * rows] for o in range(5)]
             own = slice(p * rows, (p + 1) * rows)
-            here = slice(halo + p * rows, halo + (p + 1) * rows)
+            here = rows_of_slot(p + 4)
             d_normed = mixed_at(window, taps[::-1], mask_ref, 5 * (p + 2))
             product = d_normed * (acc[here, lanes] * inverse[here])
             total = total + jnp.sum(product.reshape(rows // 8, 8, LANES), axis=0)
@@ -409,9 +411,19 @@
         return carry
 
     copies = []
-    parts = 4
-    size = channels // parts
     for i in range(parts):
+        for copy in cot_loads[3 * i : 3 * i + 3]:
+            copy.wait()
+        if pairs:
+
+            @pl.when(place_ref[1 + pairs] != i)
+            def _(i=i):
+                pltpu.make_async_copy(
+                    early_ref.at[0],
+                    acc.at[pl.ds(own_row, early_ref.shape[1]), pl.ds(i * group, group)],
+                    in_sems.at[i],
+                ).wait()
+
         lax.fori_loop(i * size // LANES, (i + 1) * size // LANES, columns, 0)
         lanes = pl.ds(i * size, size)
         copy = pltpu.make_async_copy(feats.at[:, lanes], feat_ref.at[:, lanes], out_sems.at[i])
@@ -422,32 +434,45 @@
 
     def finish_columns(t, carry):
         lanes = pl.ds(pl.multiple_of(t * LANES, LANES), LANES)
-        inv = inverse[halo : halo + tokens]
-        unit = acc[halo : halo + tokens, lanes] * inv
+        inv = inverse[own_row:body]
+        unit = acc[own_row:body, lanes] * inv
         value = cots[edge : edge + tokens, lanes].astype(F32) + inv * (
             gated[:, lanes] - unit * squares[0:tokens]
         )
         d_stem[:, lanes] = value.astype(BF16)
         return carry
 
-    lax.fori_loop(0, channels // LANES, finish_columns, 0)
-    copies.append(pltpu.make_async_copy(d_stem, stem_ref, out_sems.at[parts]))
-    copies[-1].start()
     shard = group // 2
-    room = lanes_of_core.shape[2] // (channels // group)
-    for f in range(channels // shard):
-        first = f // 2 * room
-        lanes_of_core[f % 2, :, first : first + shard] = d_stem[:, f * shard : (f + 1) * shard]
-        if room > shard:
-            lanes_of_core[f % 2, :, first + shard : first + room] = jnp.zeros(
-                (tokens, room - shard), BF16
+    room = lanes_of_core.shape[2] // chips
+    steps = chips if group % LANES == 0 else 1
+    for i in range(steps):
+        lax.fori_loop(
+            i * channels // steps // LANES, (i + 1) * channels // steps // LANES, finish_columns, 0
+        )
+        lanes = pl.ds(i * (channels // steps), channels // steps)
+        copies.append(
+            pltpu.make_async_copy(d_stem.at[:, lanes], stem_ref.at[:, lanes], stem_sems.at[i, 0])
+        )
+        copies[-1].start()
+        for z in range(i * chips // steps, (i + 1) * chips // steps):
+            for h in range(2):
+                first = (2 * z + h) * shard
+                lanes_of_core[h, :, z * room : z * room + shard] = d_stem[:, first : first + shard]
+                if room > shard:
+                    lanes_of_core[h, :, z * room + shard : (z + 1) * room] = jnp.zeros(
+                        (tokens, room - shard), BF16
+                    )
+        width = chips // steps * room
+        lanes = pl.ds(i * width, width)
+        for h, ref in enumerate((keep_ref, give_ref)):
+            copies.append(
+                pltpu.make_async_copy(
+                    lanes_of_core.at[(core + h) % 2, :, lanes],
+                    ref.at[:, lanes],
+                    stem_sems.at[i, 1 + h],
+                )
             )
-    for h, ref in enumerate((keep_ref, give_ref)):
-        copy = pltpu.make_async_copy(
-            lanes_of_core.at[(core + h) % 2], ref, out_sems.at[parts + 1 + h]
-        )
-        copy.start()
-        copies.append(copy)
+            copies[-1].start()
     for copy in copies:
         copy.wait()
 
@@ -457,8 +482,8 @@
     padded = main.shape[1]
     halo, edge = low.shape[0], cot_low.shape[0]
     total = main.shape[0] + 2 * halo
-    late = len(shards) // 2
     pairs = early[0].shape[0] if early else 0
+    late = len(shards) // 2 - pairs
     shard = shards[0].shape[0]
     half = channels // (2 * shard) * round_up(shard, LANES)
     return pl.pallas_call(
@@ -469,10 +494,10 @@
             in_specs=[VMEM_SPEC] * 3
             + [ANY_SPEC] * 3
             + [ANY_SPEC] * len(shards)
-            + ([ANY_SPEC] * 2 + [VMEM_SPEC] * 2 if pairs else []),
+            + ([ANY_SPEC, VMEM_SPEC] if pairs else []),
             out_specs=[VMEM_SPEC] + [ANY_SPEC] * 4,
             scratch_shapes=[
-                pltpu.VMEM((late * 2 * shards[0].shape[0], padded), BF16),
+                pltpu.VMEM((channels, padded), BF16),
                 pltpu.VMEM((total, padded), BF16),
                 pltpu.VMEM((total, channels), F32),
                 pltpu.VMEM((tokens + 2 * edge, channels), BF16),
@@ -483,10 +508,11 @@
                 pltpu.VMEM((tokens + 2 * edge, LANES), F32),
                 pltpu.VMEM((total, LANES), F32),
                 pltpu.VMEM((total, LANES), F32),
-                pltpu.SemaphoreType.DMA((2 * late,)),
-                pltpu.SemaphoreType.DMA((max(pairs, 1), 4)),
-                pltpu.SemaphoreType.DMA((3,)),
-                pltpu.SemaphoreType.DMA((7,)),
+                pltpu.SemaphoreType.DMA((len(shards),)),
+                pltpu.SemaphoreType.DMA((len(shards) // 2,)),
+                pltpu.SemaphoreType.DMA((4, 3)),
+                pltpu.SemaphoreType.DMA((4,)),
+                pltpu.SemaphoreType.DMA((len(shards) // 2, 3)),
             ],
         ),
         out_shape=[
@@ -496,7 +522,7 @@
             jax.ShapeDtypeStruct((tokens, half), BF16),
             jax.ShapeDtypeStruct((tokens, half), BF16),
         ],
-        compiler_params=kernel_params(),
+        compiler_params=kernel_params(60),
     )(places, mask, main, low, high, cot, cot_low, cot_high, *shards, *early)
 
 
@@ -537,7 +563,7 @@
             ],
         ),
         out_shape=jax.ShapeDtypeStruct((tokens, end), BF16),
-        compiler_params=kernel_params(),
+        compiler_params=kernel_params(60),
     )(places, d_stem, *shards, *([before] if begin else []))
 
 
@@ -557,7 +583,7 @@
         in_specs=[VMEM_SPEC] * 2,
         out_specs=VMEM_SPEC,
         out_shape=jax.ShapeDtypeStruct((height, round_up(2 * tokens, LANES)), BF16),
-        compiler_params=kernel_params(),
+        compiler_params=kernel_params(16),
     )(packed, packed_other)
 
 
@@ -656,7 +682,7 @@
             ],
         ),
         out_shape=[plane, plane, line],
-        compiler_params=kernel_params(),
+        compiler_params=kernel_params(24 if give else 60),
     )(where, pixels, keep, got)
 
 
@@ -664,86 +690,112 @@
     return (index // bit) % 2
 
 
-def sums_kernel(at_ref, *refs, plan):
-    count = sum(n for alternatives, _, _ in plan for n in alternatives)
-    ins, outs = list(refs[:count]), list(refs[count:])
+def fetched(at_ref, refs, buffers, sems, indices):
+    copies = []
+    for n, (ref, buffer, index) in enumerate(zip(refs, buffers, indices)):
+        place = tuple(slice(None) if p is None else at_ref[p] for p in index)
+        source = ref.at[place] if place else ref
+        copies.append(pltpu.make_async_copy(source, buffer, sems.at[n]))
+        copies[-1].start()
+    return copies
+
+
+def total_of(copies, buffers):
+    total = None
+    for copy, buffer in zip(copies, buffers):
+        copy.wait()
+        value = buffer[...].astype(F32)
+        total = value if total is None else total + value
+    return total
+
+
+def sums_kernel(at_ref, *refs, plan, indices):
+    count = len(indices)
+    results = sum(2 if keep else 1 for _, _, keep in plan)
+    ins, outs = refs[:count], refs[count : count + results]
+    buffers = list(refs[count + results : 2 * count + results])
+    stores = list(refs[2 * count + results : 2 * count + 2 * results])
+    sems, out_sems = refs[2 * count + 2 * results :]
+    copies = fetched(at_ref, ins, buffers, sems, indices)
+    written = []
+
+    def write(value):
+        n = len(written)
+        stores[n][...] = value.astype(stores[n].dtype)
+        written.append(pltpu.make_async_copy(stores[n], outs[n], out_sems.at[n]))
+        written[-1].start()
+
     for alternatives, selector, keep in plan:
         totals = []
         for n in alternatives:
-            terms, ins = ins[:n], ins[n:]
-            total = terms[0][...].astype(F32)
-            for term in terms[1:]:
-                total = total + term[...].astype(F32)
-            totals.append(total)
-        if selector is None:
-            give = kept = totals[0]
+            totals.append(total_of(copies[:n], buffers[:n]))
+            copies, buffers = copies[n:], buffers[n:]
+        if keep:
+            upper = at_ref[selector] == 1
+            write(jnp.where(upper, totals[0], totals[1]))
+            write(jnp.where(upper, totals[1], totals[0]))
+        elif len(totals) == 1:
+            write(totals[0])
         else:
-            upper = at_ref[selector] == 1
-            give = jnp.where(upper, totals[0], totals[1])
-            kept = jnp.where(upper, totals[1], totals[0])
-        out = outs.pop(0)
-        out[...] = give.astype(out.dtype)
-        if keep:
-            outs.pop(0)[...] = kept
+            write(jnp.stack(totals, axis=0))
+    for copy in written:
+        copy.wait()
+
+
+def part_shape(array, index):
+    return tuple(array.shape[d] for d, at in enumerate(index) if at is None) + tuple(
+        array.shape[-2:]
+    )
 
 
 def sums(units):
-    scalars, arrays, in_specs, outs, plan = [], [], [], [], []
+    scalars, arrays, indices, buffers, outs, plan = [], [], [], [], [], []
 
     def scalar(value):
         scalars.append(value)
         return len(scalars) - 1
 
-    def spec(array, places):
-        lead = [None if at is not None else array.shape[d] for d, at in enumerate(places)]
-        return pl.BlockSpec(
-            tuple(lead) + tuple(array.shape[-2:]),
-            lambda i, at_ref: tuple(0 if p is None else at_ref[p] for p in places) + (0, 0),
-        )
-
     for alternatives, selector, kind in units:
         for terms in alternatives:
             for array, index in terms:
-                places = [None if at is None else scalar(at) for at in index]
+                shape = part_shape(array, index)
                 arrays.append(array)
-                in_specs.append(spec(array, places))
-                shape = tuple(
-                    array.shape[d] for d, at in enumerate(index) if at is None
-                ) + tuple(array.shape[-2:])
-        keep = len(alternatives) > 1
-        plan.append(
-            ([len(t) for t in alternatives], scalar(selector) if keep else None, keep)
-        )
-        outs.append(jax.ShapeDtypeStruct(shape, kind))
+                indices.append([None if at is None else scalar(at) for at in index])
+                buffers.append(pltpu.VMEM(shape, array.dtype))
+        keep = selector is not None
+        plan.append(([len(t) for t in alternatives], scalar(selector) if keep else None, keep))
+        stacked = () if keep or len(alternatives) == 1 else (len(alternatives),)
+        outs.append(jax.ShapeDtypeStruct(stacked + shape, kind))
         if keep:
             outs.append(jax.ShapeDtypeStruct(shape, F32))
     if not scalars:
         scalars = [jnp.int32(0)]
-
-    def whole(shape):
-        return pl.BlockSpec(shape, lambda i, at_ref: (0,) * len(shape))
-
     results = list(
         pl.pallas_call(
-            functools.partial(sums_kernel, plan=plan),
+            functools.partial(sums_kernel, plan=plan, indices=indices),
             grid_spec=pltpu.PrefetchScalarGridSpec(
                 num_scalar_prefetch=1,
-                grid=(1,),
-                in_specs=in_specs,
-                out_specs=[whole(o.shape) for o in outs],
+                grid=(),
+                in_specs=[ANY_SPEC] * len(arrays),
+                out_specs=[ANY_SPEC] * len(outs),
+                scratch_shapes=buffers
+                + [pltpu.VMEM(o.shape, o.dtype) for o in outs]
+                + [pltpu.SemaphoreType.DMA((len(arrays),)), pltpu.SemaphoreType.DMA((len(outs),))],
             ),
             out_shape=outs,
-            compiler_params=kernel_params(),
+            compiler_params=kernel_params(60),
         )(jnp.stack([jnp.asarray(s, jnp.int32) for s in scalars]), *arrays)
     )
     return [(results.pop(0), results.pop(0) if keep else None) for _, _, keep in plan]
 
 
 def at_own(terms, mine, done, label=None):
-    return [
-        (array, [1 - mine[b] if b == label else mine[b] if b in done else None for b in labels])
-        for array, labels in terms
-    ]
+    def place(b):
+        if isinstance(b, int):
+            return b
+        return 1 - mine[b] if b == label else mine[b] if b in done else None
+
+    return [(array, [place(b) for b in labels]) for array, labels in terms]
 
 
 def split_view(array, labels):
@@ -768,10 +820,14 @@
         rest = without(labels, order[:1])
         terms.append([(split_view(keep, rest), rest), (split_view(arrived, rest), rest)])
     for i in range(1, len(orders[0])):
-        units = [
-            ([at_own(t, mine, order[:i], order[i])], None, BF16) for t, order in zip(terms, orders)
-        ]
-        came = yield units, [route_of(order[i]) for order in orders]
+        parts = [at_own(t, mine, order[:i], order[i]) for t, order in zip(terms, orders)]
+        if len(orders) == 2 and orders[0][i] == orders[1][i]:
+            ((arrived, _, _),) = yield [(parts, None, BF16)], [route_of(orders[0][i])]
+            for g, (t, order) in enumerate(zip(terms, orders)):
+                rest = without(labels, order[: i + 1])
+                t.append((split_view(arrived, [g] + rest), [g] + rest))
+            continue
+        came = yield [([p], None, BF16) for p in parts], [route_of(order[i]) for order in orders]
         for t, (arrived, _, _), order in zip(terms, came, orders):
             rest = without(labels, order[: i + 1])
             t.append((split_view(arrived, rest), rest))
@@ -791,21 +847,18 @@
 
 def in_rounds(chains, beside):
     waiting = [next(chain) for chain in chains]
-    first, done = True, None
+    count, done = 0, None
     while any(routes is not None for _, routes in waiting):
         units = [u for values, routes in waiting if routes is not None for u in values]
         routes = [r for _, some in waiting if some is not None for r in some]
-        ready = [(value, None) for value in units] if first else sums(units)
-        first = False
+        ready = sums(units) if count else [(value, None) for value in units]
         came = [sent(give, route) for (give, _), route in zip(ready, routes)]
-        if beside:
-            if done is not None:
-                ready, done = together(ready, done)
-            done = beside[0](done)
-            beside = beside[1:]
+        if count in beside:
+            ready, done = beside[count](ready, done)
             came, done = together(came, done)
         else:
             (came,) = together(came)
+        count += 1
         arrived = [(value, kept, give) for value, (give, kept) in zip(came, ready)]
         for i, (values, some) in enumerate(waiting):
             if some is not None:
@@ -814,49 +867,74 @@
     return [values for values, _ in waiting], done
 
 
-def finish_kernel(at_ref, *refs, counts, scale):
-    ins, out_ref = list(refs[:-1]), refs[-1]
+def unpack_kernel(at_ref, *refs, share, line_share):
+    pieces, (out_ref, rows_all) = refs[:-2], refs[-2:]
+    width = out_ref.shape[1]
+    for o, piece in enumerate(pieces):
+        p = at_ref[0] ^ o
+        first = pl.multiple_of(p * share, 16)
+        rows_all[pl.ds(first, share), :] = piece[0:share]
+        first = pl.multiple_of(len(pieces) * share + p * line_share, 16)
+        rows_all[pl.ds(first, line_share), :] = piece[share:]
+    for first in range(0, width, LANES):
+        size = min(LANES, width - first)
+        out_ref[:, first : first + size] = rows_all[first : first + LANES].T[:, :size]
+
+
+def unpacked(pieces, seq_index, width, share, line_share):
+    height, shard = pieces[0].shape
+    return pl.pallas_call(
+        functools.partial(unpack_kernel, share=share, line_share=line_share),
+        grid_spec=pltpu.PrefetchScalarGridSpec(
+            num_scalar_prefetch=1,
+            grid=(),
+            in_specs=[VMEM_SPEC] * len(pieces),
+            out_specs=VMEM_SPEC,
+            scratch_shapes=[pltpu.VMEM((len(pieces) * height, shard), BF16)],
+        ),
+        out_shape=jax.ShapeDtypeStruct((shard, width), BF16),
+        compiler_params=kernel_params(60),
+    )(seq_index.astype(jnp.int32).reshape(1), *pieces)
+
+
+def finish_kernel(at_ref, *refs, counts, indices, scale):
+    count = len(indices)
+    ins, out_ref = refs[:count], refs[count]
+    buffers, sems = list(refs[count + 1 : -1]), refs[-1]
+    copies = fetched(at_ref, ins, buffers, sems, indices)
     shard = out_ref.shape[1]
     begin = 0
     for n in counts:
-        terms, ins = ins[:n], ins[n:]
-        total = terms[0][...].astype(F32)
-        for term in terms[1:]:
-            total = total + term[...].astype(F32)
-        total = (total * scale).astype(BF16)
+        total = (total_of(copies[:n], buffers[:n]) * scale).astype(BF16)
+        copies, buffers = copies[n:], buffers[n:]
         for part in (total[:, :shard], total[:, shard:]):
             out_ref[begin : begin + part.shape[0], :] = part
             begin += part.shape[0]
 
 
 def finish(chains, scale):
-    scalars, arrays, in_specs, height = [], [], [], 0
+    scalars, arrays, indices, buffers, height = [], [], [], [], 0
     for terms in chains:
         for array, index in terms:
-            first = len(scalars)
+            indices.append(list(range(len(scalars), len(scalars) + len(index))))
             scalars += index
             arrays.append(array)
-            in_specs.append(
-                pl.BlockSpec(
-                    (None,) * len(index) + tuple(array.shape[-2:]),
-                    lambda i, at_ref, first=first, n=len(index): tuple(
-                        at_ref[first + d] for d in range(n)
-                    )
-                    + (0, 0),
-                )
-            )
+            buffers.append(pltpu.VMEM(tuple(array.shape[-2:]), array.dtype))
         height += 2 * terms[0][0].shape[-2]
     shard = arrays[0].shape[-1] // 2
     return pl.pallas_call(
-        functools.partial(finish_kernel, counts=[len(t) for t in chains], scale=scale),
+        functools.partial(
+            finish_kernel, counts=[len(t) for t in chains], indices=indices, scale=scale
+        ),
         grid_spec=pltpu.PrefetchScalarGridSpec(
             num_scalar_prefetch=1,
-            grid=(1,),
-            in_specs=in_specs,
-            out_specs=pl.BlockSpec((height, shard), lambda i, at_ref: (0, 0)),
+            grid=(),
+            in_specs=[ANY_SPEC] * len(arrays),
+            out_specs=VMEM_SPEC,
+            scratch_shapes=buffers + [pltpu.SemaphoreType.DMA((len(arrays),))],
         ),
         out_shape=jax.ShapeDtypeStruct((height, shard), BF16),
-        compiler_params=kernel_params(),
+        compiler_params=kernel_params(60),
     )(jnp.stack([jnp.asarray(s, jnp.int32) for s in scalars]), *arrays)
 
 
@@ -881,7 +959,6 @@
     def preceding(s, f):
         return (s - 1, f) if s > 0 else None
 
-    tail, head = cot[tokens - edge :], cot[:edge]
     own = jnp.concatenate(
         [
             stem_weight,
@@ -891,7 +968,8 @@
         ],
         axis=1,
     )
-    own, tail, patches = together(own, tail, patches)
+    own, cot, patches = together(own, cot, patches)
+    tail, head = cot[tokens - edge :], cot[:edge]
     frames = patches[0].reshape(slots, rows, width)
     boxes = outgoing(frames, send_slot[0], seq_index, seq_size, padded)
     rising, falling = {0: own}, {0: own}
@@ -909,7 +987,7 @@
         for o, box in zip(numbers, boxes):
             inbox[o - 1], spots[o - 1] = box, box[:, 0, width]
 
-    def add_shard(k):
+    def add_shard(k, rising, falling):
         options, which, origin = chain_slot(rising, falling, k, chip, chips)
         lane_shards.append(chosen(options, which))
         core_shards.append(swapped(lane_shards[-1], 0, 1))
@@ -927,44 +1005,47 @@
             came = [swapped(boxes[o - 1], o, 0) for o in others]
             cot_low = sent(tail, following)
             if split:
-                add_shard(1)
+                rising[1], falling[1], spots = together(rising[1], falling[1], spots)
+                add_shard(1, rising, falling)
             rising, falling, cot_low, came, core_shards, lane_shards, spots, head = together(
                 rising, falling, cot_low, came, core_shards, lane_shards, spots, head
             )
             arrive(others, came)
             cot_high = sent(head, preceding)
             pick = arrivals(send_slot[0], jnp.stack(spots, axis=0), seq_index)
-            main = scalar_call(
+            main, main_head, main_tail = scalar_call(
                 place_kernel,
-                jax.ShapeDtypeStruct((tokens + 16, padded), BF16),
+                [
+                    jax.ShapeDtypeStruct((count, padded), BF16)
+                    for count in (tokens + 16, 2 * edge, 2 * edge)
+                ],
                 [pick],
                 [frames] + inbox,
             )
             if split:
-                add_shard(2)
-                main, lane_shards, core_shards = together(main, lane_shards, core_shards)
-            low = sent(main[tokens - 2 * edge : tokens], following)
-            high = sent(main[: 2 * edge], preceding)
+                add_shard(2, rising, falling)
+                main, main_head, main_tail, lane_shards, core_shards = together(
+                    main, main_head, main_tail, lane_shards, core_shards
+                )
+            low = sent(main_tail, following)
+            high = sent(main_head, preceding)
         elif k == 3 and split:
             pairs = [v for both in zip(lane_shards, core_shards) for v in both]
-            early_main, main_squares = stem_early([main], pairs, core_id)
-            rising, falling, early_main, low, high, cot_high, main = together(
-                rising, falling, early_main, low, high, cot_high, main
+            early_main, main_squares = stem_early(main, pairs, core_id)
+            rising, falling, early_main, low, high, main, cot_high = together(
+                rising, falling, early_main, low, high, main, cot_high
             )
         else:
             rising, falling = together(rising, falling)
     for k in range(len(lane_shards), chips):
-        add_shard(k)
+        add_shard(k, rising, falling)
     height = round_up(width, 64 * seq_size)
     main_other = swapped(main, 0, 1)
     places = jnp.stack([core] + chip_of).astype(jnp.int32)
     all_pairs = [v for both in zip(lane_shards, core_shards) for v in both]
-    late_pairs = all_pairs
     if split:
-        late_pairs = all_pairs[len(pairs) :]
-        early_halo, halo_squares = stem_early([low, high], pairs, core_id)
-        early_halo, main_other = together(early_halo, main_other)
-        early = [early_main, early_halo, main_squares, halo_squares]
+        all_pairs, main_other = together(all_pairs, main_other)
+        early = [early_main, main_squares]
 
     ids = segments[0]
     total_slots = ids.shape[0]
@@ -976,7 +1057,7 @@
     )
     mask = (inside & same).astype(F32).reshape(-1)
     chan_part, features, d_stem, give, keep = layer(
-        main, low, high, cot, cot_low, cot_high, late_pairs, early, places, mask, slots, channels
+        main, low, high, cot, cot_low, cot_high, all_pairs, early, places, mask, slots, channels
     )
     chan_part = chan_part + swapped(chan_part, 0, 1)
     got = swapped(give, 0, 1)
@@ -1016,19 +1097,19 @@
         ),
         all_sum(chan_part, [route_of(label) for label in seq_labels + chip_labels]),
     ]
-    (plane, line, chan), grad_rows = in_rounds(
-        chains,
-        [
-            lambda _: pixel_grads(d_stem, all_pairs, places, 0, middle),
-            lambda before: pixel_grads(d_stem, all_pairs, places, middle, width, before),
-        ],
-    )
+    last_round = len(seq_bits) + len(chip_bits) - 1
+
+    def left_pixels(ready, _):
+        inputs, ready = together(d_stem, ready)
+        return ready, pixel_grads(inputs, all_pairs, places, 0, middle)
+
+    (plane, line, chan), grad_rows = in_rounds(chains, {last_round: left_pixels})
     rows_mine = finish([plane, line], scale)
+    d_stem, rows_mine = together(d_stem, rows_mine)
     pieces = [rows_mine] + [swapped(rows_mine, o, 0) for o in range(1, seq_size)]
-    stack = by_position(pieces, seq_index)
-    grad_weight = jnp.concatenate(
-        [stack[:, :share].reshape(-1, shard), stack[:, share:].reshape(-1, shard)], axis=0
-    )[:width].T
+    grad_rows = pixel_grads(d_stem, all_pairs, places, middle, width, grad_rows)
+    pieces, grad_rows = together(pieces, grad_rows)
+    grad_weight = unpacked(pieces, seq_index, width, share, line_share)
     first = fsdp_index * shard
     grad_channels = scale * (
         lax.dynamic_slice_in_dim(chan[0], first, shard, axis=1)[:6]

time: 298 us -> 279 us (0.936)
  Pallas kernels: 116 us -> 104 us
  waiting for transfers between devices: 87.2 us -> 78.6 us
  other arithmetic: 10.9 us -> 7.18 us
  starting transfers between devices: 54.6 us -> 58 us
    ppermute x38 -> x37, waiting for transfers between devices: 87.2 us -> 78.6 us  [sent(): return lax.ppermute(value, AXES, pairs)]
    pallas_call x5, Pallas kernels: 28.8 us -> 20.4 us  [the longest x3 10.1 us: sums(): pl.pallas_call(functools.partial(sums_kernel, plan=plan, indices=indices)...]
    unnamed x83 -> x89, local copies, waits for them, and re-layouts: 10.6 us -> 15.3 us
    ppermute x38 -> x37, starting transfers between devices: 54.6 us -> 58 us  [sent(): return lax.ppermute(value, AXES, pairs)]
  transfers between devices with their start and end apart: 38 -> 37, of which waited for: 14 -> 16; matrix products, arithmetic and copies ran while one was open for 6% -> 5% of each run, Pallas kernels for 19% -> 16%
where the time goes in v3:
time: 279 us; the launch traced here: 278 us
  Pallas kernels  104 us (37%)
  waiting for transfers between devices  78.6 us (28%)
  starting transfers between devices  58 us (21%)
  local copies, waits for them, and re-layouts  28.3 us (10%)
  other arithmetic  7.18 us (3%)
    ppermute x37, waiting for transfers between devices, sent(): return lax.ppermute(value, AXES, pairs)  78.6 us
    ppermute x37, starting transfers between devices, sent(): return lax.ppermute(value, AXES, pairs)  58 us
    pallas_call x1, Pallas kernels, layer(): pl.pallas_call(functools.partial(layer_kernel, pairs=pairs, late=late, sl...  35.6 us
    pallas_call x2, Pallas kernels, pixel_grads(): pl.pallas_call(functools.partial(pixel_kernel, chips=chips, begin=begin,...  18.8 us
    pallas_call x2, Pallas kernels, weight_part(): pl.pallas_call(functools.partial(weight_kernel, bits=bits, share=share, l...  16.5 us
    unnamed x89, local copies, waits for them, and re-layouts  15.3 us
    pallas_call x3, Pallas kernels, sums(): pl.pallas_call(functools.partial(sums_kernel, plan=plan, indices=indices)...  10.1 us
    pallas_call x2, Pallas kernels, scalar_call(): pl.pallas_call(kernel, grid_spec=pltpu.PrefetchScalarGridSpec(num_scalar_...  7.93 us
  transfers between devices with their start and end apart: 37, of which 16 were waited for; matrix products, arithmetic and copies ran while one was open for 5% of the time, Pallas kernels for 16%

profile of v3, /device:TPU:0, one launch (start us, length us, event | category | flops | bytes accessed | tf_op | source)
XLA Modules:
  0.0 277.7 jit_solution(4581615382549983657)
XLA Ops:
  5.3 4.6 %collective-permute-start = (bf16[448,1280]{1,0:T(8,128)(2,1)S(1)}, bf16[448,1280]{1,0:T(8,128)(2,1)S(1)}, u32[]{:S(2)}, u32[]{:S(2)}) collective-permute-start(bf16[448,1280]{1,0:T(8,128)(2,1)S(1)} %concatenate.3.refs_0_), channel_id=1, source_target_pairs={{0,2},{1,3},{2,4},{3,5},{4,6},{5,7},{8,10},{9,11},{10,12},{11,13},... | collective-permute-start | bytes 3440648 | tf_op jit(solution)/shard_map/ppermute | solution.py:34
  12.9 3.4 %shard_map.102 = (bf16[8,32,1280]{2,1,0:T(8,128)(2,1)}, bf16[8,32,1280]{2,1,0:T(8,128)(2,1)}, bf16[8,32,1280]{2,1,0:T(8,128)(2,1)}) custom-call(s32[24]{0:T(128)} %reshape.240.order_ref, f32[24]{0:T(128)} %convert_element_type.27.spot_ref, bf16[17,32,1176]{2,1,0:T(8,128)(2,1)} %bitcast.46), custom_call_target="tpu_custom_call" | custom-call | tf_op jit(solution)/shard_map/pallas_call | solution.py:106
  21.3 13.6 %collective-permute-done = bf16[448,1280]{1,0:T(8,128)(2,1)S(1)} collective-permute-done((bf16[448,1280]{1,0:T(8,128)(2,1)S(1)}, bf16[448,1280]{1,0:T(8,128)(2,1)S(1)}, u32[]{:S(2)}, u32[]{:S(2)}) %collective-permute-start) | collective-permute-done | bytes 1146912 | tf_op jit(solution)/shard_map/ppermute | solution.py:34
  34.9 4.3 %collective-permute-done.1 = bf16[448,1280]{1,0:T(8,128)(2,1)} collective-permute-done((bf16[448,1280]{1,0:T(8,128)(2,1)S(1)}, bf16[448,1280]{1,0:T(8,128)(2,1)}, u32[]{:S(2)}, u32[]{:S(2)}) %collective-permute-start.1) | collective-permute-done | bytes 1146912 | tf_op jit(solution)/shard_map/ppermute | solution.py:34
  50.0 22.0 %collective-permute-done.7.cot_low_ref = bf16[64,3584]{1,0:T(8,128)(2,1)S(1)} collective-permute-done((bf16[64,3584]{1,0:T(8,128)(2,1)S(1)}, bf16[64,3584]{1,0:T(8,128)(2,1)S(1)}, u32[]{:S(2)}, u32[]{:S(2)}) %collective-permute-start.7) | collective-permute-done | bytes 458784 | tf_op jit(solution)/shard_map/ppermute | solution.py:34
  81.3 4.5 %shard_map.103 = (bf16[560,1280]{1,0:T(8,128)(2,1)}, bf16[128,1280]{1,0:T(8,128)(2,1)}, bf16[128,1280]{1,0:T(8,128)(2,1)}) custom-call(s32[17]{0:T(128)} %add.215.pick_ref, bf16[17,32,1176]{2,1,0:T(8,128)(2,1)} %bitcast.47, bf16[8,32,1280]{2,1,0:T(8,128)(2,1)} %copy-done.27, bf16[8,32,1280]{2,1,0:T(8,128)(2,1)} %copy-done.28, bf16[8,32,1280]{2,1,0:T(8,128)(2,1)} %copy-done.29), custom_call_target="tpu_custom_call" | custom-call | tf_op jit(solution)/shard_map/pallas_call | solution.py:106
  85.8 5.3 %collective-permute-start.13 = (bf16[128,1280]{1,0:T(8,128)(2,1)}, bf16[128,1280]{1,0:T(8,128)(2,1)}, u32[]{:S(2)}, u32[]{:S(2)}) collective-permute-start(bf16[128,1280]{1,0:T(8,128)(2,1)} %get-tuple-element.160), channel_id=1, source_target_pairs={{0,8},{1,9},{2,10},{3,11},{4,12},{5,13},{6,14},{7,15},{8,16},{9,17... | collective-permute-start | bytes 983048 | tf_op jit(solution)/shard_map/ppermute | solution.py:34
  95.1 7.6 %shard_map.104 = (f32[3,560,896]{2,1,0:T(8,128)S(1)}, f32[560,128]{1,0:T(8,128)S(1)}) custom-call(s32[1]{0:T(128)} %bitcast.place_ref, bf16[560,1280]{1,0:T(8,128)(2,1)} %get-tuple-element.163.rows_ref.main_ref.first_ref, bf16[448,1280]{1,0:T(8,128)(2,1)S(1)} %concatenate.3.refs_0_, bf16[448,1280]{1,0:T(8,128)(2,1)S(1)} %copy-done.7, ...), custom_call_target="tpu_custom_call" | custom-call | tf_op jit(solution)/shard_map/pallas_call | solution.py:243
  113.9 35.6 %shard_map.105 = (f32[8,3584]{1,0:T(8,128)}, bf16[544,3584]{1,0:T(8,128)(2,1)}, bf16[544,3584]{1,0:T(8,128)(2,1)}, bf16[544,2048]{1,0:T(8,128)(2,1)}, bf16[544,2048]{1,0:T(8,128)(2,1)}) custom-call(s32[5]{0:T(128)} %stack.51.place_ref, f32[105]{0:T(128)} %reshape.245.mask_ref, bf16[560,1280]{1,0:T(8,128)(2,1)} %get-tuple-element.163.rows_ref.main_ref.first_ref, ...), custom_call_target="tpu_custom_call" | custom-call | tf_op jit(solution)/shard_map/pallas_call | solution.py:489
  154.1 7.5 %shard_map.108 = (bf16[2,2,128,896]{3,2,1,0:T(8,128)(2,1)}, bf16[2,2,128,896]{3,2,1,0:T(8,128)(2,1)}, bf16[2,4,32,896]{3,2,1,0:T(8,128)(2,1)S(1)}) custom-call(s32[2]{0:T(128)S(1)} %pad_add_fusion.where_ref, bf16[1280,1152]{1,0:T(8,128)(2,1)S(1)} %shard_map.106.pixels_ref, bf16[544,2048]{1,0:T(8,128)(2,1)S(1)} %copy-done.10, ...), custom_call_target="tpu_custom_call" | custom-call | tf_op jit(solution)/shard_map/pallas_call | solution.py:667
  164.2 3.9 %collective-permute-start.21 = (bf16[2,4,32,896]{3,2,1,0:T(8,128)(2,1)S(1)}, bf16[2,4,32,896]{3,2,1,0:T(8,128)(2,1)S(1)}, u32[]{:S(2)}, u32[]{:S(2)}) collective-permute-start(bf16[2,4,32,896]{3,2,1,0:T(8,128)(2,1)S(1)} %get-tuple-element.190), channel_id=1, source_target_pairs={{0,2},{1,3},{2,0},{3,1},{4,6},{5,7},{6,4},{7,5},{8,10},{9,11},{10,... | collective-permute-start | bytes 1376264 | tf_op jit(solution)/shard_map/ppermute | solution.py:34
  170.8 9.0 %shard_map.107 = (f32[2,2,128,896]{3,2,1,0:T(8,128)}, f32[2,2,128,896]{3,2,1,0:T(8,128)}, f32[2,4,32,896]{3,2,1,0:T(8,128)}) custom-call(s32[2]{0:T(128)} %copy-done.16, bf16[1280,1152]{1,0:T(8,128)(2,1)} %copy-done.5, bf16[544,2048]{1,0:T(8,128)(2,1)} %get-tuple-element.185.keep_ref, bf16[544,2048]{1,0:T(8,128)(2,1)} %copy-done.11), custom_call_target="tpu_custom_call" | custom-call | tf_op jit(solution)/shard_map/pallas_call | solution.py:667
  179.8 7.7 %collective-permute-done.23.refs_7_ = f32[8,3584]{1,0:T(8,128)S(1)} collective-permute-done((f32[8,3584]{1,0:T(8,128)S(1)}, f32[8,3584]{1,0:T(8,128)S(1)}, u32[]{:S(2)}, u32[]{:S(2)}) %collective-permute-start.23) | collective-permute-done | bytes 114720 | tf_op jit(solution)/shard_map/ppermute | solution.py:34
  188.9 3.5 %shard_map.109 = (bf16[2,128,896]{2,1,0:T(8,128)(2,1)}, bf16[2,128,896]{2,1,0:T(8,128)(2,1)}, bf16[2,2,32,896]{3,2,1,0:T(8,128)(2,1)}, f32[8,3584]{1,0:T(8,128)}) custom-call(s32[6]{0:T(128)} %stack.132.at_ref, f32[2,2,128,896]{3,2,1,0:T(8,128)} %get-tuple-element.187.refs_0_, bf16[2,2,128,896]{3,2,1,0:T(8,128)(2,1)} %copy-done.18, ...), custom_call_target="tpu_custom_call" | custom-call | tf_op jit(solution)/shard_map/pallas_call | solution.py:774
  194.3 6.5 %collective-permute-start.26 = (bf16[2,2,32,896]{3,2,1,0:T(8,128)(2,1)}, bf16[2,2,32,896]{3,2,1,0:T(8,128)(2,1)S(1)}, u32[]{:S(2)}, u32[]{:S(2)}) collective-permute-start(bf16[2,2,32,896]{3,2,1,0:T(8,128)(2,1)} %get-tuple-element.200), channel_id=1, source_target_pairs={{0,4},{1,5},{2,6},{3,7},{4,0},{5,1},{6,2},{7,3},{8,12},{9,13},{10,... | collective-permute-start | bytes 688136 | tf_op jit(solution)/shard_map/ppermute | solution.py:34
  203.4 3.7 %collective-permute-done.27.refs_10_ = f32[8,3584]{1,0:T(8,128)S(1)} collective-permute-done((f32[8,3584]{1,0:T(8,128)}, f32[8,3584]{1,0:T(8,128)S(1)}, u32[]{:S(2)}, u32[]{:S(2)}) %collective-permute-start.27) | collective-permute-done | bytes 114720 | tf_op jit(solution)/shard_map/ppermute | solution.py:34
  207.2 3.1 %collective-permute-done.26.refs_8_.refs_10_.refs_4_ = bf16[2,2,32,896]{3,2,1,0:T(8,128)(2,1)S(1)} collective-permute-done((bf16[2,2,32,896]{3,2,1,0:T(8,128)(2,1)}, bf16[2,2,32,896]{3,2,1,0:T(8,128)(2,1)S(1)}, u32[]{:S(2)}, u32[]{:S(2)}) %collective-permute-start.26) | collective-permute-done | bytes 229408 | tf_op jit(solution)/shard_map/ppermute | solution.py:34
  211.9 3.2 %shard_map.110 = (bf16[2,128,896]{2,1,0:T(8,128)(2,1)}, bf16[2,32,896]{2,1,0:T(8,128)(2,1)}, f32[8,3584]{1,0:T(8,128)}) custom-call(s32[15]{0:T(128)} %stack.134.at_ref, f32[2,2,128,896]{3,2,1,0:T(8,128)} %get-tuple-element.187.refs_0_, bf16[2,2,128,896]{3,2,1,0:T(8,128)(2,1)} %copy-done.18, bf16[2,128,896]{2,1,0:T(8,128)(2,1)} %copy-done.24, ...), custom_call_target="tpu_custom_call" | custom-call | tf_op jit(solution)/shard_map/pallas_call | solution.py:774
  221.1 9.2 %collective-permute-done.30.refs_13_ = f32[8,3584]{1,0:T(8,128)S(1)} collective-permute-done((f32[8,3584]{1,0:T(8,128)}, f32[8,3584]{1,0:T(8,128)S(1)}, u32[]{:S(2)}, u32[]{:S(2)}) %collective-permute-start.30) | collective-permute-done | bytes 114720 | tf_op jit(solution)/shard_map/ppermute | solution.py:34
  231.7 3.4 %shard_map.111 = (bf16[128,896]{1,0:T(8,128)(2,1)}, f32[128,896]{1,0:T(8,128)}, bf16[32,896]{1,0:T(8,128)(2,1)}, f32[8,3584]{1,0:T(8,128)}) custom-call(s32[22]{0:T(128)} %stack.61.at_ref, f32[2,2,128,896]{3,2,1,0:T(8,128)} %get-tuple-element.187.refs_0_, bf16[2,2,128,896]{3,2,1,0:T(8,128)(2,1)} %copy-done.18, bf16[2,128,896]{2,1,0:T(8,128)(2,1)} %copy-done.24, ...), custom_call_target="tpu_custom_call" | custom-call | tf_op jit(solution)/shard_map/pallas_call | solution.py:774
  240.4 9.2 %shard_map.112.refs_8_ = bf16[544,640]{1,0:T(8,128)(2,1)} custom-call(s32[5]{0:T(128)} %stack.51.place_ref, bf16[544,3584]{1,0:T(8,128)(2,1)} %get-tuple-element.221.d_stem_ref, bf16[448,1280]{1,0:T(8,128)(2,1)} %copy-done.2, bf16[448,1280]{1,0:T(8,128)(2,1)} %copy-done.6, bf16[448,1280]{1,0:T(8,128)(2,1)} %copy-done.3, bf16[448,1280]{1,0:T(8,128)(2,1)} %copy-done.8, ...), custom_call_target="tpu_custom_call" | custom-call | tf_op jit(solution)/shard_map/pallas_call | solution.py:551
  252.6 2.8 shard_map.113.refs_0_
  259.5 9.6 %shard_map.114 = bf16[544,1176]{1,0:T(8,128)(2,1)} custom-call(s32[5]{0:T(128)} %stack.51.place_ref, bf16[544,3584]{1,0:T(8,128)(2,1)} %get-tuple-element.221.d_stem_ref, bf16[448,1280]{1,0:T(8,128)(2,1)} %copy-done.2, bf16[448,1280]{1,0:T(8,128)(2,1)} %copy-done.6, bf16[448,1280]{1,0:T(8,128)(2,1)} %copy-done.3, bf16[448,1280]{1,0:T(8,128)(2,1)} %copy-done.8, ...), custom_call_target="tpu_custom_call" | custom-call | tf_op jit(solution)/shard_map/pallas_call | solution.py:551
  275.0 2.7 shard_map.115
  (199 shorter events, 90.6 us)
Async XLA Ops:
  5.3 29.7 %collective-permute-start = (bf16[448,1280]{1,0:T(8,128)(2,1)S(1)}, bf16[448,1280]{1,0:T(8,128)(2,1)S(1)}, u32[]{:S(2)}, u32[]{:S(2)}) collective-permute-start(bf16[448,1280]{1,0:T(8,128)(2,1)S(1)} %concatenate.3.refs_0_), channel_id=1, source_target_pairs={{0,2},{1,3},{2,4},{3,5},{4,6},{5,7},{8,10},{9,11},{10,12},{11,13},... | collective-permute-start | bytes 3440648 | tf_op jit(solution)/shard_map/ppermute | solution.py:34
  9.8 29.4 %collective-permute-start.1 = (bf16[448,1280]{1,0:T(8,128)(2,1)S(1)}, bf16[448,1280]{1,0:T(8,128)(2,1)}, u32[]{:S(2)}, u32[]{:S(2)}) collective-permute-start(bf16[448,1280]{1,0:T(8,128)(2,1)S(1)} %concatenate.3.refs_0_), channel_id=1, source_target_pairs={{2,0},{3,1},{4,2},{5,3},{6,4},{7,5},{10,8},{11,9},{12,10},{13,11},... | collective-permute-start | bytes 3440648 | tf_op jit(solution)/shard_map/ppermute | solution.py:34
  16.3 22.9 %collective-permute-start.3 = (bf16[8,32,1280]{2,1,0:T(8,128)(2,1)}, bf16[8,32,1280]{2,1,0:T(8,128)(2,1)S(1)}, u32[]{:S(2)}, u32[]{:S(2)}) collective-permute-start(bf16[8,32,1280]{2,1,0:T(8,128)(2,1)} %get-tuple-element.122), channel_id=1, source_target_pairs={{0,8},{1,9},{2,10},{3,11},{4,12},{5,13},{6,14},{7,15},{8,0},{9,1},... | collective-permute-start | bytes 1966088 | tf_op jit(solution)/shard_map/ppermute | solution.py:34
  17.8 21.4 %collective-permute-start.4 = (bf16[8,32,1280]{2,1,0:T(8,128)(2,1)}, bf16[8,32,1280]{2,1,0:T(8,128)(2,1)S(1)}, u32[]{:S(2)}, u32[]{:S(2)}) collective-permute-start(bf16[8,32,1280]{2,1,0:T(8,128)(2,1)} %get-tuple-element.123), channel_id=1, source_target_pairs={{0,16},{1,17},{2,18},{3,19},{4,20},{5,21},{6,22},{7,23},{8,24},{9,... | collective-permute-start | bytes 1966088 | tf_op jit(solution)/shard_map/ppermute | solution.py:34
  42.0 30.1 %collective-permute-start.9 = (bf16[448,1280]{1,0:T(8,128)(2,1)S(1)}, bf16[448,1280]{1,0:T(8,128)(2,1)S(1)}, u32[]{:S(2)}, u32[]{:S(2)}) collective-permute-start(bf16[448,1280]{1,0:T(8,128)(2,1)S(1)} %broadcast_select_fusion.1.refs_2_), channel_id=1, source_target_pairs={{0,1},{1,0},{2,3},{3,2},{4,5},{5,4},{6,7},{7,6},{8,9},{9,8},{10,11... | collective-permute-start | bytes 3440648 | tf_op jit(solution)/shard_map/ppermute | solution.py:34
  42.1 31.0 %collective-permute-start.5 = (bf16[448,1280]{1,0:T(8,128)(2,1)S(1)}, bf16[448,1280]{1,0:T(8,128)(2,1)}, u32[]{:S(2)}, u32[]{:S(2)}) collective-permute-start(bf16[448,1280]{1,0:T(8,128)(2,1)S(1)} %collective-permute-done), channel_id=1, source_target_pairs={{2,4},{3,5},{4,6},{5,7},{10,12},{11,13},{12,14},{13,15},{18,20},{1... | collective-permute-start | bytes 3440648 | tf_op jit(solution)/shard_map/ppermute | solution.py:34
  43.8 30.8 %collective-permute-start.6 = (bf16[448,1280]{1,0:T(8,128)(2,1)}, bf16[448,1280]{1,0:T(8,128)(2,1)}, u32[]{:S(2)}, u32[]{:S(2)}) collective-permute-start(bf16[448,1280]{1,0:T(8,128)(2,1)} %collective-permute-done.1), channel_id=1, source_target_pairs={{2,0},{3,1},{4,2},{5,3},{10,8},{11,9},{12,10},{13,11},{18,16},{19,... | collective-permute-start | bytes 3440648 | tf_op jit(solution)/shard_map/ppermute | solution.py:34
  45.0 27.0 %collective-permute-start.8 = (bf16[8,32,1280]{2,1,0:T(8,128)(2,1)S(1)}, bf16[8,32,1280]{2,1,0:T(8,128)(2,1)S(1)}, u32[]{:S(2)}, u32[]{:S(2)}) collective-permute-start(bf16[8,32,1280]{2,1,0:T(8,128)(2,1)S(1)} %copy-done.43), channel_id=1, source_target_pairs={{0,24},{1,25},{2,26},{3,27},{4,28},{5,29},{6,30},{7,31},{8,16},{9,... | collective-permute-start | bytes 1966088 | tf_op jit(solution)/shard_map/ppermute | solution.py:34
  47.6 24.5 %collective-permute-start.7 = (bf16[64,3584]{1,0:T(8,128)(2,1)S(1)}, bf16[64,3584]{1,0:T(8,128)(2,1)S(1)}, u32[]{:S(2)}, u32[]{:S(2)}) collective-permute-start(bf16[64,3584]{1,0:T(8,128)(2,1)S(1)} %get-tuple-element.132), channel_id=1, source_target_pairs={{0,8},{1,9},{2,10},{3,11},{4,12},{5,13},{6,14},{7,15},{8,16},{9,17... | collective-permute-start | bytes 1376264 | tf_op jit(solution)/shard_map/ppermute | solution.py:34
  76.1 29.3 %collective-permute-start.10 = (bf16[448,1280]{1,0:T(8,128)(2,1)}, bf16[448,1280]{1,0:T(8,128)(2,1)}, u32[]{:S(2)}, u32[]{:S(2)}) collective-permute-start(bf16[448,1280]{1,0:T(8,128)(2,1)} %collective-permute-done.5), channel_id=1, source_target_pairs={{4,6},{5,7},{12,14},{13,15},{20,22},{21,23},{28,30},{29,31}} | collective-permute-start | bytes 3440648 | tf_op jit(solution)/shard_map/ppermute | solution.py:34
  77.7 29.9 %collective-permute-start.11 = (bf16[448,1280]{1,0:T(8,128)(2,1)}, bf16[448,1280]{1,0:T(8,128)(2,1)}, u32[]{:S(2)}, u32[]{:S(2)}) collective-permute-start(bf16[448,1280]{1,0:T(8,128)(2,1)} %collective-permute-done.6), channel_id=1, source_target_pairs={{2,0},{3,1},{10,8},{11,9},{18,16},{19,17},{26,24},{27,25}} | collective-permute-start | bytes 3440648 | tf_op jit(solution)/shard_map/ppermute | solution.py:34
  79.0 26.3 %collective-permute-start.15 = (bf16[64,3584]{1,0:T(8,128)(2,1)}, bf16[64,3584]{1,0:T(8,128)(2,1)}, u32[]{:S(2)}, u32[]{:S(2)}) collective-permute-start(bf16[64,3584]{1,0:T(8,128)(2,1)} %get-tuple-element.162), channel_id=1, source_target_pairs={{8,0},{9,1},{10,2},{11,3},{12,4},{13,5},{14,6},{15,7},{16,8},{17,9... | collective-permute-start | bytes 1376264 | tf_op jit(solution)/shard_map/ppermute | solution.py:34
  85.8 21.8 %collective-permute-start.13 = (bf16[128,1280]{1,0:T(8,128)(2,1)}, bf16[128,1280]{1,0:T(8,128)(2,1)}, u32[]{:S(2)}, u32[]{:S(2)}) collective-permute-start(bf16[128,1280]{1,0:T(8,128)(2,1)} %get-tuple-element.160), channel_id=1, source_target_pairs={{0,8},{1,9},{2,10},{3,11},{4,12},{5,13},{6,14},{7,15},{8,16},{9,17... | collective-permute-start | bytes 983048 | tf_op jit(solution)/shard_map/ppermute | solution.py:34
  91.1 17.1 %collective-permute-start.14 = (bf16[128,1280]{1,0:T(8,128)(2,1)}, bf16[128,1280]{1,0:T(8,128)(2,1)}, u32[]{:S(2)}, u32[]{:S(2)}) collective-permute-start(bf16[128,1280]{1,0:T(8,128)(2,1)} %get-tuple-element.161), channel_id=1, source_target_pairs={{8,0},{9,1},{10,2},{11,3},{12,4},{13,5},{14,6},{15,7},{16,8},{17,9... | collective-permute-start | bytes 983048 | tf_op jit(solution)/shard_map/ppermute | solution.py:34
  161.7 25.8 %collective-permute-start.19 = (bf16[2,2,128,896]{3,2,1,0:T(8,128)(2,1)}, bf16[2,2,128,896]{3,2,1,0:T(8,128)(2,1)S(1)}, u32[]{:S(2)}, u32[]{:S(2)}) collective-permute-start(bf16[2,2,128,896]{3,2,1,0:T(8,128)(2,1)} %get-tuple-element.188), channel_id=1, source_target_pairs={{0,8},{1,9},{2,10},{3,11},{4,12},{5,13},{6,14},{7,15},{8,0},{9,1},... | collective-permute-start | bytes 2752520 | tf_op jit(solution)/shard_map/ppermute | solution.py:34
  164.2 23.3 %collective-permute-start.20 = (bf16[2,2,128,896]{3,2,1,0:T(8,128)(2,1)}, bf16[2,2,128,896]{3,2,1,0:T(8,128)(2,1)S(1)}, u32[]{:S(2)}, u32[]{:S(2)}) collective-permute-start(bf16[2,2,128,896]{3,2,1,0:T(8,128)(2,1)} %get-tuple-element.189), channel_id=1, source_target_pairs={{0,16},{1,17},{2,18},{3,19},{4,20},{5,21},{6,22},{7,23},{8,24},{9,... | collective-permute-start | bytes 2752520 | tf_op jit(solution)/shard_map/ppermute | solution.py:34
  164.2 23.3 %collective-permute-start.21 = (bf16[2,4,32,896]{3,2,1,0:T(8,128)(2,1)S(1)}, bf16[2,4,32,896]{3,2,1,0:T(8,128)(2,1)S(1)}, u32[]{:S(2)}, u32[]{:S(2)}) collective-permute-start(bf16[2,4,32,896]{3,2,1,0:T(8,128)(2,1)S(1)} %get-tuple-element.190), channel_id=1, source_target_pairs={{0,2},{1,3},{2,0},{3,1},{4,6},{5,7},{6,4},{7,5},{8,10},{9,11},{10,... | collective-permute-start | bytes 1376264 | tf_op jit(solution)/shard_map/ppermute | solution.py:34
  169.5 18.0 %collective-permute-start.23 = (f32[8,3584]{1,0:T(8,128)S(1)}, f32[8,3584]{1,0:T(8,128)S(1)}, u32[]{:S(2)}, u32[]{:S(2)}) collective-permute-start(f32[8,3584]{1,0:T(8,128)S(1)} %add.221.refs_6_), channel_id=1, source_target_pairs={{0,8},{1,9},{2,10},{3,11},{4,12},{5,13},{6,14},{7,15},{8,0},{9,1},... | collective-permute-start | bytes 344072 | tf_op jit(solution)/shard_map/ppermute | solution.py:34
  192.4 17.9 %collective-permute-start.24 = (bf16[2,128,896]{2,1,0:T(8,128)(2,1)}, bf16[2,128,896]{2,1,0:T(8,128)(2,1)S(1)}, u32[]{:S(2)}, u32[]{:S(2)}) collective-permute-start(bf16[2,128,896]{2,1,0:T(8,128)(2,1)} %get-tuple-element.198), channel_id=1, source_target_pairs={{0,16},{1,17},{2,18},{3,19},{4,20},{5,21},{6,22},{7,23},{8,24},{9,... | collective-permute-start | bytes 1376264 | tf_op jit(solution)/shard_map/ppermute | solution.py:34
  193.3 17.0 %collective-permute-start.25 = (bf16[2,128,896]{2,1,0:T(8,128)(2,1)}, bf16[2,128,896]{2,1,0:T(8,128)(2,1)S(1)}, u32[]{:S(2)}, u32[]{:S(2)}) collective-permute-start(bf16[2,128,896]{2,1,0:T(8,128)(2,1)} %get-tuple-element.199), channel_id=1, source_target_pairs={{0,8},{1,9},{2,10},{3,11},{4,12},{5,13},{6,14},{7,15},{8,0},{9,1},... | collective-permute-start | bytes 1376264 | tf_op jit(solution)/shard_map/ppermute | solution.py:34
  194.3 16.0 %collective-permute-start.26 = (bf16[2,2,32,896]{3,2,1,0:T(8,128)(2,1)}, bf16[2,2,32,896]{3,2,1,0:T(8,128)(2,1)S(1)}, u32[]{:S(2)}, u32[]{:S(2)}) collective-permute-start(bf16[2,2,32,896]{3,2,1,0:T(8,128)(2,1)} %get-tuple-element.200), channel_id=1, source_target_pairs={{0,4},{1,5},{2,6},{3,7},{4,0},{5,1},{6,2},{7,3},{8,12},{9,13},{10,... | collective-permute-start | bytes 688136 | tf_op jit(solution)/shard_map/ppermute | solution.py:34
  235.1 16.8 %collective-permute-start.31 = (bf16[128,896]{1,0:T(8,128)(2,1)}, bf16[128,896]{1,0:T(8,128)(2,1)S(1)}, u32[]{:S(2)}, u32[]{:S(2)}) collective-permute-start(bf16[128,896]{1,0:T(8,128)(2,1)} %get-tuple-element.212), channel_id=1, source_target_pairs={{0,4},{1,5},{2,6},{3,7},{4,0},{5,1},{6,2},{7,3},{8,12},{9,13},{10,... | collective-permute-start | bytes 688136 | tf_op jit(solution)/shard_map/ppermute | solution.py:34
  256.0 16.5 %collective-permute-start.35 = (bf16[320,448]{1,0:T(8,128)(2,1)}, bf16[320,448]{1,0:T(8,128)(2,1)S(1)}, u32[]{:S(2)}, u32[]{:S(2)}) collective-permute-start(bf16[320,448]{1,0:T(8,128)(2,1)} %shard_map.113.refs_0_), channel_id=1, source_target_pairs={{0,16},{1,17},{2,18},{3,19},{4,20},{5,21},{6,22},{7,23},{8,24},{9,... | collective-permute-start | bytes 860168 | tf_op jit(solution)/shard_map/ppermute | solution.py:34
  258.2 16.0 %collective-permute-start.36 = (bf16[320,448]{1,0:T(8,128)(2,1)}, bf16[320,448]{1,0:T(8,128)(2,1)S(1)}, u32[]{:S(2)}, u32[]{:S(2)}) collective-permute-start(bf16[320,448]{1,0:T(8,128)(2,1)} %shard_map.113.refs_0_), channel_id=1, source_target_pairs={{0,24},{1,25},{2,26},{3,27},{4,28},{5,29},{6,30},{7,31},{8,16},{9,... | collective-permute-start | bytes 860168 | tf_op jit(solution)/shard_map/ppermute | solution.py:34
  (57 other events, 584.3 us)

commit v4 on v3

--- a/solution.py
+++ b/solution.py
@@ -278,9 +278,9 @@
     shard_refs, refs = refs[: 2 * (pairs + late)], refs[2 * (pairs + late) :]
     if pairs:
         early_ref, early_squares, refs = refs[0], refs[1], refs[2:]
-    part_ref, feat_ref, stem_ref, give_ref, keep_ref = refs[:5]
-    weights, rows_all, acc, cots, feats, d_stem, lanes_of_core, gated, slopes, squares, inverse = refs[5:16]
-    sems, in_sems, cot_sems, out_sems, stem_sems = refs[16:]
+    feat_ref, stem_ref, give_ref, keep_ref = refs[:4]
+    weights, rows_all, acc, cots, feats, d_stem, lanes_of_core, gated, slopes, squares, inverse = refs[4:15]
+    part_ref, sems, in_sems, cot_sems, out_sems, stem_sems = refs[15:]
     group = 2 * shard_refs[0].shape[0]
     chips = channels // group
     tokens = cot_ref.shape[0]
@@ -457,10 +457,14 @@
         for z in range(i * chips // steps, (i + 1) * chips // steps):
             for h in range(2):
                 first = (2 * z + h) * shard
-                lanes_of_core[h, :, z * room : z * room + shard] = d_stem[:, first : first + shard]
+                part = part_ref[:, first : first + shard]
+                rest = part - part.astype(BF16).astype(F32)
+                lanes = slice(z * room, z * room + shard)
+                lanes_of_core[h, :tokens, lanes] = d_stem[:, first : first + shard]
+                lanes_of_core[h, tokens:, lanes] = jnp.concatenate([part, rest], axis=0).astype(BF16)
                 if room > shard:
                     lanes_of_core[h, :, z * room + shard : (z + 1) * room] = jnp.zeros(
-                        (tokens, room - shard), BF16
+                        (tokens + 16, room - shard), BF16
                     )
         width = chips // steps * room
         lanes = pl.ds(i * width, width)
@@ -495,7 +499,7 @@
             + [ANY_SPEC] * 3
             + [ANY_SPEC] * len(shards)
             + ([ANY_SPEC, VMEM_SPEC] if pairs else []),
-            out_specs=[VMEM_SPEC] + [ANY_SPEC] * 4,
+            out_specs=[ANY_SPEC] * 4,
             scratch_shapes=[
                 pltpu.VMEM((channels, padded), BF16),
                 pltpu.VMEM((total, padded), BF16),
@@ -503,11 +507,12 @@
                 pltpu.VMEM((tokens + 2 * edge, channels), BF16),
                 pltpu.VMEM((tokens, channels), BF16),
                 pltpu.VMEM((tokens, channels), BF16),
-                pltpu.VMEM((2, tokens, half), BF16),
+                pltpu.VMEM((2, tokens + 16, half), BF16),
                 pltpu.VMEM((tokens, channels), F32),
                 pltpu.VMEM((tokens + 2 * edge, LANES), F32),
                 pltpu.VMEM((total, LANES), F32),
                 pltpu.VMEM((total, LANES), F32),
+                pltpu.VMEM((8, channels), F32),
                 pltpu.SemaphoreType.DMA((len(shards),)),
                 pltpu.SemaphoreType.DMA((len(shards) // 2,)),
                 pltpu.SemaphoreType.DMA((4, 3)),
@@ -516,11 +521,10 @@
             ],
         ),
         out_shape=[
-            jax.ShapeDtypeStruct((8, channels), F32),
             jax.ShapeDtypeStruct((tokens, channels), BF16),
             jax.ShapeDtypeStruct((tokens, channels), BF16),
-            jax.ShapeDtypeStruct((tokens, half), BF16),
-            jax.ShapeDtypeStruct((tokens, half), BF16),
+            jax.ShapeDtypeStruct((tokens + 16, half), BF16),
+            jax.ShapeDtypeStruct((tokens + 16, half), BF16),
         ],
         compiler_params=kernel_params(60),
     )(places, mask, main, low, high, cot, cot_low, cot_high, *shards, *early)
@@ -569,12 +573,18 @@
 
 def turn_kernel(first_ref, second_ref, out_ref, *, tokens):
     height, depth = out_ref.shape
-    out_ref[:, 2 * tokens :] = jnp.zeros((height, depth - 2 * tokens), BF16)
-    both = jnp.concatenate([first_ref[:tokens], second_ref[:tokens]], axis=0)
-    for m in range(0, first_ref.shape[1], LANES):
+    padded = first_ref.shape[1]
+    row = lax.broadcasted_iota(jnp.int32, (16, padded), 0) % 8
+    column = lax.broadcasted_iota(jnp.int32, (16, padded), 1)
+    extra = jnp.where((column == padded - 16 + row) & (row < 6), 1.0, 0.0).astype(BF16)
+    out_ref[:, 2 * tokens + 32 :] = jnp.zeros((height, depth - 2 * tokens - 32), BF16)
+    both = jnp.concatenate([first_ref[:tokens], extra, second_ref[:tokens], extra], axis=0)
+    for m in range(0, height, LANES):
         count = min(LANES, height - m)
-        if count > 0:
-            out_ref[m : m + count, : 2 * tokens] = both[:, m : m + LANES].T[:count]
+        if m < padded:
+            out_ref[m : m + count, : 2 * tokens + 32] = both[:, m : m + LANES].T[:count]
+        else:
+            out_ref[m : m + count, :] = jnp.zeros((count, depth), BF16)
 
 
 def turned(packed, packed_other, height, tokens):
@@ -582,7 +592,7 @@
         functools.partial(turn_kernel, tokens=tokens),
         in_specs=[VMEM_SPEC] * 2,
         out_specs=VMEM_SPEC,
-        out_shape=jax.ShapeDtypeStruct((height, round_up(2 * tokens, LANES)), BF16),
+        out_shape=jax.ShapeDtypeStruct((height, round_up(2 * tokens + 32, LANES)), BF16),
         compiler_params=kernel_params(16),
     )(packed, packed_other)
 
@@ -838,13 +848,6 @@
     yield final[0], None
 
 
-def all_sum(value, routes):
-    ((came, _, give),) = yield [value], routes[:1]
-    for route in routes[1:]:
-        ((came, _, give),) = yield [([[(give, []), (came, [])]], None, F32)], [route]
-    yield (give, came), None
-
-
 def in_rounds(chains, beside):
     waiting = [next(chain) for chain in chains]
     count, done = 0, None
@@ -867,32 +870,42 @@
     return [values for values, _ in waiting], done
 
 
-def unpack_kernel(at_ref, *refs, share, line_share):
-    pieces, (out_ref, rows_all) = refs[:-2], refs[-2:]
-    width = out_ref.shape[1]
+def unpack_kernel(at_ref, *refs, share, line_share, chan_row):
+    pieces, (out_ref, chan_ref, rows_all) = refs[:-3], refs[-3:]
+    shard, width = out_ref.shape
     for o, piece in enumerate(pieces):
         p = at_ref[0] ^ o
-        first = pl.multiple_of(p * share, 16)
-        rows_all[pl.ds(first, share), :] = piece[0:share]
-        first = pl.multiple_of(len(pieces) * share + p * line_share, 16)
-        rows_all[pl.ds(first, line_share), :] = piece[share:]
+        begin = 0
+        for base, count in ((p * share, share), (len(pieces) * share + p * line_share, line_share)):
+            half = count // 2
+            for h in range(2):
+                first = pl.multiple_of(base + h * half, 16)
+                rows_all[pl.ds(first, half), :] = piece[
+                    begin : begin + half, h * shard : (h + 1) * shard
+                ]
+            begin += half
     for first in range(0, width, LANES):
         size = min(LANES, width - first)
         out_ref[:, first : first + size] = rows_all[first : first + LANES].T[:, :size]
-
-
-def unpacked(pieces, seq_index, width, share, line_share):
-    height, shard = pieces[0].shape
+    chan_ref[...] = rows_all[chan_row : chan_row + 16].astype(F32)[:6]
+
+
+def unpacked(pieces, seq_index, width, share, line_share, chan_row):
+    rows, lanes = pieces[0].shape
+    shard = lanes // 2
     return pl.pallas_call(
-        functools.partial(unpack_kernel, share=share, line_share=line_share),
+        functools.partial(unpack_kernel, share=share, line_share=line_share, chan_row=chan_row),
         grid_spec=pltpu.PrefetchScalarGridSpec(
             num_scalar_prefetch=1,
             grid=(),
             in_specs=[VMEM_SPEC] * len(pieces),
-            out_specs=VMEM_SPEC,
-            scratch_shapes=[pltpu.VMEM((len(pieces) * height, shard), BF16)],
+            out_specs=[VMEM_SPEC] * 2,
+            scratch_shapes=[pltpu.VMEM((2 * len(pieces) * rows, shard), BF16)],
         ),
-        out_shape=jax.ShapeDtypeStruct((shard, width), BF16),
+        out_shape=[
+            jax.ShapeDtypeStruct((shard, width), BF16),
+            jax.ShapeDtypeStruct((6, shard), F32),
+        ],
         compiler_params=kernel_params(60),
     )(seq_index.astype(jnp.int32).reshape(1), *pieces)
 
@@ -902,14 +915,12 @@
     ins, out_ref = refs[:count], refs[count]
     buffers, sems = list(refs[count + 1 : -1]), refs[-1]
     copies = fetched(at_ref, ins, buffers, sems, indices)
-    shard = out_ref.shape[1]
     begin = 0
     for n in counts:
         total = (total_of(copies[:n], buffers[:n]) * scale).astype(BF16)
         copies, buffers = copies[n:], buffers[n:]
-        for part in (total[:, :shard], total[:, shard:]):
-            out_ref[begin : begin + part.shape[0], :] = part
-            begin += part.shape[0]
+        out_ref[begin : begin + total.shape[0], :] = total
+        begin += total.shape[0]
 
 
 def finish(chains, scale):
@@ -920,8 +931,8 @@
             scalars += index
             arrays.append(array)
             buffers.append(pltpu.VMEM(tuple(array.shape[-2:]), array.dtype))
-        height += 2 * terms[0][0].shape[-2]
-    shard = arrays[0].shape[-1] // 2
+        height += terms[0][0].shape[-2]
+    lanes = arrays[0].shape[-1]
     return pl.pallas_call(
         functools.partial(
             finish_kernel, counts=[len(t) for t in chains], indices=indices, scale=scale
@@ -933,7 +944,7 @@
             out_specs=VMEM_SPEC,
             scratch_shapes=buffers + [pltpu.SemaphoreType.DMA((len(arrays),))],
         ),
-        out_shape=jax.ShapeDtypeStruct((height, shard), BF16),
+        out_shape=jax.ShapeDtypeStruct((height, lanes), BF16),
         compiler_params=kernel_params(60),
     )(jnp.stack([jnp.asarray(s, jnp.int32) for s in scalars]), *arrays)
 
@@ -994,7 +1005,8 @@
         chip_of.append(origin)
 
     for k in range(1, chips):
-        rising[k], falling[k] = chain_step(rising[k - 1], falling[k - 1], k, chips)
+        if k < 3 or not split:
+            rising[k], falling[k] = chain_step(rising[k - 1], falling[k - 1], k, chips)
         if k == 1:
             came = [swapped(boxes[o - 1], o, 0) for o in direct]
             rising, falling, came, boxes, tail, head = together(
@@ -1007,6 +1019,7 @@
             if split:
                 rising[1], falling[1], spots = together(rising[1], falling[1], spots)
                 add_shard(1, rising, falling)
+                near = jnp.where(chip < chips // 2, rising[1], falling[1])
             rising, falling, cot_low, came, core_shards, lane_shards, spots, head = together(
                 rising, falling, cot_low, came, core_shards, lane_shards, spots, head
             )
@@ -1024,6 +1037,10 @@
             )
             if split:
                 add_shard(2, rising, falling)
+                final = sent(
+                    lane_shards[2],
+                    lambda s, f: (s, f + 2) if f // 2 == 2 else (s, f - 2) if f // 2 == 1 else None,
+                )
                 main, main_head, main_tail, lane_shards, core_shards = together(
                     main, main_head, main_tail, lane_shards, core_shards
                 )
@@ -1032,9 +1049,13 @@
         elif k == 3 and split:
             pairs = [v for both in zip(lane_shards, core_shards) for v in both]
             early_main, main_squares = stem_early(main, pairs, core_id)
-            rising, falling, early_main, low, high, main, cot_high = together(
-                rising, falling, early_main, low, high, main, cot_high
+            final, early_main, low, high, main, cot_high = together(
+                final, early_main, low, high, main, cot_high
             )
+            outer = (chip == 0) | (chip == chips - 1)
+            lane_shards.append(jnp.where(outer, final, near))
+            core_shards.append(swapped(lane_shards[-1], 0, 1))
+            chip_of.append(jnp.where(outer, chips - 1 - chip, jnp.where(chip == 1, 0, chips - 1)))
         else:
             rising, falling = together(rising, falling)
     for k in range(len(lane_shards), chips):
@@ -1056,10 +1077,9 @@
         ids[jnp.clip(near, 0, total_slots - 1)] == ids[jnp.clip(centre, 0, total_slots - 1)][:, None]
     )
     mask = (inside & same).astype(F32).reshape(-1)
-    chan_part, features, d_stem, give, keep = layer(
+    features, d_stem, give, keep = layer(
         main, low, high, cot, cot_low, cot_high, all_pairs, early, places, mask, slots, channels
     )
-    chan_part = chan_part + swapped(chan_part, 0, 1)
     got = swapped(give, 0, 1)
     pixels = turned(main, main_other, height, tokens)
     middle = round_up(width // 2, LANES)
@@ -1095,7 +1115,6 @@
             [chip_labels + seq_labels],
             mine,
         ),
-        all_sum(chan_part, [route_of(label) for label in seq_labels + chip_labels]),
     ]
     last_round = len(seq_bits) + len(chip_bits) - 1
 
@@ -1103,17 +1122,14 @@
         inputs, ready = together(d_stem, ready)
         return ready, pixel_grads(inputs, all_pairs, places, 0, middle)
 
-    (plane, line, chan), grad_rows = in_rounds(chains, {last_round: left_pixels})
+    (plane, line), grad_rows = in_rounds(chains, {last_round: left_pixels})
     rows_mine = finish([plane, line], scale)
     d_stem, rows_mine = together(d_stem, rows_mine)
     pieces = [rows_mine] + [swapped(rows_mine, o, 0) for o in range(1, seq_size)]
     grad_rows = pixel_grads(d_stem, all_pairs, places, middle, width, grad_rows)
     pieces, grad_rows = together(pieces, grad_rows)
-    grad_weight = unpacked(pieces, seq_index, width, share, line_share)
-    first = fsdp_index * shard
-    grad_channels = scale * (
-        lax.dynamic_slice_in_dim(chan[0], first, shard, axis=1)[:6]
-        + lax.dynamic_slice_in_dim(chan[1], first, shard, axis=1)[:6]
+    grad_weight, grad_channels = unpacked(
+        pieces, seq_index, width, share, line_share, padded - 16
     )
     return (features[None], grad_rows[None], grad_weight, grad_channels)
 

time: 279 us -> 258 us (0.925)
  starting transfers between devices: 58 us -> 46.9 us
  waiting for transfers between devices: 78.6 us -> 73.8 us
  other arithmetic: 7.18 us -> 4.38 us
    ppermute x37 -> x31, starting transfers between devices: 58 us -> 46.9 us  [sent(): return lax.ppermute(value, AXES, pairs)]
    ppermute x37 -> x31, waiting for transfers between devices: 78.6 us -> 73.8 us  [sent(): return lax.ppermute(value, AXES, pairs)]
    select_n x3 -> x2, other arithmetic: 4.32 us -> 1.52 us  [chosen(): value = jnp.where(which == i, option, value)]
    unnamed x89 -> x79, local copies, waits for them, and re-layouts: 15.3 us -> 14.1 us
  transfers between devices with their start and end apart: 37 -> 31, of which waited for: 16 -> 14; matrix products, arithmetic and copies ran while one was open for 5% -> 5% of each run, Pallas kernels for 16% -> 18%
where the time goes in v4:
time: 258 us; the launch traced here: 257 us
  Pallas kernels  104 us (40%)
  waiting for transfers between devices  73.8 us (29%)
  starting transfers between devices  46.9 us (18%)
  local copies, waits for them, and re-layouts  27.2 us (11%)
  other arithmetic  4.38 us (2%)
    ppermute x31, waiting for transfers between devices, sent(): return lax.ppermute(value, AXES, pairs)  73.8 us
    ppermute x31, starting transfers between devices, sent(): return lax.ppermute(value, AXES, pairs)  46.9 us
    pallas_call x1, Pallas kernels, layer(): pl.pallas_call(functools.partial(layer_kernel, pairs=pairs, late=late, sl...  34.9 us
    pallas_call x2, Pallas kernels, pixel_grads(): pl.pallas_call(functools.partial(pixel_kernel, chips=chips, begin=begin,...  19 us
    pallas_call x2, Pallas kernels, weight_part(): pl.pallas_call(functools.partial(weight_kernel, bits=bits, share=share, l...  16.6 us
    unnamed x79, local copies, waits for them, and re-layouts  14.1 us
    pallas_call x3, Pallas kernels, sums(): pl.pallas_call(functools.partial(sums_kernel, plan=plan, indices=indices)...  9.84 us
    pallas_call x2, Pallas kernels, scalar_call(): pl.pallas_call(kernel, grid_spec=pltpu.PrefetchScalarGridSpec(num_scalar_...  7.94 us
  transfers between devices with their start and end apart: 31, of which 14 were waited for; matrix products, arithmetic and copies ran while one was open for 5% of the time, Pallas kernels for 18%

profile of v4, /device:TPU:0, one launch (start us, length us, event | category | flops | bytes accessed | tf_op | source)
XLA Modules:
  0.0 257.2 jit_solution(12128476940890983479)
XLA Ops:
  4.8 5.0 %collective-permute-start = (bf16[448,1280]{1,0:T(8,128)(2,1)S(1)}, bf16[448,1280]{1,0:T(8,128)(2,1)S(1)}, u32[]{:S(2)}, u32[]{:S(2)}) collective-permute-start(bf16[448,1280]{1,0:T(8,128)(2,1)S(1)} %concatenate.3.refs_0_), channel_id=1, source_target_pairs={{0,2},{1,3},{2,4},{3,5},{4,6},{5,7},{8,10},{9,11},{10,12},{11,13},... | collective-permute-start | bytes 3440648 | tf_op jit(solution)/shard_map/ppermute | solution.py:34
  12.9 3.4 %shard_map.102 = (bf16[8,32,1280]{2,1,0:T(8,128)(2,1)}, bf16[8,32,1280]{2,1,0:T(8,128)(2,1)}, bf16[8,32,1280]{2,1,0:T(8,128)(2,1)}) custom-call(s32[24]{0:T(128)} %reshape.240.order_ref, f32[24]{0:T(128)} %convert_element_type.27.spot_ref, bf16[17,32,1176]{2,1,0:T(8,128)(2,1)} %bitcast.46), custom_call_target="tpu_custom_call" | custom-call | tf_op jit(solution)/shard_map/pallas_call | solution.py:106
  21.3 12.9 %collective-permute-done = bf16[448,1280]{1,0:T(8,128)(2,1)S(1)} collective-permute-done((bf16[448,1280]{1,0:T(8,128)(2,1)S(1)}, bf16[448,1280]{1,0:T(8,128)(2,1)S(1)}, u32[]{:S(2)}, u32[]{:S(2)}) %collective-permute-start) | collective-permute-done | bytes 1146912 | tf_op jit(solution)/shard_map/ppermute | solution.py:34
  34.2 4.3 %collective-permute-done.1 = bf16[448,1280]{1,0:T(8,128)(2,1)} collective-permute-done((bf16[448,1280]{1,0:T(8,128)(2,1)S(1)}, bf16[448,1280]{1,0:T(8,128)(2,1)}, u32[]{:S(2)}, u32[]{:S(2)}) %collective-permute-start.1) | collective-permute-done | bytes 1146912 | tf_op jit(solution)/shard_map/ppermute | solution.py:34
  47.6 22.0 %collective-permute-done.7.cot_low_ref = bf16[64,3584]{1,0:T(8,128)(2,1)S(1)} collective-permute-done((bf16[64,3584]{1,0:T(8,128)(2,1)S(1)}, bf16[64,3584]{1,0:T(8,128)(2,1)S(1)}, u32[]{:S(2)}, u32[]{:S(2)}) %collective-permute-start.7) | collective-permute-done | bytes 458784 | tf_op jit(solution)/shard_map/ppermute | solution.py:34
  75.2 4.5 %shard_map.103 = (bf16[560,1280]{1,0:T(8,128)(2,1)}, bf16[128,1280]{1,0:T(8,128)(2,1)}, bf16[128,1280]{1,0:T(8,128)(2,1)}) custom-call(s32[17]{0:T(128)} %add.198.pick_ref, bf16[17,32,1176]{2,1,0:T(8,128)(2,1)} %bitcast.47, bf16[8,32,1280]{2,1,0:T(8,128)(2,1)} %copy-done.27, bf16[8,32,1280]{2,1,0:T(8,128)(2,1)} %copy-done.28, bf16[8,32,1280]{2,1,0:T(8,128)(2,1)} %copy-done.29), custom_call_target="tpu_custom_call" | custom-call | tf_op jit(solution)/shard_map/pallas_call | solution.py:106
  79.7 5.7 %collective-permute-start.12 = (bf16[128,1280]{1,0:T(8,128)(2,1)}, bf16[128,1280]{1,0:T(8,128)(2,1)}, u32[]{:S(2)}, u32[]{:S(2)}) collective-permute-start(bf16[128,1280]{1,0:T(8,128)(2,1)} %get-tuple-element.146), channel_id=1, source_target_pairs={{0,8},{1,9},{2,10},{3,11},{4,12},{5,13},{6,14},{7,15},{8,16},{9,17... | collective-permute-start | bytes 983048 | tf_op jit(solution)/shard_map/ppermute | solution.py:34
  89.5 7.6 %shard_map.104 = (f32[3,560,896]{2,1,0:T(8,128)S(1)}, f32[560,128]{1,0:T(8,128)S(1)}) custom-call(s32[1]{0:T(128)} %bitcast.place_ref, bf16[560,1280]{1,0:T(8,128)(2,1)} %get-tuple-element.149.rows_ref.main_ref.first_ref, bf16[448,1280]{1,0:T(8,128)(2,1)S(1)} %concatenate.3.refs_0_, bf16[448,1280]{1,0:T(8,128)(2,1)S(1)} %copy-done.7, ...), custom_call_target="tpu_custom_call" | custom-call | tf_op jit(solution)/shard_map/pallas_call | solution.py:243
  99.6 4.2 %collective-permute-done.10 = bf16[448,1280]{1,0:T(8,128)(2,1)} collective-permute-done((bf16[448,1280]{1,0:T(8,128)(2,1)S(1)}, bf16[448,1280]{1,0:T(8,128)(2,1)}, u32[]{:S(2)}, u32[]{:S(2)}) %collective-permute-start.10) | collective-permute-done | bytes 1146912 | tf_op jit(solution)/shard_map/ppermute | solution.py:34
  109.6 34.9 %shard_map.105 = (bf16[544,3584]{1,0:T(8,128)(2,1)}, bf16[544,3584]{1,0:T(8,128)(2,1)}, bf16[560,2048]{1,0:T(8,128)(2,1)}, bf16[560,2048]{1,0:T(8,128)(2,1)}) custom-call(s32[5]{0:T(128)} %stack.51.place_ref, f32[105]{0:T(128)} %reshape.245.mask_ref, bf16[560,1280]{1,0:T(8,128)(2,1)} %get-tuple-element.149.rows_ref.main_ref.first_ref, ...), custom_call_target="tpu_custom_call" | custom-call | tf_op jit(solution)/shard_map/pallas_call | solution.py:493
  149.2 7.6 %shard_map.108 = (bf16[2,2,128,896]{3,2,1,0:T(8,128)(2,1)}, bf16[2,2,128,896]{3,2,1,0:T(8,128)(2,1)}, bf16[2,4,32,896]{3,2,1,0:T(8,128)(2,1)S(1)}) custom-call(s32[2]{0:T(128)S(1)} %pad_add_fusion.where_ref, bf16[1280,1152]{1,0:T(8,128)(2,1)S(1)} %shard_map.106.pixels_ref, bf16[560,2048]{1,0:T(8,128)(2,1)S(1)} %copy-done.10, ...), custom_call_target="tpu_custom_call" | custom-call | tf_op jit(solution)/shard_map/pallas_call | solution.py:677
  159.9 3.8 %collective-permute-start.20 = (bf16[2,4,32,896]{3,2,1,0:T(8,128)(2,1)S(1)}, bf16[2,4,32,896]{3,2,1,0:T(8,128)(2,1)S(1)}, u32[]{:S(2)}, u32[]{:S(2)}) collective-permute-start(bf16[2,4,32,896]{3,2,1,0:T(8,128)(2,1)S(1)} %get-tuple-element.173), channel_id=1, source_target_pairs={{0,2},{1,3},{2,0},{3,1},{4,6},{5,7},{6,4},{7,5},{8,10},{9,11},{10,... | collective-permute-start | bytes 1376264 | tf_op jit(solution)/shard_map/ppermute | solution.py:34
  164.4 9.0 %shard_map.107 = (f32[2,2,128,896]{3,2,1,0:T(8,128)}, f32[2,2,128,896]{3,2,1,0:T(8,128)}, f32[2,4,32,896]{3,2,1,0:T(8,128)}) custom-call(s32[2]{0:T(128)} %copy-done.16, bf16[1280,1152]{1,0:T(8,128)(2,1)} %copy-done.5, bf16[560,2048]{1,0:T(8,128)(2,1)} %get-tuple-element.168.keep_ref, bf16[560,2048]{1,0:T(8,128)(2,1)} %copy-done.11), custom_call_target="tpu_custom_call" | custom-call | tf_op jit(solution)/shard_map/pallas_call | solution.py:677
  174.2 6.0 %collective-permute-done.18.refs_1_ = bf16[2,2,128,896]{3,2,1,0:T(8,128)(2,1)S(1)} collective-permute-done((bf16[2,2,128,896]{3,2,1,0:T(8,128)(2,1)}, bf16[2,2,128,896]{3,2,1,0:T(8,128)(2,1)S(1)}, u32[]{:S(2)}, u32[]{:S(2)}) %collective-permute-start.18) | collective-permute-done | bytes 917536 | tf_op jit(solution)/shard_map/ppermute | solution.py:34
  182.6 3.4 %shard_map.109 = (bf16[2,128,896]{2,1,0:T(8,128)(2,1)}, bf16[2,128,896]{2,1,0:T(8,128)(2,1)}, bf16[2,2,32,896]{3,2,1,0:T(8,128)(2,1)}) custom-call(s32[6]{0:T(128)} %stack.132.at_ref, f32[2,2,128,896]{3,2,1,0:T(8,128)} %get-tuple-element.170.refs_0_, bf16[2,2,128,896]{3,2,1,0:T(8,128)(2,1)} %copy-done.18, ...), custom_call_target="tpu_custom_call" | custom-call | tf_op jit(solution)/shard_map/pallas_call | solution.py:784
  188.1 4.1 %collective-permute-start.23 = (bf16[2,2,32,896]{3,2,1,0:T(8,128)(2,1)}, bf16[2,2,32,896]{3,2,1,0:T(8,128)(2,1)S(1)}, u32[]{:S(2)}, u32[]{:S(2)}) collective-permute-start(bf16[2,2,32,896]{3,2,1,0:T(8,128)(2,1)} %get-tuple-element.181), channel_id=1, source_target_pairs={{0,4},{1,5},{2,6},{3,7},{4,0},{5,1},{6,2},{7,3},{8,12},{9,13},{10,... | collective-permute-start | bytes 688136 | tf_op jit(solution)/shard_map/ppermute | solution.py:34
  192.8 9.3 %collective-permute-done.23.refs_8_.refs_10_.refs_4_ = bf16[2,2,32,896]{3,2,1,0:T(8,128)(2,1)S(1)} collective-permute-done((bf16[2,2,32,896]{3,2,1,0:T(8,128)(2,1)}, bf16[2,2,32,896]{3,2,1,0:T(8,128)(2,1)S(1)}, u32[]{:S(2)}, u32[]{:S(2)}) %collective-permute-start.23) | collective-permute-done | bytes 229408 | tf_op jit(solution)/shard_map/ppermute | solution.py:34
  203.7 3.1 %shard_map.110 = (bf16[2,128,896]{2,1,0:T(8,128)(2,1)}, bf16[2,32,896]{2,1,0:T(8,128)(2,1)}) custom-call(s32[15]{0:T(128)} %stack.134.at_ref, f32[2,2,128,896]{3,2,1,0:T(8,128)} %get-tuple-element.170.refs_0_, bf16[2,2,128,896]{3,2,1,0:T(8,128)(2,1)} %copy-done.18, bf16[2,128,896]{2,1,0:T(8,128)(2,1)} %copy-done.24, ...), custom_call_target="tpu_custom_call" | custom-call | tf_op jit(solution)/shard_map/pallas_call | solution.py:784
  209.0 3.0 %collective-permute-done.25.refs_11_.refs_5_ = bf16[2,32,896]{2,1,0:T(8,128)(2,1)S(1)} collective-permute-done((bf16[2,32,896]{2,1,0:T(8,128)(2,1)}, bf16[2,32,896]{2,1,0:T(8,128)(2,1)S(1)}, u32[]{:S(2)}, u32[]{:S(2)}) %collective-permute-start.25) | collective-permute-done | bytes 114720 | tf_op jit(solution)/shard_map/ppermute | solution.py:34
  212.0 6.5 %collective-permute-done.24.refs_3_.refs_7_ = bf16[2,128,896]{2,1,0:T(8,128)(2,1)S(1)} collective-permute-done((bf16[2,128,896]{2,1,0:T(8,128)(2,1)}, bf16[2,128,896]{2,1,0:T(8,128)(2,1)S(1)}, u32[]{:S(2)}, u32[]{:S(2)}) %collective-permute-start.24) | collective-permute-done | bytes 458784 | tf_op jit(solution)/shard_map/ppermute | solution.py:34
  219.2 3.4 %shard_map.111 = (bf16[128,896]{1,0:T(8,128)(2,1)}, f32[128,896]{1,0:T(8,128)}, bf16[32,896]{1,0:T(8,128)(2,1)}) custom-call(s32[22]{0:T(128)} %stack.61.at_ref, f32[2,2,128,896]{3,2,1,0:T(8,128)} %get-tuple-element.170.refs_0_, bf16[2,2,128,896]{3,2,1,0:T(8,128)(2,1)} %copy-done.18, bf16[2,128,896]{2,1,0:T(8,128)(2,1)} %copy-done.24, ...), custom_call_target="tpu_custom_call" | custom-call | tf_op jit(solution)/shard_map/pallas_call | solution.py:784
  225.0 9.2 %shard_map.112.refs_8_ = bf16[544,640]{1,0:T(8,128)(2,1)} custom-call(s32[5]{0:T(128)} %stack.51.place_ref, bf16[544,3584]{1,0:T(8,128)(2,1)} %get-tuple-element.197.d_stem_ref, bf16[448,1280]{1,0:T(8,128)(2,1)} %copy-done.2, bf16[448,1280]{1,0:T(8,128)(2,1)} %copy-done.6, bf16[448,1280]{1,0:T(8,128)(2,1)} %copy-done.3, bf16[448,1280]{1,0:T(8,128)(2,1)} %copy-done.8, ...), custom_call_target="tpu_custom_call" | custom-call | tf_op jit(solution)/shard_map/pallas_call | solution.py:555
  241.8 9.7 %shard_map.114 = bf16[544,1176]{1,0:T(8,128)(2,1)} custom-call(s32[5]{0:T(128)} %stack.51.place_ref, bf16[544,3584]{1,0:T(8,128)(2,1)} %get-tuple-element.197.d_stem_ref, bf16[448,1280]{1,0:T(8,128)(2,1)} %copy-done.2, bf16[448,1280]{1,0:T(8,128)(2,1)} %copy-done.6, bf16[448,1280]{1,0:T(8,128)(2,1)} %copy-done.3, bf16[448,1280]{1,0:T(8,128)(2,1)} %copy-done.8, ...), custom_call_target="tpu_custom_call" | custom-call | tf_op jit(solution)/shard_map/pallas_call | solution.py:555
  254.4 2.8 %shard_map.115 = (bf16[448,1176]{1,0:T(8,128)(2,1)}, f32[6,448]{1,0:T(8,128)}) custom-call(s32[1]{0:T(128)} %bitcast.20.at_ref, bf16[160,896]{1,0:T(8,128)(2,1)} %shard_map.113.refs_0_, bf16[160,896]{1,0:T(8,128)(2,1)} %copy-done.32, bf16[160,896]{1,0:T(8,128)(2,1)} %copy-done.33, bf16[160,896]{1,0:T(8,128)(2,1)} %copy-done.34), custom_call_target="tpu_custom_call" | custom-call | tf_op jit(solution)/shard_map/pallas_call | solution.py:896
  (175 shorter events, 70.5 us)
Async XLA Ops:
  4.8 29.4 %collective-permute-start = (bf16[448,1280]{1,0:T(8,128)(2,1)S(1)}, bf16[448,1280]{1,0:T(8,128)(2,1)S(1)}, u32[]{:S(2)}, u32[]{:S(2)}) collective-permute-start(bf16[448,1280]{1,0:T(8,128)(2,1)S(1)} %concatenate.3.refs_0_), channel_id=1, source_target_pairs={{0,2},{1,3},{2,4},{3,5},{4,6},{5,7},{8,10},{9,11},{10,12},{11,13},... | collective-permute-start | bytes 3440648 | tf_op jit(solution)/shard_map/ppermute | solution.py:34
  9.8 28.7 %collective-permute-start.1 = (bf16[448,1280]{1,0:T(8,128)(2,1)S(1)}, bf16[448,1280]{1,0:T(8,128)(2,1)}, u32[]{:S(2)}, u32[]{:S(2)}) collective-permute-start(bf16[448,1280]{1,0:T(8,128)(2,1)S(1)} %concatenate.3.refs_0_), channel_id=1, source_target_pairs={{2,0},{3,1},{4,2},{5,3},{6,4},{7,5},{10,8},{11,9},{12,10},{13,11},... | collective-permute-start | bytes 3440648 | tf_op jit(solution)/shard_map/ppermute | solution.py:34
  16.3 22.2 %collective-permute-start.3 = (bf16[8,32,1280]{2,1,0:T(8,128)(2,1)}, bf16[8,32,1280]{2,1,0:T(8,128)(2,1)S(1)}, u32[]{:S(2)}, u32[]{:S(2)}) collective-permute-start(bf16[8,32,1280]{2,1,0:T(8,128)(2,1)} %get-tuple-element.110), channel_id=1, source_target_pairs={{0,8},{1,9},{2,10},{3,11},{4,12},{5,13},{6,14},{7,15},{8,0},{9,1},... | collective-permute-start | bytes 1966088 | tf_op jit(solution)/shard_map/ppermute | solution.py:34
  17.8 20.7 %collective-permute-start.4 = (bf16[8,32,1280]{2,1,0:T(8,128)(2,1)}, bf16[8,32,1280]{2,1,0:T(8,128)(2,1)S(1)}, u32[]{:S(2)}, u32[]{:S(2)}) collective-permute-start(bf16[8,32,1280]{2,1,0:T(8,128)(2,1)} %get-tuple-element.111), channel_id=1, source_target_pairs={{0,16},{1,17},{2,18},{3,19},{4,20},{5,21},{6,22},{7,23},{8,24},{9,... | collective-permute-start | bytes 1966088 | tf_op jit(solution)/shard_map/ppermute | solution.py:34
  38.9 30.7 %collective-permute-start.5 = (bf16[448,1280]{1,0:T(8,128)(2,1)S(1)}, bf16[448,1280]{1,0:T(8,128)(2,1)S(1)}, u32[]{:S(2)}, u32[]{:S(2)}) collective-permute-start(bf16[448,1280]{1,0:T(8,128)(2,1)S(1)} %collective-permute-done), channel_id=1, source_target_pairs={{2,4},{3,5},{4,6},{5,7},{10,12},{11,13},{12,14},{13,15},{18,20},{1... | collective-permute-start | bytes 3440648 | tf_op jit(solution)/shard_map/ppermute | solution.py:34
  39.8 30.2 %collective-permute-start.6 = (bf16[448,1280]{1,0:T(8,128)(2,1)}, bf16[448,1280]{1,0:T(8,128)(2,1)S(1)}, u32[]{:S(2)}, u32[]{:S(2)}) collective-permute-start(bf16[448,1280]{1,0:T(8,128)(2,1)} %collective-permute-done.1), channel_id=1, source_target_pairs={{2,0},{3,1},{4,2},{5,3},{10,8},{11,9},{12,10},{13,11},{18,16},{19,... | collective-permute-start | bytes 3440648 | tf_op jit(solution)/shard_map/ppermute | solution.py:34
  42.6 27.8 %collective-permute-start.9 = (bf16[448,1280]{1,0:T(8,128)(2,1)S(1)}, bf16[448,1280]{1,0:T(8,128)(2,1)S(1)}, u32[]{:S(2)}, u32[]{:S(2)}) collective-permute-start(bf16[448,1280]{1,0:T(8,128)(2,1)S(1)} %broadcast_select_fusion.1.refs_2_), channel_id=1, source_target_pairs={{0,1},{1,0},{2,3},{3,2},{4,5},{5,4},{6,7},{7,6},{8,9},{9,8},{10,11... | collective-permute-start | bytes 3440648 | tf_op jit(solution)/shard_map/ppermute | solution.py:34
  42.7 26.9 %collective-permute-start.8 = (bf16[8,32,1280]{2,1,0:T(8,128)(2,1)S(1)}, bf16[8,32,1280]{2,1,0:T(8,128)(2,1)S(1)}, u32[]{:S(2)}, u32[]{:S(2)}) collective-permute-start(bf16[8,32,1280]{2,1,0:T(8,128)(2,1)S(1)} %copy-done.38), channel_id=1, source_target_pairs={{0,24},{1,25},{2,26},{3,27},{4,28},{5,29},{6,30},{7,31},{8,16},{9,... | collective-permute-start | bytes 1966088 | tf_op jit(solution)/shard_map/ppermute | solution.py:34
  45.2 24.4 %collective-permute-start.7 = (bf16[64,3584]{1,0:T(8,128)(2,1)S(1)}, bf16[64,3584]{1,0:T(8,128)(2,1)S(1)}, u32[]{:S(2)}, u32[]{:S(2)}) collective-permute-start(bf16[64,3584]{1,0:T(8,128)(2,1)S(1)} %get-tuple-element.120), channel_id=1, source_target_pairs={{0,8},{1,9},{2,10},{3,11},{4,12},{5,13},{6,14},{7,15},{8,16},{9,17... | collective-permute-start | bytes 1376264 | tf_op jit(solution)/shard_map/ppermute | solution.py:34
  71.6 32.2 %collective-permute-start.10 = (bf16[448,1280]{1,0:T(8,128)(2,1)S(1)}, bf16[448,1280]{1,0:T(8,128)(2,1)}, u32[]{:S(2)}, u32[]{:S(2)}) collective-permute-start(bf16[448,1280]{1,0:T(8,128)(2,1)S(1)} %broadcast_select_fusion.refs_4_), channel_id=1, source_target_pairs={{2,0},{3,1},{4,6},{5,7},{10,8},{11,9},{12,14},{13,15},{18,16},{19,... | collective-permute-start | bytes 3440648 | tf_op jit(solution)/shard_map/ppermute | solution.py:34
  72.9 26.7 %collective-permute-start.14 = (bf16[64,3584]{1,0:T(8,128)(2,1)}, bf16[64,3584]{1,0:T(8,128)(2,1)}, u32[]{:S(2)}, u32[]{:S(2)}) collective-permute-start(bf16[64,3584]{1,0:T(8,128)(2,1)} %get-tuple-element.148), channel_id=1, source_target_pairs={{8,0},{9,1},{10,2},{11,3},{12,4},{13,5},{14,6},{15,7},{16,8},{17,9... | collective-permute-start | bytes 1376264 | tf_op jit(solution)/shard_map/ppermute | solution.py:34
  79.7 24.2 %collective-permute-start.12 = (bf16[128,1280]{1,0:T(8,128)(2,1)}, bf16[128,1280]{1,0:T(8,128)(2,1)}, u32[]{:S(2)}, u32[]{:S(2)}) collective-permute-start(bf16[128,1280]{1,0:T(8,128)(2,1)} %get-tuple-element.146), channel_id=1, source_target_pairs={{0,8},{1,9},{2,10},{3,11},{4,12},{5,13},{6,14},{7,15},{8,16},{9,17... | collective-permute-start | bytes 983048 | tf_op jit(solution)/shard_map/ppermute | solution.py:34
  85.4 18.4 %collective-permute-start.13 = (bf16[128,1280]{1,0:T(8,128)(2,1)}, bf16[128,1280]{1,0:T(8,128)(2,1)}, u32[]{:S(2)}, u32[]{:S(2)}) collective-permute-start(bf16[128,1280]{1,0:T(8,128)(2,1)} %get-tuple-element.147), channel_id=1, source_target_pairs={{8,0},{9,1},{10,2},{11,3},{12,4},{13,5},{14,6},{15,7},{16,8},{17,9... | collective-permute-start | bytes 983048 | tf_op jit(solution)/shard_map/ppermute | solution.py:34
  156.8 23.4 %collective-permute-start.18 = (bf16[2,2,128,896]{3,2,1,0:T(8,128)(2,1)}, bf16[2,2,128,896]{3,2,1,0:T(8,128)(2,1)S(1)}, u32[]{:S(2)}, u32[]{:S(2)}) collective-permute-start(bf16[2,2,128,896]{3,2,1,0:T(8,128)(2,1)} %get-tuple-element.171), channel_id=1, source_target_pairs={{0,8},{1,9},{2,10},{3,11},{4,12},{5,13},{6,14},{7,15},{8,0},{9,1},... | collective-permute-start | bytes 2752520 | tf_op jit(solution)/shard_map/ppermute | solution.py:34
  159.4 22.3 %collective-permute-start.19 = (bf16[2,2,128,896]{3,2,1,0:T(8,128)(2,1)}, bf16[2,2,128,896]{3,2,1,0:T(8,128)(2,1)S(1)}, u32[]{:S(2)}, u32[]{:S(2)}) collective-permute-start(bf16[2,2,128,896]{3,2,1,0:T(8,128)(2,1)} %get-tuple-element.172), channel_id=1, source_target_pairs={{0,16},{1,17},{2,18},{3,19},{4,20},{5,21},{6,22},{7,23},{8,24},{9,... | collective-permute-start | bytes 2752520 | tf_op jit(solution)/shard_map/ppermute | solution.py:34
  159.9 14.4 %collective-permute-start.20 = (bf16[2,4,32,896]{3,2,1,0:T(8,128)(2,1)S(1)}, bf16[2,4,32,896]{3,2,1,0:T(8,128)(2,1)S(1)}, u32[]{:S(2)}, u32[]{:S(2)}) collective-permute-start(bf16[2,4,32,896]{3,2,1,0:T(8,128)(2,1)S(1)} %get-tuple-element.173), channel_id=1, source_target_pairs={{0,2},{1,3},{2,0},{3,1},{4,6},{5,7},{6,4},{7,5},{8,10},{9,11},{10,... | collective-permute-start | bytes 1376264 | tf_op jit(solution)/shard_map/ppermute | solution.py:34
  186.0 16.0 %collective-permute-start.21 = (bf16[2,128,896]{2,1,0:T(8,128)(2,1)}, bf16[2,128,896]{2,1,0:T(8,128)(2,1)S(1)}, u32[]{:S(2)}, u32[]{:S(2)}) collective-permute-start(bf16[2,128,896]{2,1,0:T(8,128)(2,1)} %get-tuple-element.179), channel_id=1, source_target_pairs={{0,16},{1,17},{2,18},{3,19},{4,20},{5,21},{6,22},{7,23},{8,24},{9,... | collective-permute-start | bytes 1376264 | tf_op jit(solution)/shard_map/ppermute | solution.py:34
  186.7 15.4 %collective-permute-start.22 = (bf16[2,128,896]{2,1,0:T(8,128)(2,1)}, bf16[2,128,896]{2,1,0:T(8,128)(2,1)S(1)}, u32[]{:S(2)}, u32[]{:S(2)}) collective-permute-start(bf16[2,128,896]{2,1,0:T(8,128)(2,1)} %get-tuple-element.180), channel_id=1, source_target_pairs={{0,8},{1,9},{2,10},{3,11},{4,12},{5,13},{6,14},{7,15},{8,0},{9,1},... | collective-permute-start | bytes 1376264 | tf_op jit(solution)/shard_map/ppermute | solution.py:34
  188.1 14.0 %collective-permute-start.23 = (bf16[2,2,32,896]{3,2,1,0:T(8,128)(2,1)}, bf16[2,2,32,896]{3,2,1,0:T(8,128)(2,1)S(1)}, u32[]{:S(2)}, u32[]{:S(2)}) collective-permute-start(bf16[2,2,32,896]{3,2,1,0:T(8,128)(2,1)} %get-tuple-element.181), channel_id=1, source_target_pairs={{0,4},{1,5},{2,6},{3,7},{4,0},{5,1},{6,2},{7,3},{8,12},{9,13},{10,... | collective-permute-start | bytes 688136 | tf_op jit(solution)/shard_map/ppermute | solution.py:34
  206.8 11.6 %collective-permute-start.24 = (bf16[2,128,896]{2,1,0:T(8,128)(2,1)}, bf16[2,128,896]{2,1,0:T(8,128)(2,1)S(1)}, u32[]{:S(2)}, u32[]{:S(2)}) collective-permute-start(bf16[2,128,896]{2,1,0:T(8,128)(2,1)} %get-tuple-element.185), channel_id=1, source_target_pairs={{0,2},{1,3},{2,0},{3,1},{4,6},{5,7},{6,4},{7,5},{8,10},{9,11},{10,... | collective-permute-start | bytes 1376264 | tf_op jit(solution)/shard_map/ppermute | solution.py:34
  222.6 11.7 %collective-permute-start.26 = (bf16[128,896]{1,0:T(8,128)(2,1)}, bf16[128,896]{1,0:T(8,128)(2,1)S(1)}, u32[]{:S(2)}, u32[]{:S(2)}) collective-permute-start(bf16[128,896]{1,0:T(8,128)(2,1)} %get-tuple-element.189), channel_id=1, source_target_pairs={{0,4},{1,5},{2,6},{3,7},{4,0},{5,1},{6,2},{7,3},{8,12},{9,13},{10,... | collective-permute-start | bytes 688136 | tf_op jit(solution)/shard_map/ppermute | solution.py:34
  238.2 13.3 %collective-permute-start.28 = (bf16[160,896]{1,0:T(8,128)(2,1)}, bf16[160,896]{1,0:T(8,128)(2,1)S(1)}, u32[]{:S(2)}, u32[]{:S(2)}) collective-permute-start(bf16[160,896]{1,0:T(8,128)(2,1)} %shard_map.113.refs_0_), channel_id=1, source_target_pairs={{0,8},{1,9},{2,10},{3,11},{4,12},{5,13},{6,14},{7,15},{8,0},{9,1},... | collective-permute-start | bytes 860168 | tf_op jit(solution)/shard_map/ppermute | solution.py:34
  239.4 13.3 %collective-permute-start.29 = (bf16[160,896]{1,0:T(8,128)(2,1)}, bf16[160,896]{1,0:T(8,128)(2,1)S(1)}, u32[]{:S(2)}, u32[]{:S(2)}) collective-permute-start(bf16[160,896]{1,0:T(8,128)(2,1)} %shard_map.113.refs_0_), channel_id=1, source_target_pairs={{0,16},{1,17},{2,18},{3,19},{4,20},{5,21},{6,22},{7,23},{8,24},{9,... | collective-permute-start | bytes 860168 | tf_op jit(solution)/shard_map/ppermute | solution.py:34
  240.4 13.3 %collective-permute-start.30 = (bf16[160,896]{1,0:T(8,128)(2,1)}, bf16[160,896]{1,0:T(8,128)(2,1)S(1)}, u32[]{:S(2)}, u32[]{:S(2)}) collective-permute-start(bf16[160,896]{1,0:T(8,128)(2,1)} %shard_map.113.refs_0_), channel_id=1, source_target_pairs={{0,24},{1,25},{2,26},{3,27},{4,28},{5,29},{6,30},{7,31},{8,16},{9,... | collective-permute-start | bytes 860168 | tf_op jit(solution)/shard_map/ppermute | solution.py:34
  (46 other events, 471.3 us)

commit v5 on v4

--- a/solution.py
+++ b/solution.py
@@ -692,7 +692,7 @@
             ],
         ),
         out_shape=[plane, plane, line],
-        compiler_params=kernel_params(24 if give else 60),
+        compiler_params=kernel_params(24),
     )(where, pixels, keep, got)
 
 
@@ -758,7 +758,7 @@
     )
 
 
-def sums(units):
+def sums(units, mebibytes):
     scalars, arrays, indices, buffers, outs, plan = [], [], [], [], [], []
 
     def scalar(value):
@@ -793,7 +793,7 @@
                 + [pltpu.SemaphoreType.DMA((len(arrays),)), pltpu.SemaphoreType.DMA((len(outs),))],
             ),
             out_shape=outs,
-            compiler_params=kernel_params(60),
+            compiler_params=kernel_params(mebibytes),
         )(jnp.stack([jnp.asarray(s, jnp.int32) for s in scalars]), *arrays)
     )
     return [(results.pop(0), results.pop(0) if keep else None) for _, _, keep in plan]
@@ -854,7 +854,7 @@
     while any(routes is not None for _, routes in waiting):
         units = [u for values, routes in waiting if routes is not None for u in values]
         routes = [r for _, some in waiting if some is not None for r in some]
-        ready = sums(units) if count else [(value, None) for value in units]
+        ready = sums(units, 24 if count == 1 else 60) if count else [(value, None) for value in units]
         came = [sent(give, route) for (give, _), route in zip(ready, routes)]
         if count in beside:
             ready, done = beside[count](ready, done)
@@ -906,7 +906,7 @@
             jax.ShapeDtypeStruct((shard, width), BF16),
             jax.ShapeDtypeStruct((6, shard), F32),
         ],
-        compiler_params=kernel_params(60),
+        compiler_params=kernel_params(24),
     )(seq_index.astype(jnp.int32).reshape(1), *pieces)
 
 
@@ -945,7 +945,7 @@
             scratch_shapes=buffers + [pltpu.SemaphoreType.DMA((len(arrays),))],
         ),
         out_shape=jax.ShapeDtypeStruct((height, lanes), BF16),
-        compiler_params=kernel_params(60),
+        compiler_params=kernel_params(24),
     )(jnp.stack([jnp.asarray(s, jnp.int32) for s in scalars]), *arrays)
 
 

time: 258 us -> 253 us (0.981)
  Pallas kernels: 104 us -> 99.9 us
    unnamed x79 -> x81, local copies, waits for them, and re-layouts: 14.1 us -> 14.5 us
  transfers between devices with their start and end apart: 31 -> 31, of which waited for: 14 -> 13; matrix products, arithmetic and copies ran while one was open for 5% -> 5% of each run, Pallas kernels for 18% -> 17%
where the time goes in v5:
time: 253 us; the launch traced here: 252 us
  Pallas kernels  99.9 us (39%)
  waiting for transfers between devices  73 us (29%)
  starting transfers between devices  47.2 us (19%)
  local copies, waits for them, and re-layouts  26.4 us (10%)
  other arithmetic  4.38 us (2%)
    ppermute x31, waiting for transfers between devices, sent(): return lax.ppermute(value, AXES, pairs)  73 us
    ppermute x31, starting transfers between devices, sent(): return lax.ppermute(value, AXES, pairs)  47.2 us
    pallas_call x1, Pallas kernels, layer(): pl.pallas_call(functools.partial(layer_kernel, pairs=pairs, late=late, sl...  35.2 us
    pallas_call x2, Pallas kernels, pixel_grads(): pl.pallas_call(functools.partial(pixel_kernel, chips=chips, begin=begin,...  19 us
    pallas_call x2, Pallas kernels, weight_part(): pl.pallas_call(functools.partial(weight_kernel, bits=bits, share=share, l...  14.9 us
    unnamed x81, local copies, waits for them, and re-layouts  14.5 us
    pallas_call x3, Pallas kernels, sums(): pl.pallas_call(functools.partial(sums_kernel, plan=plan, indices=indices)...  9.36 us
    pallas_call x2, Pallas kernels, scalar_call(): pl.pallas_call(kernel, grid_spec=pltpu.PrefetchScalarGridSpec(num_scalar_...  7.94 us
  transfers between devices with their start and end apart: 31, of which 13 were waited for; matrix products, arithmetic and copies ran while one was open for 5% of the time, Pallas kernels for 17%

profile of v5, /device:TPU:0, one launch (start us, length us, event | category | flops | bytes accessed | tf_op | source)
XLA Modules:
  0.0 252.2 jit_solution(9482010338778994057)
XLA Ops:
  4.8 5.0 %collective-permute-start = (bf16[448,1280]{1,0:T(8,128)(2,1)S(1)}, bf16[448,1280]{1,0:T(8,128)(2,1)S(1)}, u32[]{:S(2)}, u32[]{:S(2)}) collective-permute-start(bf16[448,1280]{1,0:T(8,128)(2,1)S(1)} %concatenate.3.refs_0_), channel_id=1, source_target_pairs={{0,2},{1,3},{2,4},{3,5},{4,6},{5,7},{8,10},{9,11},{10,12},{11,13},... | collective-permute-start | bytes 3440648 | tf_op jit(solution)/shard_map/ppermute | solution.py:34
  12.9 3.4 %shard_map.102 = (bf16[8,32,1280]{2,1,0:T(8,128)(2,1)}, bf16[8,32,1280]{2,1,0:T(8,128)(2,1)}, bf16[8,32,1280]{2,1,0:T(8,128)(2,1)}) custom-call(s32[24]{0:T(128)} %reshape.240.order_ref, f32[24]{0:T(128)} %convert_element_type.27.spot_ref, bf16[17,32,1176]{2,1,0:T(8,128)(2,1)} %bitcast.46), custom_call_target="tpu_custom_call" | custom-call | tf_op jit(solution)/shard_map/pallas_call | solution.py:106
  21.3 12.9 %collective-permute-done = bf16[448,1280]{1,0:T(8,128)(2,1)S(1)} collective-permute-done((bf16[448,1280]{1,0:T(8,128)(2,1)S(1)}, bf16[448,1280]{1,0:T(8,128)(2,1)S(1)}, u32[]{:S(2)}, u32[]{:S(2)}) %collective-permute-start) | collective-permute-done | bytes 1146912 | tf_op jit(solution)/shard_map/ppermute | solution.py:34
  34.2 4.3 %collective-permute-done.1 = bf16[448,1280]{1,0:T(8,128)(2,1)} collective-permute-done((bf16[448,1280]{1,0:T(8,128)(2,1)S(1)}, bf16[448,1280]{1,0:T(8,128)(2,1)}, u32[]{:S(2)}, u32[]{:S(2)}) %collective-permute-start.1) | collective-permute-done | bytes 1146912 | tf_op jit(solution)/shard_map/ppermute | solution.py:34
  47.6 22.0 %collective-permute-done.7.cot_low_ref = bf16[64,3584]{1,0:T(8,128)(2,1)S(1)} collective-permute-done((bf16[64,3584]{1,0:T(8,128)(2,1)S(1)}, bf16[64,3584]{1,0:T(8,128)(2,1)S(1)}, u32[]{:S(2)}, u32[]{:S(2)}) %collective-permute-start.7) | collective-permute-done | bytes 458784 | tf_op jit(solution)/shard_map/ppermute | solution.py:34
  75.2 4.5 %shard_map.103 = (bf16[560,1280]{1,0:T(8,128)(2,1)}, bf16[128,1280]{1,0:T(8,128)(2,1)}, bf16[128,1280]{1,0:T(8,128)(2,1)}) custom-call(s32[17]{0:T(128)} %add.198.pick_ref, bf16[17,32,1176]{2,1,0:T(8,128)(2,1)} %bitcast.47, bf16[8,32,1280]{2,1,0:T(8,128)(2,1)} %copy-done.34, bf16[8,32,1280]{2,1,0:T(8,128)(2,1)} %copy-done.35, bf16[8,32,1280]{2,1,0:T(8,128)(2,1)} %copy-done.36), custom_call_target="tpu_custom_call" | custom-call | tf_op jit(solution)/shard_map/pallas_call | solution.py:106
  79.7 5.7 %collective-permute-start.12 = (bf16[128,1280]{1,0:T(8,128)(2,1)}, bf16[128,1280]{1,0:T(8,128)(2,1)}, u32[]{:S(2)}, u32[]{:S(2)}) collective-permute-start(bf16[128,1280]{1,0:T(8,128)(2,1)} %get-tuple-element.146), channel_id=1, source_target_pairs={{0,8},{1,9},{2,10},{3,11},{4,12},{5,13},{6,14},{7,15},{8,16},{9,17... | collective-permute-start | bytes 983048 | tf_op jit(solution)/shard_map/ppermute | solution.py:34
  89.5 7.6 %shard_map.104 = (f32[3,560,896]{2,1,0:T(8,128)S(1)}, f32[560,128]{1,0:T(8,128)S(1)}) custom-call(s32[1]{0:T(128)} %bitcast.place_ref, bf16[560,1280]{1,0:T(8,128)(2,1)} %get-tuple-element.149.rows_ref.main_ref.first_ref, bf16[448,1280]{1,0:T(8,128)(2,1)S(1)} %concatenate.3.refs_0_, bf16[448,1280]{1,0:T(8,128)(2,1)S(1)} %copy-done.6, ...), custom_call_target="tpu_custom_call" | custom-call | tf_op jit(solution)/shard_map/pallas_call | solution.py:243
  99.6 4.2 %collective-permute-done.10 = bf16[448,1280]{1,0:T(8,128)(2,1)} collective-permute-done((bf16[448,1280]{1,0:T(8,128)(2,1)S(1)}, bf16[448,1280]{1,0:T(8,128)(2,1)}, u32[]{:S(2)}, u32[]{:S(2)}) %collective-permute-start.10) | collective-permute-done | bytes 1146912 | tf_op jit(solution)/shard_map/ppermute | solution.py:34
  109.5 35.2 %shard_map.105 = (bf16[544,3584]{1,0:T(8,128)(2,1)}, bf16[544,3584]{1,0:T(8,128)(2,1)}, bf16[560,2048]{1,0:T(8,128)(2,1)}, bf16[560,2048]{1,0:T(8,128)(2,1)}) custom-call(s32[5]{0:T(128)} %stack.51.place_ref, f32[105]{0:T(128)} %reshape.245.mask_ref, bf16[560,1280]{1,0:T(8,128)(2,1)} %get-tuple-element.149.rows_ref.main_ref.first_ref, ...), custom_call_target="tpu_custom_call" | custom-call | tf_op jit(solution)/shard_map/pallas_call | solution.py:493
  149.4 7.8 %shard_map.108 = (bf16[2,2,128,896]{3,2,1,0:T(8,128)(2,1)}, bf16[2,2,128,896]{3,2,1,0:T(8,128)(2,1)}, bf16[2,4,32,896]{3,2,1,0:T(8,128)(2,1)}) custom-call(s32[2]{0:T(128)S(1)} %pad_add_fusion.where_ref, bf16[1280,1152]{1,0:T(8,128)(2,1)S(1)} %shard_map.106.pixels_ref, bf16[560,2048]{1,0:T(8,128)(2,1)S(1)} %copy-done.13, ...), custom_call_target="tpu_custom_call" | custom-call | tf_op jit(solution)/shard_map/pallas_call | solution.py:677
  160.3 3.9 %collective-permute-start.20 = (bf16[2,4,32,896]{3,2,1,0:T(8,128)(2,1)}, bf16[2,4,32,896]{3,2,1,0:T(8,128)(2,1)S(1)}, u32[]{:S(2)}, u32[]{:S(2)}) collective-permute-start(bf16[2,4,32,896]{3,2,1,0:T(8,128)(2,1)} %get-tuple-element.173), channel_id=1, source_target_pairs={{0,2},{1,3},{2,0},{3,1},{4,6},{5,7},{6,4},{7,5},{8,10},{9,11},{10,... | collective-permute-start | bytes 1376264 | tf_op jit(solution)/shard_map/ppermute | solution.py:34
  167.5 7.1 %shard_map.107 = (f32[2,2,128,896]{3,2,1,0:T(8,128)S(1)}, f32[2,2,128,896]{3,2,1,0:T(8,128)S(1)}, f32[2,4,32,896]{3,2,1,0:T(8,128)S(1)}) custom-call(s32[2]{0:T(128)S(1)} %pad_add_fusion.where_ref, bf16[1280,1152]{1,0:T(8,128)(2,1)S(1)} %shard_map.106.pixels_ref, bf16[560,2048]{1,0:T(8,128)(2,1)S(1)} %copy-done.14, bf16[560,2048]{1,0:T(8,128)(2,1)S(1)} %copy-done.16), custom_call_target="tpu_custom_call" | custom-call | tf_op jit(solution)/shard_map/pallas_call | solution.py:677
  174.9 5.8 %collective-permute-done.18.refs_1_ = bf16[2,2,128,896]{3,2,1,0:T(8,128)(2,1)} collective-permute-done((bf16[2,2,128,896]{3,2,1,0:T(8,128)(2,1)}, bf16[2,2,128,896]{3,2,1,0:T(8,128)(2,1)}, u32[]{:S(2)}, u32[]{:S(2)}) %collective-permute-start.18) | collective-permute-done | bytes 917536 | tf_op jit(solution)/shard_map/ppermute | solution.py:34
  182.2 2.9 %shard_map.109 = (bf16[2,128,896]{2,1,0:T(8,128)(2,1)S(1)}, bf16[2,128,896]{2,1,0:T(8,128)(2,1)S(1)}, bf16[2,2,32,896]{3,2,1,0:T(8,128)(2,1)S(1)}) custom-call(s32[6]{0:T(128)S(1)} %stack.132.at_ref, f32[2,2,128,896]{3,2,1,0:T(8,128)S(1)} %get-tuple-element.170.refs_0_, bf16[2,2,128,896]{3,2,1,0:T(8,128)(2,1)} %collective-permute-done.18.refs_1_, ...), custom_call_target="tpu_custom_call" | custom-call | tf_op jit(solution)/shard_map/pallas_call | solution.py:784
  187.2 4.0 %collective-permute-start.23 = (bf16[2,2,32,896]{3,2,1,0:T(8,128)(2,1)S(1)}, bf16[2,2,32,896]{3,2,1,0:T(8,128)(2,1)S(1)}, u32[]{:S(2)}, u32[]{:S(2)}) collective-permute-start(bf16[2,2,32,896]{3,2,1,0:T(8,128)(2,1)S(1)} %get-tuple-element.181), channel_id=1, source_target_pairs={{0,4},{1,5},{2,6},{3,7},{4,0},{5,1},{6,2},{7,3},{8,12},{9,13},{10,... | collective-permute-start | bytes 688136 | tf_op jit(solution)/shard_map/ppermute | solution.py:34
  191.8 8.9 %collective-permute-done.23.refs_8_.refs_10_.refs_4_ = bf16[2,2,32,896]{3,2,1,0:T(8,128)(2,1)S(1)} collective-permute-done((bf16[2,2,32,896]{3,2,1,0:T(8,128)(2,1)S(1)}, bf16[2,2,32,896]{3,2,1,0:T(8,128)(2,1)S(1)}, u32[]{:S(2)}, u32[]{:S(2)}) %collective-permute-start.23) | collective-permute-done | bytes 229408 | tf_op jit(solution)/shard_map/ppermute | solution.py:34
  202.3 3.1 %shard_map.110 = (bf16[2,128,896]{2,1,0:T(8,128)(2,1)}, bf16[2,32,896]{2,1,0:T(8,128)(2,1)}) custom-call(s32[15]{0:T(128)} %stack.134.at_ref, f32[2,2,128,896]{3,2,1,0:T(8,128)} %copy-done.9, bf16[2,2,128,896]{3,2,1,0:T(8,128)(2,1)} %collective-permute-done.18.refs_1_, bf16[2,128,896]{2,1,0:T(8,128)(2,1)} %copy-done.31, f32[2,2,128,896]{3,2,1,0:T(8,128)} %copy-done.10, ...), custom_call_target="tpu_custom_call" | custom-call | tf_op jit(solution)/shard_map/pallas_call | solution.py:784
  207.8 2.9 %collective-permute-done.25.refs_11_.refs_5_ = bf16[2,32,896]{2,1,0:T(8,128)(2,1)S(1)} collective-permute-done((bf16[2,32,896]{2,1,0:T(8,128)(2,1)}, bf16[2,32,896]{2,1,0:T(8,128)(2,1)S(1)}, u32[]{:S(2)}, u32[]{:S(2)}) %collective-permute-start.25) | collective-permute-done | bytes 114720 | tf_op jit(solution)/shard_map/ppermute | solution.py:34
  210.8 6.2 %collective-permute-done.24.refs_3_.refs_7_ = bf16[2,128,896]{2,1,0:T(8,128)(2,1)S(1)} collective-permute-done((bf16[2,128,896]{2,1,0:T(8,128)(2,1)}, bf16[2,128,896]{2,1,0:T(8,128)(2,1)S(1)}, u32[]{:S(2)}, u32[]{:S(2)}) %collective-permute-start.24) | collective-permute-done | bytes 458784 | tf_op jit(solution)/shard_map/ppermute | solution.py:34
  217.7 3.3 %shard_map.111 = (bf16[128,896]{1,0:T(8,128)(2,1)}, f32[128,896]{1,0:T(8,128)}, bf16[32,896]{1,0:T(8,128)(2,1)}) custom-call(s32[22]{0:T(128)} %stack.61.at_ref, f32[2,2,128,896]{3,2,1,0:T(8,128)} %copy-done.9, bf16[2,2,128,896]{3,2,1,0:T(8,128)(2,1)} %collective-permute-done.18.refs_1_, bf16[2,128,896]{2,1,0:T(8,128)(2,1)} %copy-done.31, ...), custom_call_target="tpu_custom_call" | custom-call | tf_op jit(solution)/shard_map/pallas_call | solution.py:784
  223.0 9.3 %shard_map.112.refs_8_ = bf16[544,640]{1,0:T(8,128)(2,1)} custom-call(s32[5]{0:T(128)} %stack.51.place_ref, bf16[544,3584]{1,0:T(8,128)(2,1)} %get-tuple-element.197.d_stem_ref, bf16[448,1280]{1,0:T(8,128)(2,1)} %copy-done.2, bf16[448,1280]{1,0:T(8,128)(2,1)} %copy-done.5, bf16[448,1280]{1,0:T(8,128)(2,1)} %copy-done.3, bf16[448,1280]{1,0:T(8,128)(2,1)} %copy-done.7, ...), custom_call_target="tpu_custom_call" | custom-call | tf_op jit(solution)/shard_map/pallas_call | solution.py:555
  238.0 9.7 %shard_map.114 = bf16[544,1176]{1,0:T(8,128)(2,1)} custom-call(s32[5]{0:T(128)} %stack.51.place_ref, bf16[544,3584]{1,0:T(8,128)(2,1)} %get-tuple-element.197.d_stem_ref, bf16[448,1280]{1,0:T(8,128)(2,1)} %copy-done.2, bf16[448,1280]{1,0:T(8,128)(2,1)} %copy-done.5, bf16[448,1280]{1,0:T(8,128)(2,1)} %copy-done.3, bf16[448,1280]{1,0:T(8,128)(2,1)} %copy-done.7, ...), custom_call_target="tpu_custom_call" | custom-call | tf_op jit(solution)/shard_map/pallas_call | solution.py:555
  247.7 2.9 %collective-permute-done.29.refs_2_ = bf16[160,896]{1,0:T(8,128)(2,1)S(1)} collective-permute-done((bf16[160,896]{1,0:T(8,128)(2,1)S(1)}, bf16[160,896]{1,0:T(8,128)(2,1)S(1)}, u32[]{:S(2)}, u32[]{:S(2)}) %collective-permute-start.29) | collective-permute-done | bytes 286752 | tf_op jit(solution)/shard_map/ppermute | solution.py:34
  (177 shorter events, 68.3 us)
Async XLA Ops:
  4.8 29.4 %collective-permute-start = (bf16[448,1280]{1,0:T(8,128)(2,1)S(1)}, bf16[448,1280]{1,0:T(8,128)(2,1)S(1)}, u32[]{:S(2)}, u32[]{:S(2)}) collective-permute-start(bf16[448,1280]{1,0:T(8,128)(2,1)S(1)} %concatenate.3.refs_0_), channel_id=1, source_target_pairs={{0,2},{1,3},{2,4},{3,5},{4,6},{5,7},{8,10},{9,11},{10,12},{11,13},... | collective-permute-start | bytes 3440648 | tf_op jit(solution)/shard_map/ppermute | solution.py:34
  9.8 28.7 %collective-permute-start.1 = (bf16[448,1280]{1,0:T(8,128)(2,1)S(1)}, bf16[448,1280]{1,0:T(8,128)(2,1)}, u32[]{:S(2)}, u32[]{:S(2)}) collective-permute-start(bf16[448,1280]{1,0:T(8,128)(2,1)S(1)} %concatenate.3.refs_0_), channel_id=1, source_target_pairs={{2,0},{3,1},{4,2},{5,3},{6,4},{7,5},{10,8},{11,9},{12,10},{13,11},... | collective-permute-start | bytes 3440648 | tf_op jit(solution)/shard_map/ppermute | solution.py:34
  16.3 22.2 %collective-permute-start.3 = (bf16[8,32,1280]{2,1,0:T(8,128)(2,1)}, bf16[8,32,1280]{2,1,0:T(8,128)(2,1)S(1)}, u32[]{:S(2)}, u32[]{:S(2)}) collective-permute-start(bf16[8,32,1280]{2,1,0:T(8,128)(2,1)} %get-tuple-element.110), channel_id=1, source_target_pairs={{0,8},{1,9},{2,10},{3,11},{4,12},{5,13},{6,14},{7,15},{8,0},{9,1},... | collective-permute-start | bytes 1966088 | tf_op jit(solution)/shard_map/ppermute | solution.py:34
  17.8 20.7 %collective-permute-start.4 = (bf16[8,32,1280]{2,1,0:T(8,128)(2,1)}, bf16[8,32,1280]{2,1,0:T(8,128)(2,1)S(1)}, u32[]{:S(2)}, u32[]{:S(2)}) collective-permute-start(bf16[8,32,1280]{2,1,0:T(8,128)(2,1)} %get-tuple-element.111), channel_id=1, source_target_pairs={{0,16},{1,17},{2,18},{3,19},{4,20},{5,21},{6,22},{7,23},{8,24},{9,... | collective-permute-start | bytes 1966088 | tf_op jit(solution)/shard_map/ppermute | solution.py:34
  38.9 30.7 %collective-permute-start.5 = (bf16[448,1280]{1,0:T(8,128)(2,1)S(1)}, bf16[448,1280]{1,0:T(8,128)(2,1)S(1)}, u32[]{:S(2)}, u32[]{:S(2)}) collective-permute-start(bf16[448,1280]{1,0:T(8,128)(2,1)S(1)} %collective-permute-done), channel_id=1, source_target_pairs={{2,4},{3,5},{4,6},{5,7},{10,12},{11,13},{12,14},{13,15},{18,20},{1... | collective-permute-start | bytes 3440648 | tf_op jit(solution)/shard_map/ppermute | solution.py:34
  39.8 30.2 %collective-permute-start.6 = (bf16[448,1280]{1,0:T(8,128)(2,1)}, bf16[448,1280]{1,0:T(8,128)(2,1)S(1)}, u32[]{:S(2)}, u32[]{:S(2)}) collective-permute-start(bf16[448,1280]{1,0:T(8,128)(2,1)} %collective-permute-done.1), channel_id=1, source_target_pairs={{2,0},{3,1},{4,2},{5,3},{10,8},{11,9},{12,10},{13,11},{18,16},{19,... | collective-permute-start | bytes 3440648 | tf_op jit(solution)/shard_map/ppermute | solution.py:34
  42.6 27.8 %collective-permute-start.9 = (bf16[448,1280]{1,0:T(8,128)(2,1)S(1)}, bf16[448,1280]{1,0:T(8,128)(2,1)S(1)}, u32[]{:S(2)}, u32[]{:S(2)}) collective-permute-start(bf16[448,1280]{1,0:T(8,128)(2,1)S(1)} %broadcast_select_fusion.1.refs_2_), channel_id=1, source_target_pairs={{0,1},{1,0},{2,3},{3,2},{4,5},{5,4},{6,7},{7,6},{8,9},{9,8},{10,11... | collective-permute-start | bytes 3440648 | tf_op jit(solution)/shard_map/ppermute | solution.py:34
  42.7 26.9 %collective-permute-start.8 = (bf16[8,32,1280]{2,1,0:T(8,128)(2,1)S(1)}, bf16[8,32,1280]{2,1,0:T(8,128)(2,1)S(1)}, u32[]{:S(2)}, u32[]{:S(2)}) collective-permute-start(bf16[8,32,1280]{2,1,0:T(8,128)(2,1)S(1)} %copy-done.39), channel_id=1, source_target_pairs={{0,24},{1,25},{2,26},{3,27},{4,28},{5,29},{6,30},{7,31},{8,16},{9,... | collective-permute-start | bytes 1966088 | tf_op jit(solution)/shard_map/ppermute | solution.py:34
  45.2 24.4 %collective-permute-start.7 = (bf16[64,3584]{1,0:T(8,128)(2,1)S(1)}, bf16[64,3584]{1,0:T(8,128)(2,1)S(1)}, u32[]{:S(2)}, u32[]{:S(2)}) collective-permute-start(bf16[64,3584]{1,0:T(8,128)(2,1)S(1)} %get-tuple-element.120), channel_id=1, source_target_pairs={{0,8},{1,9},{2,10},{3,11},{4,12},{5,13},{6,14},{7,15},{8,16},{9,17... | collective-permute-start | bytes 1376264 | tf_op jit(solution)/shard_map/ppermute | solution.py:34
  71.6 32.2 %collective-permute-start.10 = (bf16[448,1280]{1,0:T(8,128)(2,1)S(1)}, bf16[448,1280]{1,0:T(8,128)(2,1)}, u32[]{:S(2)}, u32[]{:S(2)}) collective-permute-start(bf16[448,1280]{1,0:T(8,128)(2,1)S(1)} %broadcast_select_fusion.refs_4_), channel_id=1, source_target_pairs={{2,0},{3,1},{4,6},{5,7},{10,8},{11,9},{12,14},{13,15},{18,16},{19,... | collective-permute-start | bytes 3440648 | tf_op jit(solution)/shard_map/ppermute | solution.py:34
  72.9 26.7 %collective-permute-start.14 = (bf16[64,3584]{1,0:T(8,128)(2,1)}, bf16[64,3584]{1,0:T(8,128)(2,1)}, u32[]{:S(2)}, u32[]{:S(2)}) collective-permute-start(bf16[64,3584]{1,0:T(8,128)(2,1)} %get-tuple-element.148), channel_id=1, source_target_pairs={{8,0},{9,1},{10,2},{11,3},{12,4},{13,5},{14,6},{15,7},{16,8},{17,9... | collective-permute-start | bytes 1376264 | tf_op jit(solution)/shard_map/ppermute | solution.py:34
  79.7 24.2 %collective-permute-start.12 = (bf16[128,1280]{1,0:T(8,128)(2,1)}, bf16[128,1280]{1,0:T(8,128)(2,1)}, u32[]{:S(2)}, u32[]{:S(2)}) collective-permute-start(bf16[128,1280]{1,0:T(8,128)(2,1)} %get-tuple-element.146), channel_id=1, source_target_pairs={{0,8},{1,9},{2,10},{3,11},{4,12},{5,13},{6,14},{7,15},{8,16},{9,17... | collective-permute-start | bytes 983048 | tf_op jit(solution)/shard_map/ppermute | solution.py:34
  85.4 18.4 %collective-permute-start.13 = (bf16[128,1280]{1,0:T(8,128)(2,1)}, bf16[128,1280]{1,0:T(8,128)(2,1)}, u32[]{:S(2)}, u32[]{:S(2)}) collective-permute-start(bf16[128,1280]{1,0:T(8,128)(2,1)} %get-tuple-element.147), channel_id=1, source_target_pairs={{8,0},{9,1},{10,2},{11,3},{12,4},{13,5},{14,6},{15,7},{16,8},{17,9... | collective-permute-start | bytes 983048 | tf_op jit(solution)/shard_map/ppermute | solution.py:34
  157.2 23.5 %collective-permute-start.18 = (bf16[2,2,128,896]{3,2,1,0:T(8,128)(2,1)}, bf16[2,2,128,896]{3,2,1,0:T(8,128)(2,1)}, u32[]{:S(2)}, u32[]{:S(2)}) collective-permute-start(bf16[2,2,128,896]{3,2,1,0:T(8,128)(2,1)} %get-tuple-element.171), channel_id=1, source_target_pairs={{0,8},{1,9},{2,10},{3,11},{4,12},{5,13},{6,14},{7,15},{8,0},{9,1},... | collective-permute-start | bytes 2752520 | tf_op jit(solution)/shard_map/ppermute | solution.py:34
  159.8 22.4 %collective-permute-start.19 = (bf16[2,2,128,896]{3,2,1,0:T(8,128)(2,1)}, bf16[2,2,128,896]{3,2,1,0:T(8,128)(2,1)}, u32[]{:S(2)}, u32[]{:S(2)}) collective-permute-start(bf16[2,2,128,896]{3,2,1,0:T(8,128)(2,1)} %get-tuple-element.172), channel_id=1, source_target_pairs={{0,16},{1,17},{2,18},{3,19},{4,20},{5,21},{6,22},{7,23},{8,24},{9,... | collective-permute-start | bytes 2752520 | tf_op jit(solution)/shard_map/ppermute | solution.py:34
  160.3 14.6 %collective-permute-start.20 = (bf16[2,4,32,896]{3,2,1,0:T(8,128)(2,1)}, bf16[2,4,32,896]{3,2,1,0:T(8,128)(2,1)S(1)}, u32[]{:S(2)}, u32[]{:S(2)}) collective-permute-start(bf16[2,4,32,896]{3,2,1,0:T(8,128)(2,1)} %get-tuple-element.173), channel_id=1, source_target_pairs={{0,2},{1,3},{2,0},{3,1},{4,6},{5,7},{6,4},{7,5},{8,10},{9,11},{10,... | collective-permute-start | bytes 1376264 | tf_op jit(solution)/shard_map/ppermute | solution.py:34
  185.2 15.5 %collective-permute-start.21 = (bf16[2,128,896]{2,1,0:T(8,128)(2,1)S(1)}, bf16[2,128,896]{2,1,0:T(8,128)(2,1)S(1)}, u32[]{:S(2)}, u32[]{:S(2)}) collective-permute-start(bf16[2,128,896]{2,1,0:T(8,128)(2,1)S(1)} %get-tuple-element.179), channel_id=1, source_target_pairs={{0,16},{1,17},{2,18},{3,19},{4,20},{5,21},{6,22},{7,23},{8,24},{9,... | collective-permute-start | bytes 1376264 | tf_op jit(solution)/shard_map/ppermute | solution.py:34
  185.7 15.0 %collective-permute-start.22 = (bf16[2,128,896]{2,1,0:T(8,128)(2,1)S(1)}, bf16[2,128,896]{2,1,0:T(8,128)(2,1)S(1)}, u32[]{:S(2)}, u32[]{:S(2)}) collective-permute-start(bf16[2,128,896]{2,1,0:T(8,128)(2,1)S(1)} %get-tuple-element.180), channel_id=1, source_target_pairs={{0,8},{1,9},{2,10},{3,11},{4,12},{5,13},{6,14},{7,15},{8,0},{9,1},... | collective-permute-start | bytes 1376264 | tf_op jit(solution)/shard_map/ppermute | solution.py:34
  187.2 13.5 %collective-permute-start.23 = (bf16[2,2,32,896]{3,2,1,0:T(8,128)(2,1)S(1)}, bf16[2,2,32,896]{3,2,1,0:T(8,128)(2,1)S(1)}, u32[]{:S(2)}, u32[]{:S(2)}) collective-permute-start(bf16[2,2,32,896]{3,2,1,0:T(8,128)(2,1)S(1)} %get-tuple-element.181), channel_id=1, source_target_pairs={{0,4},{1,5},{2,6},{3,7},{4,0},{5,1},{6,2},{7,3},{8,12},{9,13},{10,... | collective-permute-start | bytes 688136 | tf_op jit(solution)/shard_map/ppermute | solution.py:34
  205.4 11.5 %collective-permute-start.24 = (bf16[2,128,896]{2,1,0:T(8,128)(2,1)}, bf16[2,128,896]{2,1,0:T(8,128)(2,1)S(1)}, u32[]{:S(2)}, u32[]{:S(2)}) collective-permute-start(bf16[2,128,896]{2,1,0:T(8,128)(2,1)} %get-tuple-element.185), channel_id=1, source_target_pairs={{0,2},{1,3},{2,0},{3,1},{4,6},{5,7},{6,4},{7,5},{8,10},{9,11},{10,... | collective-permute-start | bytes 1376264 | tf_op jit(solution)/shard_map/ppermute | solution.py:34
  221.1 11.2 %collective-permute-start.26 = (bf16[128,896]{1,0:T(8,128)(2,1)}, bf16[128,896]{1,0:T(8,128)(2,1)S(1)}, u32[]{:S(2)}, u32[]{:S(2)}) collective-permute-start(bf16[128,896]{1,0:T(8,128)(2,1)} %get-tuple-element.189), channel_id=1, source_target_pairs={{0,4},{1,5},{2,6},{3,7},{4,0},{5,1},{6,2},{7,3},{8,12},{9,13},{10,... | collective-permute-start | bytes 688136 | tf_op jit(solution)/shard_map/ppermute | solution.py:34
  234.4 13.2 %collective-permute-start.28 = (bf16[160,896]{1,0:T(8,128)(2,1)S(1)}, bf16[160,896]{1,0:T(8,128)(2,1)S(1)}, u32[]{:S(2)}, u32[]{:S(2)}) collective-permute-start(bf16[160,896]{1,0:T(8,128)(2,1)S(1)} %shard_map.113.refs_0_), channel_id=1, source_target_pairs={{0,8},{1,9},{2,10},{3,11},{4,12},{5,13},{6,14},{7,15},{8,0},{9,1},... | collective-permute-start | bytes 860168 | tf_op jit(solution)/shard_map/ppermute | solution.py:34
  236.3 14.3 %collective-permute-start.29 = (bf16[160,896]{1,0:T(8,128)(2,1)S(1)}, bf16[160,896]{1,0:T(8,128)(2,1)S(1)}, u32[]{:S(2)}, u32[]{:S(2)}) collective-permute-start(bf16[160,896]{1,0:T(8,128)(2,1)S(1)} %shard_map.113.refs_0_), channel_id=1, source_target_pairs={{0,16},{1,17},{2,18},{3,19},{4,20},{5,21},{6,22},{7,23},{8,24},{9,... | collective-permute-start | bytes 860168 | tf_op jit(solution)/shard_map/ppermute | solution.py:34
  237.7 12.9 %collective-permute-start.30 = (bf16[160,896]{1,0:T(8,128)(2,1)S(1)}, bf16[160,896]{1,0:T(8,128)(2,1)S(1)}, u32[]{:S(2)}, u32[]{:S(2)}) collective-permute-start(bf16[160,896]{1,0:T(8,128)(2,1)S(1)} %shard_map.113.refs_0_), channel_id=1, source_target_pairs={{0,24},{1,25},{2,26},{3,27},{4,28},{5,29},{6,30},{7,31},{8,16},{9,... | collective-permute-start | bytes 860168 | tf_op jit(solution)/shard_map/ppermute | solution.py:34
  (47 other events, 534.5 us)

commit v6 on v5

--- a/solution.py
+++ b/solution.py
@@ -660,10 +660,10 @@
             fill(outs[g].at[z], value, half, share)
     for copy in arrive[chips]:
         copy.wait()
-    mine = chip % 2
+    mine = chip // (chips // 2)
     wanted = 1 - mine if give else mine
     for i in range(chips // 2):
-        columns = pl.ds(pl.multiple_of((2 * i + wanted) * room, LANES), room)
+        columns = pl.ds(pl.multiple_of((wanted * (chips // 2) + i) * room, LANES), room)
         value = jnp.dot(line[...], d_stem[:, columns], preferred_element_type=F32)
         fill(outs[2].at[i], value, seq_size, line_share)
 
@@ -1112,7 +1112,7 @@
             gives[2:],
             keeps[2:],
             chip_labels[::-1] + seq_labels[::-1],
-            [chip_labels + seq_labels],
+            [chip_labels[::-1] + seq_labels],
             mine,
         ),
     ]

time: 253 us -> 250 us (0.988)
  starting transfers between devices: 47.2 us -> 43.8 us
    ppermute x31, starting transfers between devices: 47.2 us -> 43.8 us  [sent(): return lax.ppermute(value, AXES, pairs)]
  transfers between devices with their start and end apart: 31 -> 31, of which waited for: 13 -> 13; matrix products, arithmetic and copies ran while one was open for 5% -> 5% of each run, Pallas kernels for 17% -> 18%
where the time goes in v6:
time: 250 us; the launch traced here: 249 us
  Pallas kernels  99.9 us (40%)
  waiting for transfers between devices  74.1 us (30%)
  starting transfers between devices  43.8 us (18%)
  local copies, waits for them, and re-layouts  25.5 us (10%)
  other arithmetic  4.38 us (2%)
    ppermute x31, waiting for transfers between devices, sent(): return lax.ppermute(value, AXES, pairs)  74.1 us
    ppermute x31, starting transfers between devices, sent(): return lax.ppermute(value, AXES, pairs)  43.8 us
    pallas_call x1, Pallas kernels, layer(): pl.pallas_call(functools.partial(layer_kernel, pairs=pairs, late=late, sl...  35.2 us
    pallas_call x2, Pallas kernels, pixel_grads(): pl.pallas_call(functools.partial(pixel_kernel, chips=chips, begin=begin,...  19 us
    pallas_call x2, Pallas kernels, weight_part(): pl.pallas_call(functools.partial(weight_kernel, bits=bits, share=share, l...  14.9 us
    unnamed x81, local copies, waits for them, and re-layouts  13.6 us
    pallas_call x3, Pallas kernels, sums(): pl.pallas_call(functools.partial(sums_kernel, plan=plan, indices=indices)...  9.33 us
    pallas_call x2, Pallas kernels, scalar_call(): pl.pallas_call(kernel, grid_spec=pltpu.PrefetchScalarGridSpec(num_scalar_...  7.94 us
  transfers between devices with their start and end apart: 31, of which 13 were waited for; matrix products, arithmetic and copies ran while one was open for 5% of the time, Pallas kernels for 18%

profile of v6, /device:TPU:0, one launch (start us, length us, event | category | flops | bytes accessed | tf_op | source)
XLA Modules:
  0.0 249.1 jit_solution(7777021997730621743)
XLA Ops:
  4.8 5.0 %collective-permute-start = (bf16[448,1280]{1,0:T(8,128)(2,1)S(1)}, bf16[448,1280]{1,0:T(8,128)(2,1)S(1)}, u32[]{:S(2)}, u32[]{:S(2)}) collective-permute-start(bf16[448,1280]{1,0:T(8,128)(2,1)S(1)} %concatenate.3.refs_0_), channel_id=1, source_target_pairs={{0,2},{1,3},{2,4},{3,5},{4,6},{5,7},{8,10},{9,11},{10,12},{11,13},... | collective-permute-start | bytes 3440648 | tf_op jit(solution)/shard_map/ppermute | solution.py:34
  12.9 3.4 %shard_map.102 = (bf16[8,32,1280]{2,1,0:T(8,128)(2,1)}, bf16[8,32,1280]{2,1,0:T(8,128)(2,1)}, bf16[8,32,1280]{2,1,0:T(8,128)(2,1)}) custom-call(s32[24]{0:T(128)} %reshape.240.order_ref, f32[24]{0:T(128)} %convert_element_type.27.spot_ref, bf16[17,32,1176]{2,1,0:T(8,128)(2,1)} %bitcast.45), custom_call_target="tpu_custom_call" | custom-call | tf_op jit(solution)/shard_map/pallas_call | solution.py:106
  21.3 12.9 %collective-permute-done = bf16[448,1280]{1,0:T(8,128)(2,1)S(1)} collective-permute-done((bf16[448,1280]{1,0:T(8,128)(2,1)S(1)}, bf16[448,1280]{1,0:T(8,128)(2,1)S(1)}, u32[]{:S(2)}, u32[]{:S(2)}) %collective-permute-start) | collective-permute-done | bytes 1146912 | tf_op jit(solution)/shard_map/ppermute | solution.py:34
  34.2 4.3 %collective-permute-done.1 = bf16[448,1280]{1,0:T(8,128)(2,1)} collective-permute-done((bf16[448,1280]{1,0:T(8,128)(2,1)S(1)}, bf16[448,1280]{1,0:T(8,128)(2,1)}, u32[]{:S(2)}, u32[]{:S(2)}) %collective-permute-start.1) | collective-permute-done | bytes 1146912 | tf_op jit(solution)/shard_map/ppermute | solution.py:34
  47.6 22.0 %collective-permute-done.7.cot_low_ref = bf16[64,3584]{1,0:T(8,128)(2,1)S(1)} collective-permute-done((bf16[64,3584]{1,0:T(8,128)(2,1)S(1)}, bf16[64,3584]{1,0:T(8,128)(2,1)S(1)}, u32[]{:S(2)}, u32[]{:S(2)}) %collective-permute-start.7) | collective-permute-done | bytes 458784 | tf_op jit(solution)/shard_map/ppermute | solution.py:34
  75.2 4.5 %shard_map.103 = (bf16[560,1280]{1,0:T(8,128)(2,1)}, bf16[128,1280]{1,0:T(8,128)(2,1)}, bf16[128,1280]{1,0:T(8,128)(2,1)}) custom-call(s32[17]{0:T(128)} %add.198.pick_ref, bf16[17,32,1176]{2,1,0:T(8,128)(2,1)} %bitcast.46, bf16[8,32,1280]{2,1,0:T(8,128)(2,1)} %copy-done.34, bf16[8,32,1280]{2,1,0:T(8,128)(2,1)} %copy-done.35, bf16[8,32,1280]{2,1,0:T(8,128)(2,1)} %copy-done.36), custom_call_target="tpu_custom_call" | custom-call | tf_op jit(solution)/shard_map/pallas_call | solution.py:106
  79.7 5.7 %collective-permute-start.12 = (bf16[128,1280]{1,0:T(8,128)(2,1)}, bf16[128,1280]{1,0:T(8,128)(2,1)}, u32[]{:S(2)}, u32[]{:S(2)}) collective-permute-start(bf16[128,1280]{1,0:T(8,128)(2,1)} %get-tuple-element.146), channel_id=1, source_target_pairs={{0,8},{1,9},{2,10},{3,11},{4,12},{5,13},{6,14},{7,15},{8,16},{9,17... | collective-permute-start | bytes 983048 | tf_op jit(solution)/shard_map/ppermute | solution.py:34
  89.5 7.6 %shard_map.104 = (f32[3,560,896]{2,1,0:T(8,128)S(1)}, f32[560,128]{1,0:T(8,128)S(1)}) custom-call(s32[1]{0:T(128)} %bitcast.place_ref, bf16[560,1280]{1,0:T(8,128)(2,1)} %get-tuple-element.149.rows_ref.main_ref.first_ref, bf16[448,1280]{1,0:T(8,128)(2,1)S(1)} %concatenate.3.refs_0_, bf16[448,1280]{1,0:T(8,128)(2,1)S(1)} %copy-done.6, ...), custom_call_target="tpu_custom_call" | custom-call | tf_op jit(solution)/shard_map/pallas_call | solution.py:243
  97.0 2.6 %copy-done.19 = f32[3,560,896]{2,1,0:T(8,128)} copy-done((f32[3,560,896]{2,1,0:T(8,128)}, f32[3,560,896]{2,1,0:T(8,128)S(1)}, u32[]{:S(2)}) %copy-start.19) | copy-done | bytes 6021144
  99.6 4.2 %collective-permute-done.10 = bf16[448,1280]{1,0:T(8,128)(2,1)} collective-permute-done((bf16[448,1280]{1,0:T(8,128)(2,1)S(1)}, bf16[448,1280]{1,0:T(8,128)(2,1)}, u32[]{:S(2)}, u32[]{:S(2)}) %collective-permute-start.10) | collective-permute-done | bytes 1146912 | tf_op jit(solution)/shard_map/ppermute | solution.py:34
  109.5 35.2 %shard_map.105 = (bf16[544,3584]{1,0:T(8,128)(2,1)}, bf16[544,3584]{1,0:T(8,128)(2,1)}, bf16[560,2048]{1,0:T(8,128)(2,1)}, bf16[560,2048]{1,0:T(8,128)(2,1)}) custom-call(s32[5]{0:T(128)} %stack.49.place_ref, f32[105]{0:T(128)} %reshape.245.mask_ref, bf16[560,1280]{1,0:T(8,128)(2,1)} %get-tuple-element.149.rows_ref.main_ref.first_ref, ...), custom_call_target="tpu_custom_call" | custom-call | tf_op jit(solution)/shard_map/pallas_call | solution.py:493
  149.4 7.8 %shard_map.108 = (bf16[2,2,128,896]{3,2,1,0:T(8,128)(2,1)}, bf16[2,2,128,896]{3,2,1,0:T(8,128)(2,1)}, bf16[2,4,32,896]{3,2,1,0:T(8,128)(2,1)}) custom-call(s32[2]{0:T(128)S(1)} %pad_add_fusion.where_ref, bf16[1280,1152]{1,0:T(8,128)(2,1)S(1)} %shard_map.106.pixels_ref, bf16[560,2048]{1,0:T(8,128)(2,1)S(1)} %copy-done.13, ...), custom_call_target="tpu_custom_call" | custom-call | tf_op jit(solution)/shard_map/pallas_call | solution.py:677
  160.3 4.8 %collective-permute-start.20 = (bf16[2,4,32,896]{3,2,1,0:T(8,128)(2,1)}, bf16[2,4,32,896]{3,2,1,0:T(8,128)(2,1)S(1)}, u32[]{:S(2)}, u32[]{:S(2)}) collective-permute-start(bf16[2,4,32,896]{3,2,1,0:T(8,128)(2,1)} %get-tuple-element.173), channel_id=1, source_target_pairs={{0,4},{1,5},{2,6},{3,7},{4,0},{5,1},{6,2},{7,3},{8,12},{9,13},{10,... | collective-permute-start | bytes 1376264 | tf_op jit(solution)/shard_map/ppermute | solution.py:34
  168.5 7.1 %shard_map.107 = (f32[2,2,128,896]{3,2,1,0:T(8,128)S(1)}, f32[2,2,128,896]{3,2,1,0:T(8,128)S(1)}, f32[2,4,32,896]{3,2,1,0:T(8,128)S(1)}) custom-call(s32[2]{0:T(128)S(1)} %pad_add_fusion.where_ref, bf16[1280,1152]{1,0:T(8,128)(2,1)S(1)} %shard_map.106.pixels_ref, bf16[560,2048]{1,0:T(8,128)(2,1)S(1)} %copy-done.14, bf16[560,2048]{1,0:T(8,128)(2,1)S(1)} %copy-done.16), custom_call_target="tpu_custom_call" | custom-call | tf_op jit(solution)/shard_map/pallas_call | solution.py:677
  175.7 10.0 %collective-permute-done.20 = bf16[2,4,32,896]{3,2,1,0:T(8,128)(2,1)S(1)} collective-permute-done((bf16[2,4,32,896]{3,2,1,0:T(8,128)(2,1)}, bf16[2,4,32,896]{3,2,1,0:T(8,128)(2,1)S(1)}, u32[]{:S(2)}, u32[]{:S(2)}) %collective-permute-start.20) | collective-permute-done | bytes 458784 | tf_op jit(solution)/shard_map/ppermute | solution.py:34
  185.7 2.9 %shard_map.109 = (bf16[2,128,896]{2,1,0:T(8,128)(2,1)S(1)}, bf16[2,128,896]{2,1,0:T(8,128)(2,1)S(1)}, bf16[2,2,32,896]{3,2,1,0:T(8,128)(2,1)S(1)}) custom-call(s32[6]{0:T(128)S(1)} %stack.64.at_ref, f32[2,2,128,896]{3,2,1,0:T(8,128)S(1)} %get-tuple-element.170.refs_0_, bf16[2,2,128,896]{3,2,1,0:T(8,128)(2,1)} %collective-permute-done.18.refs_1_, ...), custom_call_target="tpu_custom_call" | custom-call | tf_op jit(solution)/shard_map/pallas_call | solution.py:784
  191.5 5.6 %collective-permute-done.23.refs_8_.refs_10_.refs_4_ = bf16[2,2,32,896]{3,2,1,0:T(8,128)(2,1)S(1)} collective-permute-done((bf16[2,2,32,896]{3,2,1,0:T(8,128)(2,1)S(1)}, bf16[2,2,32,896]{3,2,1,0:T(8,128)(2,1)S(1)}, u32[]{:S(2)}, u32[]{:S(2)}) %collective-permute-start.23) | collective-permute-done | bytes 229408 | tf_op jit(solution)/shard_map/ppermute | solution.py:34
  197.1 3.4 %collective-permute-done.21.refs_2_ = bf16[2,128,896]{2,1,0:T(8,128)(2,1)S(1)} collective-permute-done((bf16[2,128,896]{2,1,0:T(8,128)(2,1)S(1)}, bf16[2,128,896]{2,1,0:T(8,128)(2,1)S(1)}, u32[]{:S(2)}, u32[]{:S(2)}) %collective-permute-start.21) | collective-permute-done | bytes 458784 | tf_op jit(solution)/shard_map/ppermute | solution.py:34
  202.4 3.1 %shard_map.110 = (bf16[2,128,896]{2,1,0:T(8,128)(2,1)}, bf16[2,32,896]{2,1,0:T(8,128)(2,1)}) custom-call(s32[15]{0:T(128)} %stack.65.at_ref, f32[2,2,128,896]{3,2,1,0:T(8,128)} %copy-done.9, bf16[2,2,128,896]{3,2,1,0:T(8,128)(2,1)} %collective-permute-done.18.refs_1_, bf16[2,128,896]{2,1,0:T(8,128)(2,1)} %copy-done.31, f32[2,2,128,896]{3,2,1,0:T(8,128)} %copy-done.10, ...), custom_call_target="tpu_custom_call" | custom-call | tf_op jit(solution)/shard_map/pallas_call | solution.py:784
  207.1 3.6 %collective-permute-done.25.refs_11_.refs_5_ = bf16[2,32,896]{2,1,0:T(8,128)(2,1)S(1)} collective-permute-done((bf16[2,32,896]{2,1,0:T(8,128)(2,1)}, bf16[2,32,896]{2,1,0:T(8,128)(2,1)S(1)}, u32[]{:S(2)}, u32[]{:S(2)}) %collective-permute-start.25) | collective-permute-done | bytes 114720 | tf_op jit(solution)/shard_map/ppermute | solution.py:34
  210.7 5.5 %collective-permute-done.24.refs_3_.refs_7_ = bf16[2,128,896]{2,1,0:T(8,128)(2,1)S(1)} collective-permute-done((bf16[2,128,896]{2,1,0:T(8,128)(2,1)}, bf16[2,128,896]{2,1,0:T(8,128)(2,1)S(1)}, u32[]{:S(2)}, u32[]{:S(2)}) %collective-permute-start.24) | collective-permute-done | bytes 458784 | tf_op jit(solution)/shard_map/ppermute | solution.py:34
  217.0 3.3 %shard_map.111 = (bf16[128,896]{1,0:T(8,128)(2,1)}, f32[128,896]{1,0:T(8,128)}, bf16[32,896]{1,0:T(8,128)(2,1)}) custom-call(s32[22]{0:T(128)} %stack.59.at_ref, f32[2,2,128,896]{3,2,1,0:T(8,128)} %copy-done.9, bf16[2,2,128,896]{3,2,1,0:T(8,128)(2,1)} %collective-permute-done.18.refs_1_, bf16[2,128,896]{2,1,0:T(8,128)(2,1)} %copy-done.31, ...), custom_call_target="tpu_custom_call" | custom-call | tf_op jit(solution)/shard_map/pallas_call | solution.py:784
  222.6 9.3 %shard_map.112.refs_8_ = bf16[544,640]{1,0:T(8,128)(2,1)} custom-call(s32[5]{0:T(128)} %stack.49.place_ref, bf16[544,3584]{1,0:T(8,128)(2,1)} %get-tuple-element.197.d_stem_ref, bf16[448,1280]{1,0:T(8,128)(2,1)} %copy-done.2, bf16[448,1280]{1,0:T(8,128)(2,1)} %copy-done.5, bf16[448,1280]{1,0:T(8,128)(2,1)} %copy-done.3, bf16[448,1280]{1,0:T(8,128)(2,1)} %copy-done.7, ...), custom_call_target="tpu_custom_call" | custom-call | tf_op jit(solution)/shard_map/pallas_call | solution.py:555
  237.6 9.7 %shard_map.114 = bf16[544,1176]{1,0:T(8,128)(2,1)} custom-call(s32[5]{0:T(128)} %stack.49.place_ref, bf16[544,3584]{1,0:T(8,128)(2,1)} %get-tuple-element.197.d_stem_ref, bf16[448,1280]{1,0:T(8,128)(2,1)} %copy-done.2, bf16[448,1280]{1,0:T(8,128)(2,1)} %copy-done.5, bf16[448,1280]{1,0:T(8,128)(2,1)} %copy-done.3, bf16[448,1280]{1,0:T(8,128)(2,1)} %copy-done.7, ...), custom_call_target="tpu_custom_call" | custom-call | tf_op jit(solution)/shard_map/pallas_call | solution.py:555
  (177 shorter events, 64.2 us)
Async XLA Ops:
  4.8 29.4 %collective-permute-start = (bf16[448,1280]{1,0:T(8,128)(2,1)S(1)}, bf16[448,1280]{1,0:T(8,128)(2,1)S(1)}, u32[]{:S(2)}, u32[]{:S(2)}) collective-permute-start(bf16[448,1280]{1,0:T(8,128)(2,1)S(1)} %concatenate.3.refs_0_), channel_id=1, source_target_pairs={{0,2},{1,3},{2,4},{3,5},{4,6},{5,7},{8,10},{9,11},{10,12},{11,13},... | collective-permute-start | bytes 3440648 | tf_op jit(solution)/shard_map/ppermute | solution.py:34
  9.8 28.7 %collective-permute-start.1 = (bf16[448,1280]{1,0:T(8,128)(2,1)S(1)}, bf16[448,1280]{1,0:T(8,128)(2,1)}, u32[]{:S(2)}, u32[]{:S(2)}) collective-permute-start(bf16[448,1280]{1,0:T(8,128)(2,1)S(1)} %concatenate.3.refs_0_), channel_id=1, source_target_pairs={{2,0},{3,1},{4,2},{5,3},{6,4},{7,5},{10,8},{11,9},{12,10},{13,11},... | collective-permute-start | bytes 3440648 | tf_op jit(solution)/shard_map/ppermute | solution.py:34
  16.3 22.2 %collective-permute-start.3 = (bf16[8,32,1280]{2,1,0:T(8,128)(2,1)}, bf16[8,32,1280]{2,1,0:T(8,128)(2,1)S(1)}, u32[]{:S(2)}, u32[]{:S(2)}) collective-permute-start(bf16[8,32,1280]{2,1,0:T(8,128)(2,1)} %get-tuple-element.110), channel_id=1, source_target_pairs={{0,8},{1,9},{2,10},{3,11},{4,12},{5,13},{6,14},{7,15},{8,0},{9,1},... | collective-permute-start | bytes 1966088 | tf_op jit(solution)/shard_map/ppermute | solution.py:34
  17.8 20.7 %collective-permute-start.4 = (bf16[8,32,1280]{2,1,0:T(8,128)(2,1)}, bf16[8,32,1280]{2,1,0:T(8,128)(2,1)S(1)}, u32[]{:S(2)}, u32[]{:S(2)}) collective-permute-start(bf16[8,32,1280]{2,1,0:T(8,128)(2,1)} %get-tuple-element.111), channel_id=1, source_target_pairs={{0,16},{1,17},{2,18},{3,19},{4,20},{5,21},{6,22},{7,23},{8,24},{9,... | collective-permute-start | bytes 1966088 | tf_op jit(solution)/shard_map/ppermute | solution.py:34
  38.9 30.7 %collective-permute-start.5 = (bf16[448,1280]{1,0:T(8,128)(2,1)S(1)}, bf16[448,1280]{1,0:T(8,128)(2,1)S(1)}, u32[]{:S(2)}, u32[]{:S(2)}) collective-permute-start(bf16[448,1280]{1,0:T(8,128)(2,1)S(1)} %collective-permute-done), channel_id=1, source_target_pairs={{2,4},{3,5},{4,6},{5,7},{10,12},{11,13},{12,14},{13,15},{18,20},{1... | collective-permute-start | bytes 3440648 | tf_op jit(solution)/shard_map/ppermute | solution.py:34
  39.8 30.2 %collective-permute-start.6 = (bf16[448,1280]{1,0:T(8,128)(2,1)}, bf16[448,1280]{1,0:T(8,128)(2,1)S(1)}, u32[]{:S(2)}, u32[]{:S(2)}) collective-permute-start(bf16[448,1280]{1,0:T(8,128)(2,1)} %collective-permute-done.1), channel_id=1, source_target_pairs={{2,0},{3,1},{4,2},{5,3},{10,8},{11,9},{12,10},{13,11},{18,16},{19,... | collective-permute-start | bytes 3440648 | tf_op jit(solution)/shard_map/ppermute | solution.py:34
  42.6 27.8 %collective-permute-start.9 = (bf16[448,1280]{1,0:T(8,128)(2,1)S(1)}, bf16[448,1280]{1,0:T(8,128)(2,1)S(1)}, u32[]{:S(2)}, u32[]{:S(2)}) collective-permute-start(bf16[448,1280]{1,0:T(8,128)(2,1)S(1)} %broadcast_select_fusion.1.refs_2_), channel_id=1, source_target_pairs={{0,1},{1,0},{2,3},{3,2},{4,5},{5,4},{6,7},{7,6},{8,9},{9,8},{10,11... | collective-permute-start | bytes 3440648 | tf_op jit(solution)/shard_map/ppermute | solution.py:34
  42.7 26.9 %collective-permute-start.8 = (bf16[8,32,1280]{2,1,0:T(8,128)(2,1)S(1)}, bf16[8,32,1280]{2,1,0:T(8,128)(2,1)S(1)}, u32[]{:S(2)}, u32[]{:S(2)}) collective-permute-start(bf16[8,32,1280]{2,1,0:T(8,128)(2,1)S(1)} %copy-done.39), channel_id=1, source_target_pairs={{0,24},{1,25},{2,26},{3,27},{4,28},{5,29},{6,30},{7,31},{8,16},{9,... | collective-permute-start | bytes 1966088 | tf_op jit(solution)/shard_map/ppermute | solution.py:34
  45.2 24.4 %collective-permute-start.7 = (bf16[64,3584]{1,0:T(8,128)(2,1)S(1)}, bf16[64,3584]{1,0:T(8,128)(2,1)S(1)}, u32[]{:S(2)}, u32[]{:S(2)}) collective-permute-start(bf16[64,3584]{1,0:T(8,128)(2,1)S(1)} %get-tuple-element.120), channel_id=1, source_target_pairs={{0,8},{1,9},{2,10},{3,11},{4,12},{5,13},{6,14},{7,15},{8,16},{9,17... | collective-permute-start | bytes 1376264 | tf_op jit(solution)/shard_map/ppermute | solution.py:34
  71.6 32.2 %collective-permute-start.10 = (bf16[448,1280]{1,0:T(8,128)(2,1)S(1)}, bf16[448,1280]{1,0:T(8,128)(2,1)}, u32[]{:S(2)}, u32[]{:S(2)}) collective-permute-start(bf16[448,1280]{1,0:T(8,128)(2,1)S(1)} %broadcast_select_fusion.refs_4_), channel_id=1, source_target_pairs={{2,0},{3,1},{4,6},{5,7},{10,8},{11,9},{12,14},{13,15},{18,16},{19,... | collective-permute-start | bytes 3440648 | tf_op jit(solution)/shard_map/ppermute | solution.py:34
  72.9 26.7 %collective-permute-start.14 = (bf16[64,3584]{1,0:T(8,128)(2,1)}, bf16[64,3584]{1,0:T(8,128)(2,1)}, u32[]{:S(2)}, u32[]{:S(2)}) collective-permute-start(bf16[64,3584]{1,0:T(8,128)(2,1)} %get-tuple-element.148), channel_id=1, source_target_pairs={{8,0},{9,1},{10,2},{11,3},{12,4},{13,5},{14,6},{15,7},{16,8},{17,9... | collective-permute-start | bytes 1376264 | tf_op jit(solution)/shard_map/ppermute | solution.py:34
  79.7 24.2 %collective-permute-start.12 = (bf16[128,1280]{1,0:T(8,128)(2,1)}, bf16[128,1280]{1,0:T(8,128)(2,1)}, u32[]{:S(2)}, u32[]{:S(2)}) collective-permute-start(bf16[128,1280]{1,0:T(8,128)(2,1)} %get-tuple-element.146), channel_id=1, source_target_pairs={{0,8},{1,9},{2,10},{3,11},{4,12},{5,13},{6,14},{7,15},{8,16},{9,17... | collective-permute-start | bytes 983048 | tf_op jit(solution)/shard_map/ppermute | solution.py:34
  85.4 18.4 %collective-permute-start.13 = (bf16[128,1280]{1,0:T(8,128)(2,1)}, bf16[128,1280]{1,0:T(8,128)(2,1)}, u32[]{:S(2)}, u32[]{:S(2)}) collective-permute-start(bf16[128,1280]{1,0:T(8,128)(2,1)} %get-tuple-element.147), channel_id=1, source_target_pairs={{8,0},{9,1},{10,2},{11,3},{12,4},{13,5},{14,6},{15,7},{16,8},{17,9... | collective-permute-start | bytes 983048 | tf_op jit(solution)/shard_map/ppermute | solution.py:34
  157.2 28.5 %collective-permute-start.18 = (bf16[2,2,128,896]{3,2,1,0:T(8,128)(2,1)}, bf16[2,2,128,896]{3,2,1,0:T(8,128)(2,1)}, u32[]{:S(2)}, u32[]{:S(2)}) collective-permute-start(bf16[2,2,128,896]{3,2,1,0:T(8,128)(2,1)} %get-tuple-element.171), channel_id=1, source_target_pairs={{0,8},{1,9},{2,10},{3,11},{4,12},{5,13},{6,14},{7,15},{8,0},{9,1},... | collective-permute-start | bytes 2752520 | tf_op jit(solution)/shard_map/ppermute | solution.py:34
  159.8 25.9 %collective-permute-start.19 = (bf16[2,2,128,896]{3,2,1,0:T(8,128)(2,1)}, bf16[2,2,128,896]{3,2,1,0:T(8,128)(2,1)}, u32[]{:S(2)}, u32[]{:S(2)}) collective-permute-start(bf16[2,2,128,896]{3,2,1,0:T(8,128)(2,1)} %get-tuple-element.172), channel_id=1, source_target_pairs={{0,16},{1,17},{2,18},{3,19},{4,20},{5,21},{6,22},{7,23},{8,24},{9,... | collective-permute-start | bytes 2752520 | tf_op jit(solution)/shard_map/ppermute | solution.py:34
  160.3 25.4 %collective-permute-start.20 = (bf16[2,4,32,896]{3,2,1,0:T(8,128)(2,1)}, bf16[2,4,32,896]{3,2,1,0:T(8,128)(2,1)S(1)}, u32[]{:S(2)}, u32[]{:S(2)}) collective-permute-start(bf16[2,4,32,896]{3,2,1,0:T(8,128)(2,1)} %get-tuple-element.173), channel_id=1, source_target_pairs={{0,4},{1,5},{2,6},{3,7},{4,0},{5,1},{6,2},{7,3},{8,12},{9,13},{10,... | collective-permute-start | bytes 1376264 | tf_op jit(solution)/shard_map/ppermute | solution.py:34
  188.7 11.8 %collective-permute-start.21 = (bf16[2,128,896]{2,1,0:T(8,128)(2,1)S(1)}, bf16[2,128,896]{2,1,0:T(8,128)(2,1)S(1)}, u32[]{:S(2)}, u32[]{:S(2)}) collective-permute-start(bf16[2,128,896]{2,1,0:T(8,128)(2,1)S(1)} %get-tuple-element.179), channel_id=1, source_target_pairs={{0,16},{1,17},{2,18},{3,19},{4,20},{5,21},{6,22},{7,23},{8,24},{9,... | collective-permute-start | bytes 1376264 | tf_op jit(solution)/shard_map/ppermute | solution.py:34
  190.5 11.1 %collective-permute-start.22 = (bf16[2,128,896]{2,1,0:T(8,128)(2,1)S(1)}, bf16[2,128,896]{2,1,0:T(8,128)(2,1)S(1)}, u32[]{:S(2)}, u32[]{:S(2)}) collective-permute-start(bf16[2,128,896]{2,1,0:T(8,128)(2,1)S(1)} %get-tuple-element.180), channel_id=1, source_target_pairs={{0,8},{1,9},{2,10},{3,11},{4,12},{5,13},{6,14},{7,15},{8,0},{9,1},... | collective-permute-start | bytes 1376264 | tf_op jit(solution)/shard_map/ppermute | solution.py:34
  205.5 10.7 %collective-permute-start.24 = (bf16[2,128,896]{2,1,0:T(8,128)(2,1)}, bf16[2,128,896]{2,1,0:T(8,128)(2,1)S(1)}, u32[]{:S(2)}, u32[]{:S(2)}) collective-permute-start(bf16[2,128,896]{2,1,0:T(8,128)(2,1)} %get-tuple-element.185), channel_id=1, source_target_pairs={{0,2},{1,3},{2,0},{3,1},{4,6},{5,7},{6,4},{7,5},{8,10},{9,11},{10,... | collective-permute-start | bytes 1376264 | tf_op jit(solution)/shard_map/ppermute | solution.py:34
  220.3 11.6 %collective-permute-start.26 = (bf16[128,896]{1,0:T(8,128)(2,1)}, bf16[128,896]{1,0:T(8,128)(2,1)S(1)}, u32[]{:S(2)}, u32[]{:S(2)}) collective-permute-start(bf16[128,896]{1,0:T(8,128)(2,1)} %get-tuple-element.189), channel_id=1, source_target_pairs={{0,4},{1,5},{2,6},{3,7},{4,0},{5,1},{6,2},{7,3},{8,12},{9,13},{10,... | collective-permute-start | bytes 688136 | tf_op jit(solution)/shard_map/ppermute | solution.py:34
  221.6 10.3 %collective-permute-start.27 = (bf16[32,896]{1,0:T(8,128)(2,1)}, bf16[32,896]{1,0:T(8,128)(2,1)S(1)}, u32[]{:S(2)}, u32[]{:S(2)}) collective-permute-start(bf16[32,896]{1,0:T(8,128)(2,1)} %get-tuple-element.191), channel_id=1, source_target_pairs={{0,16},{1,17},{2,18},{3,19},{4,20},{5,21},{6,22},{7,23},{8,24},{9,... | collective-permute-start | bytes 172040 | tf_op jit(solution)/shard_map/ppermute | solution.py:34
  234.0 13.2 %collective-permute-start.28 = (bf16[160,896]{1,0:T(8,128)(2,1)S(1)}, bf16[160,896]{1,0:T(8,128)(2,1)S(1)}, u32[]{:S(2)}, u32[]{:S(2)}) collective-permute-start(bf16[160,896]{1,0:T(8,128)(2,1)S(1)} %shard_map.113.refs_0_), channel_id=1, source_target_pairs={{0,8},{1,9},{2,10},{3,11},{4,12},{5,13},{6,14},{7,15},{8,0},{9,1},... | collective-permute-start | bytes 860168 | tf_op jit(solution)/shard_map/ppermute | solution.py:34
  234.9 12.5 %collective-permute-start.29 = (bf16[160,896]{1,0:T(8,128)(2,1)S(1)}, bf16[160,896]{1,0:T(8,128)(2,1)S(1)}, u32[]{:S(2)}, u32[]{:S(2)}) collective-permute-start(bf16[160,896]{1,0:T(8,128)(2,1)S(1)} %shard_map.113.refs_0_), channel_id=1, source_target_pairs={{0,16},{1,17},{2,18},{3,19},{4,20},{5,21},{6,22},{7,23},{8,24},{9,... | collective-permute-start | bytes 860168 | tf_op jit(solution)/shard_map/ppermute | solution.py:34
  236.2 11.2 %collective-permute-start.30 = (bf16[160,896]{1,0:T(8,128)(2,1)S(1)}, bf16[160,896]{1,0:T(8,128)(2,1)S(1)}, u32[]{:S(2)}, u32[]{:S(2)}) collective-permute-start(bf16[160,896]{1,0:T(8,128)(2,1)S(1)} %shard_map.113.refs_0_), channel_id=1, source_target_pairs={{0,24},{1,25},{2,26},{3,27},{4,28},{5,29},{6,30},{7,31},{8,16},{9,... | collective-permute-start | bytes 860168 | tf_op jit(solution)/shard_map/ppermute | solution.py:34
  (47 other events, 531.1 us)
